TPU v7x, 32 devices: a whole 2x2x4 slice. The times are simulated.
32 devices in a mesh: ctx: 8 (over y, x, core), dp: 4 (over z).
Axes of the slice: x: 2, y: 2, z: 4, core: 2. Of those that a mesh axis runs over, the one named last changes fastest.
Arguments:
- queries: bfloat16 [4, 2048, 1024], P('dp', 'ctx'), may hold values from -6 to 6
- key_vecs: bfloat16 [4, 2048, 1024], P('dp', 'ctx'), may hold values from -6 to 6
- value_vecs: bfloat16 [4, 2048, 1024], P('dp', 'ctx'), may hold values from -6 to 6
- out_grad: bfloat16 [4, 2048, 1024], P('dp', 'ctx'), may hold values from -6 to 6
- out_weight: bfloat16 [1024, 1024], P(('ctx', 'dp')), may hold values from -0.1875 to 0.1875
Outputs:
- query_grad: bfloat16 [4, 2048, 1024], P('dp', 'ctx')
- key_grad: bfloat16 [4, 2048, 1024], P('dp', 'ctx')
- value_grad: bfloat16 [4, 2048, 1024], P('dp', 'ctx')
- weight_grad: float32 [1024, 1024], P(('ctx', 'dp'))
All inputs are finite; a program needn't handle non-finite values.
Results may differ from a plain program's by a relative error of at most 0.0057.
Values may be sent and summed in bfloat16 or wider, within the bound.
No kernel may reach another device: no remote copies, remote signals or barrier semaphores. Data moves between devices by JAX's collectives and lax.ppermute only.
A program may use at most 128 MiB of HBM per device.

v0:
```python
import math

import jax
import jax.numpy as jnp
from jax import lax
from jax.sharding import PartitionSpec as P

HEAD = 128
BLOCK = 256


def ein(form, left, right):
    return jnp.einsum(form, left, right, preferred_element_type=jnp.float32)


def per_device(queries, key_vecs, value_vecs, out_grad, out_weight):
    qry_rows = queries[0]
    tok_count = qry_rows.shape[0]
    width = qry_rows.shape[1]
    heads_n = width // HEAD
    count = tok_count // BLOCK
    n_ctx = lax.axis_size("ctx")
    n_dp = lax.axis_size("dp")
    att_scale = 1.0 / math.sqrt(HEAD * tok_count * n_ctx)
    inv_root = 1.0 / math.sqrt(n_dp * tok_count * n_ctx)
    flat_grad = out_grad[0]

    def split(array):
        return array.reshape(count, BLOCK, heads_n, HEAD)

    qry_blk = split(qry_rows)
    key_blk = split(key_vecs[0])
    val_blk = split(value_vecs[0])
    kv_block = ein("bshe,bshf->bhef", key_blk, val_blk)
    local_kv = jnp.sum(kv_block, 0)
    grad_full = lax.dot_general(
        flat_grad,
        lax.all_gather(out_weight, ("ctx", "dp"), axis=0, tiled=True),
        (((1,), (1,)), ((), ())),
        preferred_element_type=jnp.float32,
    )
    att_grad = grad_full.astype(jnp.bfloat16)
    grd_blk = split(att_grad)
    qd_block = ein("bthf,bthe->bhfe", grd_blk, qry_blk)
    local_qd = jnp.sum(qd_block, 0)
    rows_each = heads_n * HEAD // n_ctx
    kv_parts, qd_parts = (
        lax.all_to_all(
            local_kv.reshape(n_ctx, rows_each, HEAD), "ctx", split_axis=0, concat_axis=0, tiled=True
        ),
        lax.all_to_all(
            local_qd.reshape(n_ctx, rows_each, HEAD), "ctx", split_axis=0, concat_axis=0, tiled=True
        ),
    )
    kv_earlier = jnp.cumsum(kv_parts, 0) - kv_parts
    qd_later = jnp.cumsum(qd_parts[::-1], 0)[::-1] - qd_parts
    kv_back, qd_back = (
        lax.all_to_all(kv_earlier, "ctx", split_axis=0, concat_axis=0, tiled=True),
        lax.all_to_all(qd_later, "ctx", split_axis=0, concat_axis=0, tiled=True),
    )
    kv_before = kv_back.reshape(local_kv.shape)
    qd_after = qd_back.reshape(local_qd.shape)
    state_in = (kv_before[None] + jnp.cumsum(kv_block, 0) - kv_block).astype(jnp.bfloat16)
    carried = (qd_after[None] + jnp.cumsum(qd_block[::-1], 0)[::-1] - qd_block).astype(jnp.bfloat16)
    positions = jnp.arange(BLOCK)
    causal = positions[:, None] >= positions[None, :]
    scores = jnp.where(causal, ein("bthe,bshe->bhts", qry_blk, key_blk), 0.0).astype(jnp.bfloat16)
    attended = att_scale * (
        ein("bhts,bshf->bthf", scores, val_blk) + ein("bthe,bhef->bthf", qry_blk, state_in)
    )
    attended = attended.astype(jnp.bfloat16).reshape(tok_count, width)
    weight_grad = lax.psum_scatter(
        lax.dot_general(
            attended, flat_grad, (((0,), (0,)), ((), ())), preferred_element_type=jnp.float32
        )
        * inv_root,
        ("ctx", "dp"),
        scatter_dimension=0,
        tiled=True,
    )
    dscores = jnp.where(causal, ein("bthf,bshf->bhts", grd_blk, val_blk), 0.0).astype(jnp.bfloat16)
    query_grad = att_scale * (
        ein("bhts,bshe->bthe", dscores, key_blk) + ein("bthf,bhef->bthe", grd_blk, state_in)
    )
    key_grad = att_scale * (
        ein("bhts,bthe->bshe", dscores, qry_blk) + ein("bshf,bhfe->bshe", val_blk, carried)
    )
    value_grad = att_scale * (
        ein("bhts,bthf->bshf", scores, grd_blk) + ein("bshe,bhfe->bshf", key_blk, carried)
    )
    shape_out = (1, tok_count, width)
    return (
        query_grad.astype(jnp.bfloat16).reshape(shape_out),
        key_grad.astype(jnp.bfloat16).reshape(shape_out),
        value_grad.astype(jnp.bfloat16).reshape(shape_out),
        weight_grad,
    )


def solution(mesh):
    placed = (
        P("dp", "ctx", None),
        P("dp", "ctx", None),
        P("dp", "ctx", None),
        P("dp", "ctx", None),
        P(("ctx", "dp"), None),
    )
    return jax.shard_map(
        per_device,
        mesh=mesh,
        in_specs=placed,
        out_specs=(
            P("dp", "ctx", None),
            P("dp", "ctx", None),
            P("dp", "ctx", None),
            P(("ctx", "dp"), None),
        ),
        check_vma=False,
    )
```

profile of v0, /device:TPU:0, one launch (start us, length us, event | category | flops | bytes accessed | tf_op | source)
XLA Modules:
  0.0 227.3 jit_solution(1039146625658339510)
XLA Ops:
  7.2 0.0 copy-start
  7.2 0.0 all-gather.2.cloned.1.call-start
  7.2 0.7 all-gather.2.cloned.1.call-update
  7.9 1.1 copy.34
  9.1 0.0 copy-start.4
  9.1 1.3 copy.33
  10.4 1.1 fusion.12
  11.5 5.2 %all-to-all-start = ((f32[8,128,128]{2,1,0:T(8,128)}), f32[8,128,128]{2,1,0:T(8,128)S(1)}, u32[]{:S(2)}, u32[]{:S(2)}) async-start(f32[8,128,128]{2,1,0:T(8,128)} %fusion.12), calls=%async_computation | async-start | bytes 1048576 | tf_op jit(solution)/shard_map/all_to_all | solution.py:48
  16.7 0.0 copy-done.4
  16.7 0.1 copy.35
  16.8 0.0 copy-start.1
  16.8 10.0 %all-to-all-done = f32[8,128,128]{2,1,0:T(8,128)S(1)} async-done(((f32[8,128,128]{2,1,0:T(8,128)}), f32[8,128,128]{2,1,0:T(8,128)S(1)}, u32[]{:S(2)}, u32[]{:S(2)}) %all-to-all-start) | async-done | bytes 524320 | tf_op jit(solution)/shard_map/all_to_all | solution.py:48
  26.9 0.8 reduce-window_subtract_fusion
  27.7 3.5 %all-to-all-start.1 = ((f32[8,128,128]{2,1,0:T(8,128)}), f32[8,128,128]{2,1,0:T(8,128)S(1)}, u32[]{:S(2)}, u32[]{:S(2)}) async-start(f32[8,128,128]{2,1,0:T(8,128)} %reduce-window_subtract_fusion), calls=%async_computation.1 | async-start | bytes 1048576 | tf_op jit(solution)/shard_map/all_to_all | solution.py:58
  31.2 0.0 reduce-scatter.2.cloned.1.call-start
  31.3 1.5 select_convert_fusion
  32.7 2.7 %convolution_bitcast_fusion.1 = f32[8,128,256]{2,1,0:T(8,128)} fusion(bf16[8,256,256]{2,1,0:T(8,128)(2,1)} %select_convert_fusion, bf16[256,8,128]{0,2,1:T(8,128)(2,1)S(1)} %bitcast.60), kind=kOutput, calls=%fused_computation.12 | convolution fusion | flops 134217728 | bytes 2621440 | tf_op jit(solution)/shard_map/bhts,bshf->bthf/dot_general | solution.py:13
  35.4 5.5 %all-to-all-done.1 = f32[8,128,128]{2,1,0:T(8,128)S(1)} async-done(((f32[8,128,128]{2,1,0:T(8,128)}), f32[8,128,128]{2,1,0:T(8,128)S(1)}, u32[]{:S(2)}, u32[]{:S(2)}) %all-to-all-start.1) | async-done | bytes 524320 | tf_op jit(solution)/shard_map/all_to_all | solution.py:58
  40.9 1.1 fusion.8
  42.0 1.6 fusion.7
  43.6 0.0 copy-done
  43.6 2.7 %convolution_multiply_fusion = f32[1024,1024]{1,0:T(8,128)} fusion(bf16[256,1024]{0,1:T(8,128)(2,1)S(1)} %bitcast.75, bf16[1,256,1024]{2,1,0:T(8,128)(2,1)S(1)} %copy-done), kind=kOutput, calls=%fused_computation | convolution fusion | flops 537919488 | bytes 5242880 | tf_op jit(solution)/shard_map/dot_general | solution.py:73
  46.2 0.0 reduce-scatter.2.cloned.1.call-update
  46.3 24.0 %all-gather.2.cloned.1.call-done = bf16[1024,1024]{1,0:T(8,128)(2,1)} async-done(((bf16[32,1024]{1,0:T(8,128)(2,1)}), bf16[1024,1024]{1,0:T(8,128)(2,1)}) %all-gather.2.cloned.1.call-update) | async-done | bytes 2097168 | tf_op jit(solution)/shard_map/all_gather | solution.py:38
  70.3 2.3 %convolution_convert_fusion = bf16[256,1024]{1,0:T(8,128)(2,1)S(1)} fusion(bf16[1024,1024]{1,0:T(8,128)(2,1)} %all-gather.2.cloned.1.call-done, bf16[1,256,1024]{2,1,0:T(8,128)(2,1)S(1)} %copy-done), kind=kOutput, calls=%fused_computation.18 | convolution fusion | flops 537133056 | bytes 3145728 | tf_op jit(solution)/shard_map/dot_general | solution.py:36
  72.6 0.2 copy.32
  72.8 0.0 copy-done.1
  72.8 1.1 fusion.20
  73.9 4.1 %all-to-all-start.2 = ((f32[8,128,128]{2,1,0:T(8,128)}), f32[8,128,128]{2,1,0:T(8,128)}, u32[]{:S(2)}, u32[]{:S(2)}) async-start(f32[8,128,128]{2,1,0:T(8,128)} %fusion.20), calls=%async_computation.2 | async-start | bytes 1048576 | tf_op jit(solution)/shard_map/all_to_all | solution.py:51
  78.0 0.5 select_convert_fusion.1
  78.5 0.5 convolution_bitcast_fusion.2
  79.0 1.1 fusion.4
  80.1 2.0 copy.27
  82.2 7.1 %all-to-all-done.2 = f32[8,128,128]{2,1,0:T(8,128)} async-done(((f32[8,128,128]{2,1,0:T(8,128)}), f32[8,128,128]{2,1,0:T(8,128)}, u32[]{:S(2)}, u32[]{:S(2)}) %all-to-all-start.2) | async-done | bytes 524320 | tf_op jit(solution)/shard_map/all_to_all | solution.py:51
  89.2 1.9 rev.6
  91.1 1.1 fusion.22
  92.2 1.9 reverse_subtract_fusion
  94.1 4.1 %all-to-all-start.3 = ((f32[8,128,128]{2,1,0:T(8,128)}), f32[8,128,128]{2,1,0:T(8,128)}, u32[]{:S(2)}, u32[]{:S(2)}) async-start(f32[8,128,128]{2,1,0:T(8,128)} %reverse_subtract_fusion), calls=%async_computation.3 | async-start | bytes 1048576 | tf_op jit(solution)/shard_map/all_to_all | solution.py:59
  98.2 0.0 copy-start.2
  98.2 2.6 %fusion.23 = f32[8,128,256]{2,1,0:T(8,128)} fusion(bf16[256,8,128]{0,2,1:T(8,128)(2,1)S(1)} %bitcast.66, bf16[8,256,256]{2,1,0:T(8,128)(2,1)} %select_convert_fusion), kind=kOutput, calls=%fused_computation.39 | convolution fusion | flops 134217728 | bytes 2621440 | tf_op jit(solution)/shard_map/bhts,bthf->bshf/dot_general | solution.py:13
  100.8 0.0 copy-done.2
  100.8 1.3 convolution_bitcast_fusion
  102.1 0.0 copy-start.3
  102.1 7.1 %all-to-all-done.3 = f32[8,128,128]{2,1,0:T(8,128)} async-done(((f32[8,128,128]{2,1,0:T(8,128)}), f32[8,128,128]{2,1,0:T(8,128)}, u32[]{:S(2)}, u32[]{:S(2)}) %all-to-all-start.3) | async-done | bytes 524320 | tf_op jit(solution)/shard_map/all_to_all | solution.py:59
  109.2 1.3 fusion.9
  110.5 2.3 %fusion.6 = bf16[8,128,256]{2,1,0:T(8,128)(2,1)} fusion(f32[8,128,256]{2,1,0:T(8,128)} %fusion.23, bf16[8,128,128]{2,1,0:T(8,128)(2,1)S(1)} %fusion.9, bf16[256,8,128]{2,1,0:T(8,128)(2,1)S(1)} %bitcast.70), kind=kOutput, calls=%fused_computation.16 | convolution fusion | flops 67895296 | bytes 2359296 | tf_op jit(solution)/shard_map/bshe,bhfe->bshf/dot_general | solution.py:13
  112.8 2.0 copy.29
  114.8 0.0 copy-done.3
  114.8 0.3 fusion.5
  115.2 1.0 copy.28
  116.2 104.3 %reduce-scatter.2.cloned.1.call-done = f32[32,1024]{1,0:T(8,128)} async-done(((f32[1024,1024]{1,0:T(8,128)}), f32[32,1024]{1,0:T(8,128)}) %reduce-scatter.2.cloned.1.call-update) | async-done | bytes 131088 | tf_op jit(solution)/shard_map/reduce_scatter | solution.py:72
  (1 shorter events, 0.0 us)
Async XLA Ops:
  7.2 36.4 %copy-start = (bf16[1,256,1024]{2,1,0:T(8,128)(2,1)S(1)}, bf16[1,256,1024]{2,1,0:T(8,128)(2,1)}, u32[]{:S(2)}) copy-start(bf16[1,256,1024]{2,1,0:T(8,128)(2,1)} %param.8) | copy-start | bytes 1572868
  7.2 63.1 %all-gather.2.cloned.1.call-start = ((), (), s32[]{:S(2)}) async-start(), calls=%async_computation.5 | async-start | bytes 2162688 | tf_op jit(solution)/shard_map/all_gather | solution.py:38
  9.1 7.6 %copy-start.4 = (bf16[1,256,1024]{2,1,0:T(8,128)(2,1)S(1)}, bf16[1,256,1024]{2,1,0:T(8,128)(2,1)}, u32[]{:S(2)}) copy-start(bf16[1,256,1024]{2,1,0:T(8,128)(2,1)} %param.5) | copy-start | bytes 1572868
  11.5 15.3 %all-to-all-start = ((f32[8,128,128]{2,1,0:T(8,128)}), f32[8,128,128]{2,1,0:T(8,128)S(1)}, u32[]{:S(2)}, u32[]{:S(2)}) async-start(f32[8,128,128]{2,1,0:T(8,128)} %fusion.12), calls=%async_computation | async-start | bytes 1048576 | tf_op jit(solution)/shard_map/all_to_all | solution.py:48
  16.8 56.0 %copy-start.1 = (bf16[32,8,8,128]{3,2,1,0:T(8,128)(2,1)}, bf16[32,8,8,128]{3,2,1,0:T(8,128)(2,1)S(1)}, u32[]{:S(2)}) copy-start(bf16[32,8,8,128]{3,2,1,0:T(8,128)(2,1)S(1)} %copy.35) | copy-start | bytes 1572868
  27.7 13.2 %all-to-all-start.1 = ((f32[8,128,128]{2,1,0:T(8,128)}), f32[8,128,128]{2,1,0:T(8,128)S(1)}, u32[]{:S(2)}, u32[]{:S(2)}) async-start(f32[8,128,128]{2,1,0:T(8,128)} %reduce-window_subtract_fusion), calls=%async_computation.1 | async-start | bytes 1048576 | tf_op jit(solution)/shard_map/all_to_all | solution.py:58
  31.2 189.3 %reduce-scatter.2.cloned.1.call-start = ((), (), s32[]{:S(2)}) async-start(), calls=%async_computation.6 | async-start | bytes 4325376 | tf_op jit(solution)/shard_map/reduce_scatter | solution.py:72
  73.9 15.3 %all-to-all-start.2 = ((f32[8,128,128]{2,1,0:T(8,128)}), f32[8,128,128]{2,1,0:T(8,128)}, u32[]{:S(2)}, u32[]{:S(2)}) async-start(f32[8,128,128]{2,1,0:T(8,128)} %fusion.20), calls=%async_computation.2 | async-start | bytes 1048576 | tf_op jit(solution)/shard_map/all_to_all | solution.py:51
  94.1 15.1 %all-to-all-start.3 = ((f32[8,128,128]{2,1,0:T(8,128)}), f32[8,128,128]{2,1,0:T(8,128)}, u32[]{:S(2)}, u32[]{:S(2)}) async-start(f32[8,128,128]{2,1,0:T(8,128)} %reverse_subtract_fusion), calls=%async_computation.3 | async-start | bytes 1048576 | tf_op jit(solution)/shard_map/all_to_all | solution.py:59
  98.2 2.6 %copy-start.2 = (bf16[32,8,8,128]{3,2,1,0:T(8,128)(2,1)S(1)}, bf16[32,8,8,128]{3,2,1,0:T(8,128)(2,1)}, u32[]{:S(2)}) copy-start(bf16[32,8,8,128]{3,2,1,0:T(8,128)(2,1)} %copy-done.1) | copy-start | bytes 1572868
  102.1 12.7 %copy-start.3 = (f32[8,128,256]{2,1,0:T(8,128)S(1)}, f32[8,128,256]{2,1,0:T(8,128)}, u32[]{:S(2)}) copy-start(f32[8,128,256]{2,1,0:T(8,128)} %convolution_bitcast_fusion) | copy-start | bytes 3145732
Sparse Core Ops, SparseCore 0:
  10.9 59.2 all-gather.1
  73.1 147.3 reduce-scatter.1
where the time goes:
time: 228 us; the launch traced here: 227 us
  waiting for transfers between devices  159 us (70%)
  matrix products  21.6 us (9%)
  starting transfers between devices  17 us (7%)
  between operations  14.2 us (6%)
  local copies, waits for them, and re-layouts  9.72 us (4%)
  other arithmetic  6.19 us (3%)
    reduce_scatter x1, waiting for transfers between devices, per_device(): lax.psum_scatter(lax.dot_general(attended, flat_grad, (((0,), (0,)), ((),...  104 us
    all_gather x1, waiting for transfers between devices, per_device(): lax.all_gather(out_weight, ('ctx', 'dp'), axis=0, tiled=True)  24 us
    dot_general x12, matrix products, ein(): return jnp.einsum(form, left, right, preferred_element_type=jnp.float32)  16.6 us
    all_to_all x1, waiting for transfers between devices, per_device(): lax.all_to_all(local_kv.reshape(n_ctx, rows_each, HEAD), 'ctx', split_axi...  10 us
    all_to_all x1, waiting for transfers between devices, per_device(): lax.all_to_all(qd_later, 'ctx', split_axis=0, concat_axis=0, tiled=True)  7.07 us
    all_to_all x1, waiting for transfers between devices, per_device(): lax.all_to_all(local_qd.reshape(n_ctx, rows_each, HEAD), 'ctx', split_axi...  7.05 us
    unnamed x15, local copies, waits for them, and re-layouts  6.34 us
    all_to_all x1, waiting for transfers between devices, per_device(): lax.all_to_all(kv_earlier, 'ctx', split_axis=0, concat_axis=0, tiled=True)  5.49 us
  transfers between devices with their start and end apart: 6, of which 6 were waited for; matrix products, arithmetic and copies ran while one was open for 16% of the time, Pallas kernels for 0%

commit v1 on v0

--- a/solution.py
+++ b/solution.py
@@ -1,19 +1,287 @@
+import functools
 import math
 
 import jax
 import jax.numpy as jnp
 from jax import lax
+from jax.experimental import pallas as pl
+from jax.experimental.pallas import tpu as pltpu
 from jax.sharding import PartitionSpec as P
 
 HEAD = 128
 BLOCK = 256
+BF = jnp.bfloat16
+F32 = jnp.float32
 
 
 def ein(form, left, right):
     return jnp.einsum(form, left, right, preferred_element_type=jnp.float32)
 
 
-def per_device(queries, key_vecs, value_vecs, out_grad, out_weight):
+def nn(a, b):
+    return lax.dot_general(a, b, (((1,), (0,)), ((), ())), preferred_element_type=F32)
+
+
+def nt(a, b):
+    return lax.dot_general(a, b, (((1,), (1,)), ((), ())), preferred_element_type=F32)
+
+
+def tn(a, b):
+    return lax.dot_general(a, b, (((0,), (0,)), ((), ())), preferred_element_type=F32)
+
+
+def cols(index):
+    return pl.ds(pl.multiple_of(index * HEAD, HEAD), HEAD)
+
+
+def causal_mask():
+    t = lax.broadcasted_iota(jnp.int32, (BLOCK, BLOCK), 0)
+    s = lax.broadcasted_iota(jnp.int32, (BLOCK, BLOCK), 1)
+    return t >= s
+
+
+def place():
+    me = lax.axis_index("ctx")
+    return lax.rem(me, 2), lax.div(me, 2)
+
+
+def local_call(kernel, outs, flops, *args):
+    vmem = pl.BlockSpec(memory_space=pltpu.VMEM)
+    size = sum(a.size * a.dtype.itemsize for a in args)
+    size += sum(math.prod(s) * jnp.dtype(d).itemsize for s, d in outs)
+    return pl.pallas_call(
+        kernel,
+        out_shape=[jax.ShapeDtypeStruct(s, d) for s, d in outs],
+        in_specs=[vmem] * len(args),
+        out_specs=[vmem] * len(outs),
+        compiler_params=pltpu.CompilerParams(vmem_limit_bytes=24 << 20),
+        cost_estimate=pl.CostEstimate(flops=flops, bytes_accessed=size, transcendentals=0),
+    )(*args)
+
+
+def kv_kernel(groups, k_o, v_o, k_r, v_r, kvsel, psum):
+    par, _ = place()
+    later = par.astype(F32)
+    for j in range(groups):
+        c = cols(2 * j + par)
+        own = tn(k_o[:, c], v_o[:, c])
+        other = tn(k_r[:, c], v_r[:, c])
+        kvsel[j] = other * later + own * (1.0 - later)
+        psum[j] = (own + other).astype(BF)
+
+
+def intra_kernel(groups, q_o, k_o, v_o, q_r, k_r, v_r, intra):
+    par, _ = place()
+    mask = causal_mask()
+    for i, (q, k, v) in enumerate(((q_o, k_o, v_o), (q_r, k_r, v_r))):
+        for j in range(groups):
+            c = cols(2 * j + par)
+            scores = jnp.where(mask, nt(q[:, c], k[:, c]), 0.0).astype(BF)
+            intra[i, :, j * HEAD : (j + 1) * HEAD] = nn(scores, v[:, c])
+
+
+def attend_kernel(groups, att_scale, inv_root, q_o, q_r, g_o, g_r, intra, kvsel, *rest):
+    parts = rest[: groups - 1]
+    prod_own, prods, state_o, state_r = rest[groups - 1 :]
+    par, chip = place()
+    later = par.astype(F32)
+    for m in range(groups - 1, -1, -1):
+        j = lax.bitwise_xor(chip, m)
+        total = sum(part[j].astype(F32) for part in parts)
+        sel = kvsel[j]
+        s_o = (total + later * sel).astype(BF)
+        s_r = (total + (1.0 - later) * sel).astype(BF)
+        state_o[j] = s_o
+        state_r[j] = s_r
+        c = cols(2 * j + par)
+        a_o = (att_scale * (intra[0, :, cols(j)] + nn(q_o[:, c], s_o))).astype(BF)
+        a_r = (att_scale * (intra[1, :, cols(j)] + nn(q_r[:, c], s_r))).astype(BF)
+        term = (tn(a_o, g_o[...]) + tn(a_r, g_r[...])) * inv_root
+        if m == 0:
+            prod_own[...] = term
+        else:
+            prods[m - 1] = term.astype(BF)
+
+
+def gather_kernel(n_dp, w_own, *rest):
+    parts, full = rest[:-1], rest[-1]
+    rows = w_own.shape[0]
+    d = lax.axis_index("dp")
+    for m, part in enumerate((w_own,) + tuple(parts)):
+        at = pl.multiple_of(lax.bitwise_xor(d, m) * rows, rows)
+        full[pl.ds(at, rows), :] = part[...]
+
+
+def att_grad_kernel(groups, g_o, g_r, q_o, q_r, *rest):
+    weights = rest[:groups]
+    ag_o, ag_r, qdsel, psum = rest[groups:]
+    par, chip = place()
+    later = par.astype(F32)
+    for m in range(groups):
+        j = lax.bitwise_xor(chip, m)
+        w = weights[m][...]
+        a_o = nt(g_o[...], w).astype(BF)
+        a_r = nt(g_r[...], w).astype(BF)
+        ag_o[:, cols(j)] = a_o
+        ag_r[:, cols(j)] = a_r
+        c = cols(2 * j + par)
+        own = tn(a_o, q_o[:, c])
+        other = tn(a_r, q_r[:, c])
+        qdsel[j] = own * later + other * (1.0 - later)
+        psum[j] = (own + other).astype(BF)
+
+
+def block_kernel(groups, att_scale, q_o, k_o, v_o, ag_o, ag_p, st_o, st_p, dq, dk_in, dv_in):
+    par, _ = place()
+    mask = causal_mask()
+    for side, (ag, st) in enumerate(((ag_o, st_o), (ag_p, st_p))):
+        parity = par if side == 0 else 1 - par
+        for j in range(groups):
+            c = cols(2 * j + parity)
+            q, k, v, a = q_o[:, c], k_o[:, c], v_o[:, c], ag[:, j * HEAD : (j + 1) * HEAD]
+            dscores = jnp.where(mask, nt(a, v), 0.0).astype(BF)
+            scores = jnp.where(mask, nt(q, k), 0.0).astype(BF)
+            dq[:, c] = (att_scale * (nn(dscores, k) + nt(a, st[j]))).astype(BF)
+            dk_in[:, c] = tn(dscores, q)
+            dv_in[:, c] = tn(scores, a)
+
+
+def carried_kernel(groups, qdsel, *rest):
+    parts = rest[: groups - 1]
+    car_o, car_r = rest[groups - 1 :]
+    par, _ = place()
+    later = par.astype(F32)
+    for j in range(groups):
+        total = sum(part[j].astype(F32) for part in parts)
+        sel = qdsel[j]
+        car_o[j] = (total + (1.0 - later) * sel).astype(BF)
+        car_r[j] = (total + later * sel).astype(BF)
+
+
+def finish_kernel(groups, att_scale, k_o, v_o, car_o, car_p, dk_in, dv_in, dk, dv):
+    par, _ = place()
+    for side, car in enumerate((car_o, car_p)):
+        parity = par if side == 0 else 1 - par
+        for j in range(groups):
+            c = cols(2 * j + parity)
+            carried = car[j]
+            dk[:, c] = (att_scale * (dk_in[:, c] + nn(v_o[:, c], carried))).astype(BF)
+            dv[:, c] = (att_scale * (dv_in[:, c] + nt(k_o[:, c], carried))).astype(BF)
+
+
+def fold_kernel(n_dp, prod_own, *rest):
+    parts, (keep, send) = rest[:-2], rest[-2:]
+    rows = keep.shape[0]
+    d = lax.axis_index("dp")
+    for m in range(n_dp):
+        at = pl.ds(pl.multiple_of(lax.bitwise_xor(d, m) * rows, rows), rows)
+        total = prod_own[at, :] + sum(part[at, :].astype(F32) for part in parts)
+        if m == 0:
+            keep[...] = total
+        else:
+            send[m - 1] = total.astype(BF)
+
+
+def per_device(n_ctx, n_dp, queries, key_vecs, value_vecs, out_grad, out_weight):
+    tok_count, width = queries.shape[1:]
+    heads_n = width // HEAD
+    groups = n_ctx // 2
+    att_scale = 1.0 / math.sqrt(HEAD * tok_count * n_ctx)
+    inv_root = 1.0 / math.sqrt(n_dp * tok_count * n_ctx)
+    q_o, k_o, v_o, g_o = queries[0], key_vecs[0], value_vecs[0], out_grad[0]
+
+    def core(x):
+        return lax.ppermute(x, "ctx", [(i, i ^ 1) for i in range(n_ctx)])
+
+    def chips(x, m):
+        return lax.ppermute(x, "ctx", [(i, i ^ (2 * m)) for i in range(n_ctx)])
+
+    def to_later(x, m):
+        return lax.ppermute(x, "ctx", [(i, i ^ (2 * m)) for i in range(n_ctx) if i ^ (2 * m) > i])
+
+    def to_earlier(x, m):
+        return lax.ppermute(x, "ctx", [(i, i ^ (2 * m)) for i in range(n_ctx) if i ^ (2 * m) < i])
+
+    def along_dp(x, m):
+        return lax.ppermute(x, "dp", [(i, i ^ m) for i in range(n_dp)])
+
+    others = range(1, groups)
+    mat = HEAD * HEAD
+    state_shape = (groups, HEAD, HEAD)
+    half = groups * HEAD
+    k_r, v_r = core(k_o), core(v_o)
+    q_r, g_r = core(q_o), core(g_o)
+    w_parts = [along_dp(out_weight, m) for m in range(1, n_dp)]
+    kvsel, kv_sum = local_call(
+        functools.partial(kv_kernel, groups),
+        [(state_shape, F32), (state_shape, BF)],
+        4 * groups * mat * BLOCK,
+        k_o, v_o, k_r, v_r,
+    )
+    kv_parts = [to_later(kv_sum, m) for m in others]
+    (w_head,) = local_call(
+        functools.partial(gather_kernel, n_dp), [((HEAD, width), BF)], 0, out_weight, *w_parts
+    )
+    w_all = [w_head] + [chips(w_head, m) for m in others]
+    (intra,) = local_call(
+        functools.partial(intra_kernel, groups),
+        [((2, BLOCK, half), F32)],
+        8 * groups * BLOCK * BLOCK * HEAD,
+        q_o, k_o, v_o, q_r, k_r, v_r,
+    )
+    prod_own, prods, state_o, state_r = local_call(
+        functools.partial(attend_kernel, groups, att_scale, inv_root),
+        [
+            ((HEAD, width), F32),
+            ((groups - 1, HEAD, width), BF),
+            (state_shape, BF),
+            (state_shape, BF),
+        ],
+        4 * groups * BLOCK * (mat + HEAD * width),
+        q_o, q_r, g_o, g_r, intra, kvsel, *kv_parts,
+    )
+    terms = [chips(prods[m - 1], m) for m in others]
+    state_p = core(state_r)
+    ag_o, ag_r, qdsel, qd_sum = local_call(
+        functools.partial(att_grad_kernel, groups),
+        [((BLOCK, half), BF), ((BLOCK, half), BF), (state_shape, F32), (state_shape, BF)],
+        4 * groups * BLOCK * (mat + HEAD * width),
+        g_o, g_r, q_o, q_r, *w_all,
+    )
+    qd_parts = [to_earlier(qd_sum, m) for m in others]
+    ag_p = core(ag_r)
+    dq, dk_in, dv_in = local_call(
+        functools.partial(block_kernel, groups, att_scale),
+        [((BLOCK, width), BF), ((BLOCK, width), F32), ((BLOCK, width), F32)],
+        4 * groups * BLOCK * HEAD * (5 * BLOCK + HEAD),
+        q_o, k_o, v_o, ag_o, ag_p, state_o, state_p,
+    )
+    keep, send = local_call(
+        functools.partial(fold_kernel, n_dp),
+        [((HEAD // n_dp, width), F32), ((n_dp - 1, HEAD // n_dp, width), BF)],
+        0,
+        prod_own, *terms,
+    )
+    weight_grad = keep
+    for m in range(1, n_dp):
+        weight_grad = weight_grad + along_dp(send[m - 1], m).astype(F32)
+    car_o, car_r = local_call(
+        functools.partial(carried_kernel, groups),
+        [(state_shape, BF), (state_shape, BF)],
+        0,
+        qdsel, *qd_parts,
+    )
+    car_p = core(car_r)
+    dk, dv = local_call(
+        functools.partial(finish_kernel, groups, att_scale),
+        [((BLOCK, width), BF), ((BLOCK, width), BF)],
+        8 * groups * BLOCK * mat,
+        k_o, v_o, car_o, car_p, dk_in, dv_in,
+    )
+    return dq[None], dk[None], dv[None], weight_grad
+
+
+def general_per_device(queries, key_vecs, value_vecs, out_grad, out_weight):
     qry_rows = queries[0]
     tok_count = qry_rows.shape[0]
     width = qry_rows.shape[1]
@@ -105,8 +373,18 @@
         P("dp", "ctx", None),
         P(("ctx", "dp"), None),
     )
+    n_ctx, n_dp = mesh.shape["ctx"], mesh.shape["dp"]
+
+    def chosen(queries, key_vecs, value_vecs, out_grad, out_weight):
+        local = (queries, key_vecs, value_vecs, out_grad, out_weight)
+        one_head = out_weight.shape[0] * n_dp == HEAD and HEAD % (16 * n_dp) == 0
+        powers = n_ctx & (n_ctx - 1) == 0 and n_dp & (n_dp - 1) == 0 and n_ctx > 2
+        if one_head and powers and queries.shape[:2] == (1, BLOCK):
+            return per_device(n_ctx, n_dp, *local)
+        return general_per_device(*local)
+
     return jax.shard_map(
-        per_device,
+        chosen,
         mesh=mesh,
         in_specs=placed,
         out_specs=(

time: 228 us -> 71.9 us (0.32)
  waiting for transfers between devices: 159 us -> 20.3 us
  matrix products: 21.6 us -> 0 us
  starting transfers between devices: 17 us -> 37.5 us
  between operations: 14.2 us -> 0.86 us
  Pallas kernels: 0 us -> 10.2 us
  local copies, waits for them, and re-layouts: 9.72 us -> 1.96 us
  other arithmetic: 6.19 us -> 0.69 us
    reduce_scatter x1 -> x0, waiting for transfers between devices: 104 us -> none  [per_device(): lax.psum_scatter(lax.dot_general(attended, flat_grad, (((0,), (0,)), ((),...]
    ppermute x0 -> x25, starting transfers between devices: none -> 37.5 us  [the longest x6 14.9 us: along_dp(): return lax.ppermute(x, 'dp', [(i, i ^ m) for i in range(n_dp)])]
    all_to_all x4 -> x0, waiting for transfers between devices: 29.6 us -> none  [the longest x1 10 us: per_device(): lax.all_to_all(local_kv.reshape(n_ctx, rows_each, HEAD), 'ctx', split_axi...]
    all_gather x1 -> x0, waiting for transfers between devices: 24 us -> none  [per_device(): lax.all_gather(out_weight, ('ctx', 'dp'), axis=0, tiled=True)]
    dot_general x14 -> x0, matrix products: 21.6 us -> none  [the longest x12 16.6 us: ein(): return jnp.einsum(form, left, right, preferred_element_type=jnp.float32)]
    ppermute x0 -> x25, waiting for transfers between devices: none -> 20.3 us  [the longest x3 8.74 us: to_earlier(): lax.ppermute(x, 'ctx', [(i, i ^ 2 * m) for i in range(n_ctx) if i ^ 2 * m...]
    all_to_all x4 -> x0, starting transfers between devices: 17 us -> none  [the longest x1 5.18 us: per_device(): lax.all_to_all(local_kv.reshape(n_ctx, rows_each, HEAD), 'ctx', split_axi...]
    pallas_call x0 -> x9, Pallas kernels: none -> 10.2 us  [local_call(): pl.pallas_call(kernel, out_shape=[jax.ShapeDtypeStruct(s, d) for s, d in...]
  transfers between devices with their start and end apart: 6 -> 25, of which waited for: 6 -> 6; matrix products, arithmetic and copies ran while one was open for 16% -> 0% of each run, Pallas kernels for 0% -> 14%
where the time goes in v1:
time: 71.9 us; the launch traced here: 71.5 us
  starting transfers between devices  37.5 us (52%)
  waiting for transfers between devices  20.3 us (28%)
  Pallas kernels  10.2 us (14%)
  local copies, waits for them, and re-layouts  1.96 us (3%)
  between operations  0.86 us (1%)
    ppermute x6, starting transfers between devices, along_dp(): return lax.ppermute(x, 'dp', [(i, i ^ m) for i in range(n_dp)])  14.9 us
    pallas_call x9, Pallas kernels, local_call(): pl.pallas_call(kernel, out_shape=[jax.ShapeDtypeStruct(s, d) for s, d in...  10.2 us
    ppermute x3, starting transfers between devices, to_later(): lax.ppermute(x, 'ctx', [(i, i ^ 2 * m) for i in range(n_ctx) if i ^ 2 * m...  9.15 us
    ppermute x3, waiting for transfers between devices, to_earlier(): lax.ppermute(x, 'ctx', [(i, i ^ 2 * m) for i in range(n_ctx) if i ^ 2 * m...  8.74 us
    ppermute x6, waiting for transfers between devices, along_dp(): return lax.ppermute(x, 'dp', [(i, i ^ m) for i in range(n_dp)])  8.42 us
    ppermute x6, starting transfers between devices, chips(): return lax.ppermute(x, 'ctx', [(i, i ^ 2 * m) for i in range(n_ctx)])  7.81 us
    ppermute x3, starting transfers between devices, to_earlier(): lax.ppermute(x, 'ctx', [(i, i ^ 2 * m) for i in range(n_ctx) if i ^ 2 * m...  3.86 us
    ppermute x6, waiting for transfers between devices, chips(): return lax.ppermute(x, 'ctx', [(i, i ^ 2 * m) for i in range(n_ctx)])  3.11 us
  transfers between devices with their start and end apart: 25, of which 6 were waited for; matrix products, arithmetic and copies ran while one was open for 0% of the time, Pallas kernels for 14%

profile of v1, /device:TPU:0, one launch (start us, length us, event | category | flops | bytes accessed | tf_op | source)
XLA Modules:
  0.0 71.5 jit_solution(735851282153882216)
XLA Ops:
  0.6 0.0 copy-start
  0.6 0.5 collective-permute-start.10
  1.2 0.1 collective-permute-start.9
  1.2 0.4 collective-permute-start.1
  1.7 0.1 collective-permute-start
  1.8 3.0 %collective-permute-start.2 = (bf16[32,1024]{1,0:T(8,128)(2,1)}, bf16[32,1024]{1,0:T(8,128)(2,1)S(1)}, u32[]{:S(2)}, u32[]{:S(2)}) collective-permute-start(bf16[32,1024]{1,0:T(8,128)(2,1)} %w_own.1), channel_id=1, source_target_pairs={{0,1},{1,0},{2,3},{3,2},{4,5},{5,4},{6,7},{7,6},{8,9},{9,8},{10,11... | collective-permute-start | bytes 196616 | tf_op jit(solution)/shard_map/ppermute | solution.py:206
  4.8 2.5 %collective-permute-done.2.rest_0_ = bf16[32,1024]{1,0:T(8,128)(2,1)S(1)} collective-permute-done((bf16[32,1024]{1,0:T(8,128)(2,1)}, bf16[32,1024]{1,0:T(8,128)(2,1)S(1)}, u32[]{:S(2)}, u32[]{:S(2)}) %collective-permute-start.2) | collective-permute-done | bytes 65568 | tf_op jit(solution)/shard_map/ppermute | solution.py:206
  7.3 2.9 %collective-permute-start.3 = (bf16[32,1024]{1,0:T(8,128)(2,1)}, bf16[32,1024]{1,0:T(8,128)(2,1)S(1)}, u32[]{:S(2)}, u32[]{:S(2)}) collective-permute-start(bf16[32,1024]{1,0:T(8,128)(2,1)} %w_own.1), channel_id=1, source_target_pairs={{0,2},{1,3},{2,0},{3,1},{4,6},{5,7},{6,4},{7,5},{8,10},{9,11},{10,... | collective-permute-start | bytes 196616 | tf_op jit(solution)/shard_map/ppermute | solution.py:206
  10.2 2.5 %collective-permute-done.3.rest_1_ = bf16[32,1024]{1,0:T(8,128)(2,1)S(1)} collective-permute-done((bf16[32,1024]{1,0:T(8,128)(2,1)}, bf16[32,1024]{1,0:T(8,128)(2,1)S(1)}, u32[]{:S(2)}, u32[]{:S(2)}) %collective-permute-start.3) | collective-permute-done | bytes 65568 | tf_op jit(solution)/shard_map/ppermute | solution.py:206
  12.7 4.5 %collective-permute-start.4 = (bf16[32,1024]{1,0:T(8,128)(2,1)}, bf16[32,1024]{1,0:T(8,128)(2,1)S(1)}, u32[]{:S(2)}, u32[]{:S(2)}) collective-permute-start(bf16[32,1024]{1,0:T(8,128)(2,1)} %w_own.1), channel_id=1, source_target_pairs={{0,3},{1,2},{2,1},{3,0},{4,7},{5,6},{6,5},{7,4},{8,11},{9,10},{10,... | collective-permute-start | bytes 196616 | tf_op jit(solution)/shard_map/ppermute | solution.py:206
  17.2 2.5 %collective-permute-done.4.rest_2_ = bf16[32,1024]{1,0:T(8,128)(2,1)S(1)} collective-permute-done((bf16[32,1024]{1,0:T(8,128)(2,1)}, bf16[32,1024]{1,0:T(8,128)(2,1)S(1)}, u32[]{:S(2)}, u32[]{:S(2)}) %collective-permute-start.4) | collective-permute-done | bytes 65568 | tf_op jit(solution)/shard_map/ppermute | solution.py:206
  19.7 0.8 %copy-done.5 = bf16[32,1024]{1,0:T(8,128)(2,1)S(1)} copy-done((bf16[32,1024]{1,0:T(8,128)(2,1)S(1)}, bf16[32,1024]{1,0:T(8,128)(2,1)}, u32[]{:S(2)}) %copy-start.5) | copy-done | bytes 65560
  20.6 1.6 %collective-permute-start.5 = (bf16[128,1024]{1,0:T(8,128)(2,1)S(1)}, bf16[128,1024]{1,0:T(8,128)(2,1)S(1)}, u32[]{:S(2)}, u32[]{:S(2)}) collective-permute-start(bf16[128,1024]{1,0:T(8,128)(2,1)S(1)} %shard_map.84.rest_0_), channel_id=1, source_target_pairs={{0,8},{4,12},{8,0},{12,4},{16,24},{20,28},{24,16},{28,20},{1,9},{5... | collective-permute-start | bytes 786440 | tf_op jit(solution)/shard_map/ppermute | solution.py:197
  22.1 0.0 collective-permute-done.10.v_r
  22.1 1.5 %collective-permute-start.6 = (bf16[128,1024]{1,0:T(8,128)(2,1)S(1)}, bf16[128,1024]{1,0:T(8,128)(2,1)S(1)}, u32[]{:S(2)}, u32[]{:S(2)}) collective-permute-start(bf16[128,1024]{1,0:T(8,128)(2,1)S(1)} %shard_map.84.rest_0_), channel_id=1, source_target_pairs={{0,16},{4,20},{8,24},{12,28},{16,0},{20,4},{24,8},{28,12},{1,17},{... | collective-permute-start | bytes 786440 | tf_op jit(solution)/shard_map/ppermute | solution.py:197
  23.6 0.0 collective-permute-done.9.k_r
  23.6 0.5 collective-permute-start.7
  24.1 0.0 copy-done
  24.1 1.0 %copy-done.1 = bf16[1,256,1024]{2,1,0:T(8,128)(2,1)S(1)} copy-done((bf16[1,256,1024]{2,1,0:T(8,128)(2,1)S(1)}, bf16[1,256,1024]{2,1,0:T(8,128)(2,1)}, u32[]{:S(2)}) %copy-start.1) | copy-done | bytes 524312
  25.2 0.5 shard_map.87
  25.7 3.1 %collective-permute-done.5.rest_1_ = bf16[128,1024]{1,0:T(8,128)(2,1)S(1)} collective-permute-done((bf16[128,1024]{1,0:T(8,128)(2,1)S(1)}, bf16[128,1024]{1,0:T(8,128)(2,1)S(1)}, u32[]{:S(2)}, u32[]{:S(2)}) %collective-permute-start.5) | collective-permute-done | bytes 262176 | tf_op jit(solution)/shard_map/ppermute | solution.py:197
  28.8 4.5 %collective-permute-start.11 = (bf16[4,128,128]{2,1,0:T(8,128)(2,1)S(1)}, bf16[4,128,128]{2,1,0:T(8,128)(2,1)S(1)}, u32[]{:S(2)}, u32[]{:S(2)}) collective-permute-start(bf16[4,128,128]{2,1,0:T(8,128)(2,1)S(1)} %get-tuple-element.26), channel_id=1, source_target_pairs={{0,8},{4,12},{16,24},{20,28},{1,9},{5,13},{17,25},{21,29},{2,10},{... | collective-permute-start | bytes 393224 | tf_op jit(solution)/shard_map/ppermute | solution.py:200
  33.3 0.0 collective-permute-done.6.rest_2_
  33.3 3.3 %collective-permute-start.12 = (bf16[4,128,128]{2,1,0:T(8,128)(2,1)S(1)}, bf16[4,128,128]{2,1,0:T(8,128)(2,1)S(1)}, u32[]{:S(2)}, u32[]{:S(2)}) collective-permute-start(bf16[4,128,128]{2,1,0:T(8,128)(2,1)S(1)} %get-tuple-element.26), channel_id=1, source_target_pairs={{0,16},{4,20},{8,24},{12,28},{1,17},{5,21},{9,25},{13,29},{2,18},{... | collective-permute-start | bytes 393224 | tf_op jit(solution)/shard_map/ppermute | solution.py:200
  36.6 0.0 collective-permute-done.7.rest_3_
  36.7 1.3 %collective-permute-start.13 = (bf16[4,128,128]{2,1,0:T(8,128)(2,1)S(1)}, bf16[4,128,128]{2,1,0:T(8,128)(2,1)S(1)}, u32[]{:S(2)}, u32[]{:S(2)}) collective-permute-start(bf16[4,128,128]{2,1,0:T(8,128)(2,1)S(1)} %get-tuple-element.26), channel_id=1, source_target_pairs={{0,24},{4,28},{8,16},{12,20},{1,25},{5,29},{9,17},{13,21},{2,26},{... | collective-permute-start | bytes 393224 | tf_op jit(solution)/shard_map/ppermute | solution.py:200
  38.0 0.0 collective-permute-done.1.q_r
  38.0 0.0 collective-permute-done.g_r
  38.0 2.1 %shard_map.85 = (bf16[256,512]{1,0:T(8,128)(2,1)S(1)}, bf16[256,512]{1,0:T(8,128)(2,1)S(1)}, f32[4,128,128]{2,1,0:T(8,128)S(1)}, bf16[4,128,128]{2,1,0:T(8,128)(2,1)S(1)}) custom-call(bf16[256,1024]{1,0:T(8,128)(2,1)S(1)} %bitcast.35, bf16[256,1024]{1,0:T(8,128)(2,1)S(1)} %collective-permute-done.g_r, bf16[256,1024]{1,0:T(8,128)(2,1)S(1)} %bitcast.30, ...), custom_call_target="tpu_custom_call" | custom-call | flops 603979776 | bytes 4063232 | tf_op jit(solution)/shard_map/pallas_call | solution.py:52
  40.1 1.3 %collective-permute-start.15 = (bf16[4,128,128]{2,1,0:T(8,128)(2,1)S(1)}, bf16[4,128,128]{2,1,0:T(8,128)(2,1)S(1)}, u32[]{:S(2)}, u32[]{:S(2)}) collective-permute-start(bf16[4,128,128]{2,1,0:T(8,128)(2,1)S(1)} %get-tuple-element.31), channel_id=1, source_target_pairs={{8,0},{12,4},{24,16},{28,20},{9,1},{13,5},{25,17},{29,21},{10,2},{... | collective-permute-start | bytes 393224 | tf_op jit(solution)/shard_map/ppermute | solution.py:203
  41.4 0.9 %shard_map.86.intra = f32[2,256,512]{2,1,0:T(8,128)S(1)} custom-call(bf16[256,1024]{1,0:T(8,128)(2,1)S(1)} %bitcast.31, bf16[256,1024]{1,0:T(8,128)(2,1)S(1)} %bitcast.21, bf16[256,1024]{1,0:T(8,128)(2,1)S(1)} %bitcast.26, bf16[256,1024]{1,0:T(8,128)(2,1)S(1)} %collective-permute-done.1.q_r, bf16[256,1024]{1,0:T(8,128)(2,1)S(1)} %collective-permute-done.9.k_r, ...), custom_call_target="tpu_custom_call" | custom-call | flops 268435456 | bytes 4194304 | tf_op jit(solution)/shard_map/pallas_call | solution.py:52
  42.4 0.0 collective-permute-done.11.rest_0_
  42.4 0.0 collective-permute-done.12.rest_1_
  42.4 0.0 collective-permute-done.13.rest_2_
  42.4 1.6 %shard_map.88 = (f32[128,1024]{1,0:T(8,128)S(1)}, bf16[3,128,1024]{2,1,0:T(8,128)(2,1)S(1)}, bf16[4,128,128]{2,1,0:T(8,128)(2,1)S(1)}, bf16[4,128,128]{2,1,0:T(8,128)(2,1)S(1)}) custom-call(bf16[256,1024]{1,0:T(8,128)(2,1)S(1)} %bitcast.32, bf16[256,1024]{1,0:T(8,128)(2,1)S(1)} %collective-permute-done.1.q_r, bf16[256,1024]{1,0:T(8,128)(2,1)S(1)} %bitcast.36, ...), custom_call_target="tpu_custom_call" | custom-call | flops 603979776 | bytes 5373952 | tf_op jit(solution)/shard_map/pallas_call | solution.py:52
  44.0 0.1 slice_bitcast_fusion
  44.1 2.7 %collective-permute-start.19 = (bf16[128,1024]{1,0:T(8,128)(2,1)S(1)}, bf16[128,1024]{1,0:T(8,128)(2,1)S(1)}, u32[]{:S(2)}, u32[]{:S(2)}) collective-permute-start(bf16[128,1024]{1,0:T(8,128)(2,1)S(1)} %get-tuple-element.44), channel_id=1, source_target_pairs={{0,8},{4,12},{8,0},{12,4},{16,24},{20,28},{24,16},{28,20},{1,9},{5... | collective-permute-start | bytes 786440 | tf_op jit(solution)/shard_map/ppermute | solution.py:197
  46.8 0.0 collective-permute-start.20
  46.8 1.5 %collective-permute-start.21 = (bf16[128,1024]{1,0:T(8,128)(2,1)S(1)}, bf16[128,1024]{1,0:T(8,128)(2,1)S(1)}, u32[]{:S(2)}, u32[]{:S(2)}) collective-permute-start(bf16[128,1024]{1,0:T(8,128)(2,1)S(1)} %get-tuple-element.42), channel_id=1, source_target_pairs={{0,24},{4,28},{8,16},{12,20},{16,8},{20,12},{24,0},{28,4},{1,25},{... | collective-permute-start | bytes 786440 | tf_op jit(solution)/shard_map/ppermute | solution.py:197
  48.3 1.3 %collective-permute-start.16 = (bf16[4,128,128]{2,1,0:T(8,128)(2,1)S(1)}, bf16[4,128,128]{2,1,0:T(8,128)(2,1)S(1)}, u32[]{:S(2)}, u32[]{:S(2)}) collective-permute-start(bf16[4,128,128]{2,1,0:T(8,128)(2,1)S(1)} %get-tuple-element.31), channel_id=1, source_target_pairs={{16,0},{20,4},{24,8},{28,12},{17,1},{21,5},{25,9},{29,13},{18,2},{... | collective-permute-start | bytes 393224 | tf_op jit(solution)/shard_map/ppermute | solution.py:203
  49.6 0.0 collective-permute-done.15.rest_0_
  49.6 1.3 %collective-permute-start.17 = (bf16[4,128,128]{2,1,0:T(8,128)(2,1)S(1)}, bf16[4,128,128]{2,1,0:T(8,128)(2,1)S(1)}, u32[]{:S(2)}, u32[]{:S(2)}) collective-permute-start(bf16[4,128,128]{2,1,0:T(8,128)(2,1)S(1)} %get-tuple-element.31), channel_id=1, source_target_pairs={{16,8},{20,12},{24,0},{28,4},{17,9},{21,13},{25,1},{29,5},{18,10},... | collective-permute-start | bytes 393224 | tf_op jit(solution)/shard_map/ppermute | solution.py:203
  50.9 8.7 %collective-permute-done.16.rest_1_ = bf16[4,128,128]{2,1,0:T(8,128)(2,1)S(1)} collective-permute-done((bf16[4,128,128]{2,1,0:T(8,128)(2,1)S(1)}, bf16[4,128,128]{2,1,0:T(8,128)(2,1)S(1)}, u32[]{:S(2)}, u32[]{:S(2)}) %collective-permute-start.16) | collective-permute-done | bytes 131104 | tf_op jit(solution)/shard_map/ppermute | solution.py:203
  59.7 0.0 collective-permute-start.8
  59.7 0.0 collective-permute-done.17.rest_2_
  59.7 0.1 shard_map.90
  59.8 0.6 collective-permute-start.18
  60.3 0.0 collective-permute-done.19.rest_0_
  60.3 0.1 collective-permute-start.14
  60.4 0.0 collective-permute-done.20.rest_1_
  60.4 0.0 collective-permute-done.21.rest_2_
  60.4 0.1 shard_map.92
  60.6 0.1 collective-permute-start.22
  60.6 4.1 %collective-permute-start.23 = (bf16[32,1024]{1,0:T(8,128)(2,1)S(1)}, bf16[32,1024]{1,0:T(8,128)(2,1)S(1)}, u32[]{:S(2)}, u32[]{:S(2)}) collective-permute-start(bf16[32,1024]{1,0:T(8,128)(2,1)S(1)} %get-tuple-element.47), channel_id=1, source_target_pairs={{0,2},{1,3},{2,0},{3,1},{4,6},{5,7},{6,4},{7,5},{8,10},{9,11},{10,... | collective-permute-start | bytes 196616 | tf_op jit(solution)/shard_map/ppermute | solution.py:206
  64.7 0.0 collective-permute-done.8.ag_p
  64.7 0.3 collective-permute-start.24
  65.0 0.0 collective-permute-done.14.st_p
  65.0 3.3 %shard_map.89 = (bf16[256,1024]{1,0:T(8,128)(2,1)}, f32[256,1024]{1,0:T(8,128)S(1)}, f32[256,1024]{1,0:T(8,128)S(1)}) custom-call(bf16[256,1024]{1,0:T(8,128)(2,1)S(1)} %bitcast.33, bf16[256,1024]{1,0:T(8,128)(2,1)S(1)} %bitcast.22, bf16[256,1024]{1,0:T(8,128)(2,1)S(1)} %bitcast.27, bf16[256,512]{1,0:T(8,128)(2,1)S(1)} %get-tuple-element.23.ag_o, ...), custom_call_target="tpu_custom_call" | custom-call | flops 738197504 | bytes 4980736 | tf_op jit(solution)/shard_map/pallas_call | solution.py:52
  68.3 0.0 collective-permute-done.18.car_p
  68.3 1.6 %shard_map.91 = (bf16[256,1024]{1,0:T(8,128)(2,1)}, bf16[256,1024]{1,0:T(8,128)(2,1)}) custom-call(bf16[256,1024]{1,0:T(8,128)(2,1)S(1)} %bitcast.23, bf16[256,1024]{1,0:T(8,128)(2,1)S(1)} %bitcast.28, bf16[4,128,128]{2,1,0:T(8,128)(2,1)S(1)} %get-tuple-element.32.car_o, bf16[4,128,128]{2,1,0:T(8,128)(2,1)S(1)} %collective-permute-done.18.car_p, ...), custom_call_target="tpu_custom_call" | custom-call | flops 134217728 | bytes 4456448 | tf_op jit(solution)/shard_map/pallas_call | solution.py:52
  69.9 0.0 collective-permute-done.22
  69.9 0.0 collective-permute-done.23
  69.9 1.0 %collective-permute-done.24 = bf16[32,1024]{1,0:T(8,128)(2,1)S(1)} collective-permute-done((bf16[32,1024]{1,0:T(8,128)(2,1)S(1)}, bf16[32,1024]{1,0:T(8,128)(2,1)S(1)}, u32[]{:S(2)}, u32[]{:S(2)}) %collective-permute-start.24) | collective-permute-done | bytes 65568 | tf_op jit(solution)/shard_map/ppermute | solution.py:206
  70.9 0.7 convert_add_fusion
  (10 shorter events, 0.1 us)
Async XLA Ops:
  0.6 23.5 %copy-start = (bf16[1,256,1024]{2,1,0:T(8,128)(2,1)S(1)}, bf16[1,256,1024]{2,1,0:T(8,128)(2,1)}, u32[]{:S(2)}) copy-start(bf16[1,256,1024]{2,1,0:T(8,128)(2,1)} %param.6) | copy-start | bytes 1572868
  0.6 21.5 %collective-permute-start.10 = (bf16[256,1024]{1,0:T(8,128)(2,1)}, bf16[256,1024]{1,0:T(8,128)(2,1)S(1)}, u32[]{:S(2)}, u32[]{:S(2)}) collective-permute-start(bf16[256,1024]{1,0:T(8,128)(2,1)} %bitcast.24), channel_id=1, source_target_pairs={{0,4},{4,0},{8,12},{12,8},{16,20},{20,16},{24,28},{28,24},{1,5},{5... | collective-permute-start | bytes 1572872 | tf_op jit(solution)/shard_map/ppermute | solution.py:194
  1.2 22.5 %collective-permute-start.9 = (bf16[256,1024]{1,0:T(8,128)(2,1)}, bf16[256,1024]{1,0:T(8,128)(2,1)S(1)}, u32[]{:S(2)}, u32[]{:S(2)}) collective-permute-start(bf16[256,1024]{1,0:T(8,128)(2,1)} %bitcast.19), channel_id=1, source_target_pairs={{0,4},{4,0},{8,12},{12,8},{16,20},{20,16},{24,28},{28,24},{1,5},{5... | collective-permute-start | bytes 1572872 | tf_op jit(solution)/shard_map/ppermute | solution.py:194
  1.2 36.7 %collective-permute-start.1 = (bf16[256,1024]{1,0:T(8,128)(2,1)}, bf16[256,1024]{1,0:T(8,128)(2,1)S(1)}, u32[]{:S(2)}, u32[]{:S(2)}) collective-permute-start(bf16[256,1024]{1,0:T(8,128)(2,1)} %bitcast.29), channel_id=1, source_target_pairs={{0,4},{4,0},{8,12},{12,8},{16,20},{20,16},{24,28},{28,24},{1,5},{5... | collective-permute-start | bytes 1572872 | tf_op jit(solution)/shard_map/ppermute | solution.py:194
  1.7 36.3 %collective-permute-start = (bf16[256,1024]{1,0:T(8,128)(2,1)}, bf16[256,1024]{1,0:T(8,128)(2,1)S(1)}, u32[]{:S(2)}, u32[]{:S(2)}) collective-permute-start(bf16[256,1024]{1,0:T(8,128)(2,1)} %bitcast.34), channel_id=1, source_target_pairs={{0,4},{4,0},{8,12},{12,8},{16,20},{20,16},{24,28},{28,24},{1,5},{5... | collective-permute-start | bytes 1572872 | tf_op jit(solution)/shard_map/ppermute | solution.py:194
  1.8 5.5 %collective-permute-start.2 = (bf16[32,1024]{1,0:T(8,128)(2,1)}, bf16[32,1024]{1,0:T(8,128)(2,1)S(1)}, u32[]{:S(2)}, u32[]{:S(2)}) collective-permute-start(bf16[32,1024]{1,0:T(8,128)(2,1)} %w_own.1), channel_id=1, source_target_pairs={{0,1},{1,0},{2,3},{3,2},{4,5},{5,4},{6,7},{7,6},{8,9},{9,8},{10,11... | collective-permute-start | bytes 196616 | tf_op jit(solution)/shard_map/ppermute | solution.py:206
  7.3 5.4 %collective-permute-start.3 = (bf16[32,1024]{1,0:T(8,128)(2,1)}, bf16[32,1024]{1,0:T(8,128)(2,1)S(1)}, u32[]{:S(2)}, u32[]{:S(2)}) collective-permute-start(bf16[32,1024]{1,0:T(8,128)(2,1)} %w_own.1), channel_id=1, source_target_pairs={{0,2},{1,3},{2,0},{3,1},{4,6},{5,7},{6,4},{7,5},{8,10},{9,11},{10,... | collective-permute-start | bytes 196616 | tf_op jit(solution)/shard_map/ppermute | solution.py:206
  12.7 7.0 %collective-permute-start.4 = (bf16[32,1024]{1,0:T(8,128)(2,1)}, bf16[32,1024]{1,0:T(8,128)(2,1)S(1)}, u32[]{:S(2)}, u32[]{:S(2)}) collective-permute-start(bf16[32,1024]{1,0:T(8,128)(2,1)} %w_own.1), channel_id=1, source_target_pairs={{0,3},{1,2},{2,1},{3,0},{4,7},{5,6},{6,5},{7,4},{8,11},{9,10},{10,... | collective-permute-start | bytes 196616 | tf_op jit(solution)/shard_map/ppermute | solution.py:206
  19.7 0.8 %copy-start.5 = (bf16[32,1024]{1,0:T(8,128)(2,1)S(1)}, bf16[32,1024]{1,0:T(8,128)(2,1)}, u32[]{:S(2)}) copy-start(bf16[32,1024]{1,0:T(8,128)(2,1)} %w_own.1) | copy-start | bytes 196612
  20.6 8.2 %collective-permute-start.5 = (bf16[128,1024]{1,0:T(8,128)(2,1)S(1)}, bf16[128,1024]{1,0:T(8,128)(2,1)S(1)}, u32[]{:S(2)}, u32[]{:S(2)}) collective-permute-start(bf16[128,1024]{1,0:T(8,128)(2,1)S(1)} %shard_map.84.rest_0_), channel_id=1, source_target_pairs={{0,8},{4,12},{8,0},{12,4},{16,24},{20,28},{24,16},{28,20},{1,9},{5... | collective-permute-start | bytes 786440 | tf_op jit(solution)/shard_map/ppermute | solution.py:197
  22.1 11.2 %collective-permute-start.6 = (bf16[128,1024]{1,0:T(8,128)(2,1)S(1)}, bf16[128,1024]{1,0:T(8,128)(2,1)S(1)}, u32[]{:S(2)}, u32[]{:S(2)}) collective-permute-start(bf16[128,1024]{1,0:T(8,128)(2,1)S(1)} %shard_map.84.rest_0_), channel_id=1, source_target_pairs={{0,16},{4,20},{8,24},{12,28},{16,0},{20,4},{24,8},{28,12},{1,17},{... | collective-permute-start | bytes 786440 | tf_op jit(solution)/shard_map/ppermute | solution.py:197
  23.6 13.0 %collective-permute-start.7 = (bf16[128,1024]{1,0:T(8,128)(2,1)S(1)}, bf16[128,1024]{1,0:T(8,128)(2,1)S(1)}, u32[]{:S(2)}, u32[]{:S(2)}) collective-permute-start(bf16[128,1024]{1,0:T(8,128)(2,1)S(1)} %shard_map.84.rest_0_), channel_id=1, source_target_pairs={{0,24},{4,28},{8,16},{12,20},{16,8},{20,12},{24,0},{28,4},{1,25},{... | collective-permute-start | bytes 786440 | tf_op jit(solution)/shard_map/ppermute | solution.py:197
  24.1 1.0 %copy-start.1 = (bf16[1,256,1024]{2,1,0:T(8,128)(2,1)S(1)}, bf16[1,256,1024]{2,1,0:T(8,128)(2,1)}, u32[]{:S(2)}) copy-start(bf16[1,256,1024]{2,1,0:T(8,128)(2,1)} %param.7) | copy-start | bytes 1572868
  25.2 12.8 %copy-start.3 = (bf16[1,256,1024]{2,1,0:T(8,128)(2,1)S(1)}, bf16[1,256,1024]{2,1,0:T(8,128)(2,1)}, u32[]{:S(2)}) copy-start(bf16[1,256,1024]{2,1,0:T(8,128)(2,1)} %param.5) | copy-start | bytes 1572868
  25.2 12.8 %copy-start.4 = (bf16[1,256,1024]{2,1,0:T(8,128)(2,1)S(1)}, bf16[1,256,1024]{2,1,0:T(8,128)(2,1)}, u32[]{:S(2)}) copy-start(bf16[1,256,1024]{2,1,0:T(8,128)(2,1)} %param.8) | copy-start | bytes 1572868
  28.8 12.7 %copy-start.2 = (bf16[1,256,1024]{2,1,0:T(8,128)(2,1)S(1)}, bf16[1,256,1024]{2,1,0:T(8,128)(2,1)}, u32[]{:S(2)}) copy-start(bf16[1,256,1024]{2,1,0:T(8,128)(2,1)} %param.7) | copy-start | bytes 1572868
  28.8 13.6 %collective-permute-start.11 = (bf16[4,128,128]{2,1,0:T(8,128)(2,1)S(1)}, bf16[4,128,128]{2,1,0:T(8,128)(2,1)S(1)}, u32[]{:S(2)}, u32[]{:S(2)}) collective-permute-start(bf16[4,128,128]{2,1,0:T(8,128)(2,1)S(1)} %get-tuple-element.26), channel_id=1, source_target_pairs={{0,8},{4,12},{16,24},{20,28},{1,9},{5,13},{17,25},{21,29},{2,10},{... | collective-permute-start | bytes 393224 | tf_op jit(solution)/shard_map/ppermute | solution.py:200
  33.3 9.1 %collective-permute-start.12 = (bf16[4,128,128]{2,1,0:T(8,128)(2,1)S(1)}, bf16[4,128,128]{2,1,0:T(8,128)(2,1)S(1)}, u32[]{:S(2)}, u32[]{:S(2)}) collective-permute-start(bf16[4,128,128]{2,1,0:T(8,128)(2,1)S(1)} %get-tuple-element.26), channel_id=1, source_target_pairs={{0,16},{4,20},{8,24},{12,28},{1,17},{5,21},{9,25},{13,29},{2,18},{... | collective-permute-start | bytes 393224 | tf_op jit(solution)/shard_map/ppermute | solution.py:200
  36.7 5.8 %collective-permute-start.13 = (bf16[4,128,128]{2,1,0:T(8,128)(2,1)S(1)}, bf16[4,128,128]{2,1,0:T(8,128)(2,1)S(1)}, u32[]{:S(2)}, u32[]{:S(2)}) collective-permute-start(bf16[4,128,128]{2,1,0:T(8,128)(2,1)S(1)} %get-tuple-element.26), channel_id=1, source_target_pairs={{0,24},{4,28},{8,16},{12,20},{1,25},{5,29},{9,17},{13,21},{2,26},{... | collective-permute-start | bytes 393224 | tf_op jit(solution)/shard_map/ppermute | solution.py:200
  40.1 9.5 %collective-permute-start.15 = (bf16[4,128,128]{2,1,0:T(8,128)(2,1)S(1)}, bf16[4,128,128]{2,1,0:T(8,128)(2,1)S(1)}, u32[]{:S(2)}, u32[]{:S(2)}) collective-permute-start(bf16[4,128,128]{2,1,0:T(8,128)(2,1)S(1)} %get-tuple-element.31), channel_id=1, source_target_pairs={{8,0},{12,4},{24,16},{28,20},{9,1},{13,5},{25,17},{29,21},{10,2},{... | collective-permute-start | bytes 393224 | tf_op jit(solution)/shard_map/ppermute | solution.py:203
  44.1 16.3 %collective-permute-start.19 = (bf16[128,1024]{1,0:T(8,128)(2,1)S(1)}, bf16[128,1024]{1,0:T(8,128)(2,1)S(1)}, u32[]{:S(2)}, u32[]{:S(2)}) collective-permute-start(bf16[128,1024]{1,0:T(8,128)(2,1)S(1)} %get-tuple-element.44), channel_id=1, source_target_pairs={{0,8},{4,12},{8,0},{12,4},{16,24},{20,28},{24,16},{28,20},{1,9},{5... | collective-permute-start | bytes 786440 | tf_op jit(solution)/shard_map/ppermute | solution.py:197
  46.8 13.6 %collective-permute-start.20 = (bf16[128,1024]{1,0:T(8,128)(2,1)S(1)}, bf16[128,1024]{1,0:T(8,128)(2,1)S(1)}, u32[]{:S(2)}, u32[]{:S(2)}) collective-permute-start(bf16[128,1024]{1,0:T(8,128)(2,1)S(1)} %get-tuple-element.43), channel_id=1, source_target_pairs={{0,16},{4,20},{8,24},{12,28},{16,0},{20,4},{24,8},{28,12},{1,17},{... | collective-permute-start | bytes 786440 | tf_op jit(solution)/shard_map/ppermute | solution.py:197
  46.8 13.6 %collective-permute-start.21 = (bf16[128,1024]{1,0:T(8,128)(2,1)S(1)}, bf16[128,1024]{1,0:T(8,128)(2,1)S(1)}, u32[]{:S(2)}, u32[]{:S(2)}) collective-permute-start(bf16[128,1024]{1,0:T(8,128)(2,1)S(1)} %get-tuple-element.42), channel_id=1, source_target_pairs={{0,24},{4,28},{8,16},{12,20},{16,8},{20,12},{24,0},{28,4},{1,25},{... | collective-permute-start | bytes 786440 | tf_op jit(solution)/shard_map/ppermute | solution.py:197
  48.3 11.3 %collective-permute-start.16 = (bf16[4,128,128]{2,1,0:T(8,128)(2,1)S(1)}, bf16[4,128,128]{2,1,0:T(8,128)(2,1)S(1)}, u32[]{:S(2)}, u32[]{:S(2)}) collective-permute-start(bf16[4,128,128]{2,1,0:T(8,128)(2,1)S(1)} %get-tuple-element.31), channel_id=1, source_target_pairs={{16,0},{20,4},{24,8},{28,12},{17,1},{21,5},{25,9},{29,13},{18,2},{... | collective-permute-start | bytes 393224 | tf_op jit(solution)/shard_map/ppermute | solution.py:203
  49.6 10.0 %collective-permute-start.17 = (bf16[4,128,128]{2,1,0:T(8,128)(2,1)S(1)}, bf16[4,128,128]{2,1,0:T(8,128)(2,1)S(1)}, u32[]{:S(2)}, u32[]{:S(2)}) collective-permute-start(bf16[4,128,128]{2,1,0:T(8,128)(2,1)S(1)} %get-tuple-element.31), channel_id=1, source_target_pairs={{16,8},{20,12},{24,0},{28,4},{17,9},{21,13},{25,1},{29,5},{18,10},... | collective-permute-start | bytes 393224 | tf_op jit(solution)/shard_map/ppermute | solution.py:203
  59.7 5.1 %collective-permute-start.8 = (bf16[256,512]{1,0:T(8,128)(2,1)S(1)}, bf16[256,512]{1,0:T(8,128)(2,1)S(1)}, u32[]{:S(2)}, u32[]{:S(2)}) collective-permute-start(bf16[256,512]{1,0:T(8,128)(2,1)S(1)} %get-tuple-element.24), channel_id=1, source_target_pairs={{0,4},{4,0},{8,12},{12,8},{16,20},{20,16},{24,28},{28,24},{1,5},{5... | collective-permute-start | bytes 786440 | tf_op jit(solution)/shard_map/ppermute | solution.py:194
  59.8 8.6 %collective-permute-start.18 = (bf16[4,128,128]{2,1,0:T(8,128)(2,1)S(1)}, bf16[4,128,128]{2,1,0:T(8,128)(2,1)S(1)}, u32[]{:S(2)}, u32[]{:S(2)}) collective-permute-start(bf16[4,128,128]{2,1,0:T(8,128)(2,1)S(1)} %get-tuple-element.33), channel_id=1, source_target_pairs={{0,4},{4,0},{8,12},{12,8},{16,20},{20,16},{24,28},{28,24},{1,5},{5... | collective-permute-start | bytes 393224 | tf_op jit(solution)/shard_map/ppermute | solution.py:194
  60.3 4.7 %collective-permute-start.14 = (bf16[4,128,128]{2,1,0:T(8,128)(2,1)S(1)}, bf16[4,128,128]{2,1,0:T(8,128)(2,1)S(1)}, u32[]{:S(2)}, u32[]{:S(2)}) collective-permute-start(bf16[4,128,128]{2,1,0:T(8,128)(2,1)S(1)} %get-tuple-element.28), channel_id=1, source_target_pairs={{0,4},{4,0},{8,12},{12,8},{16,20},{20,16},{24,28},{28,24},{1,5},{5... | collective-permute-start | bytes 393224 | tf_op jit(solution)/shard_map/ppermute | solution.py:194
  60.6 9.3 %collective-permute-start.22 = (bf16[32,1024]{1,0:T(8,128)(2,1)S(1)}, bf16[32,1024]{1,0:T(8,128)(2,1)S(1)}, u32[]{:S(2)}, u32[]{:S(2)}) collective-permute-start(bf16[32,1024]{1,0:T(8,128)(2,1)S(1)} %get-tuple-element.45), channel_id=1, source_target_pairs={{0,1},{1,0},{2,3},{3,2},{4,5},{5,4},{6,7},{7,6},{8,9},{9,8},{10,11... | collective-permute-start | bytes 196616 | tf_op jit(solution)/shard_map/ppermute | solution.py:206
  60.6 9.3 %collective-permute-start.23 = (bf16[32,1024]{1,0:T(8,128)(2,1)S(1)}, bf16[32,1024]{1,0:T(8,128)(2,1)S(1)}, u32[]{:S(2)}, u32[]{:S(2)}) collective-permute-start(bf16[32,1024]{1,0:T(8,128)(2,1)S(1)} %get-tuple-element.47), channel_id=1, source_target_pairs={{0,2},{1,3},{2,0},{3,1},{4,6},{5,7},{6,4},{7,5},{8,10},{9,11},{10,... | collective-permute-start | bytes 196616 | tf_op jit(solution)/shard_map/ppermute | solution.py:206
  64.7 6.1 %collective-permute-start.24 = (bf16[32,1024]{1,0:T(8,128)(2,1)S(1)}, bf16[32,1024]{1,0:T(8,128)(2,1)S(1)}, u32[]{:S(2)}, u32[]{:S(2)}) collective-permute-start(bf16[32,1024]{1,0:T(8,128)(2,1)S(1)} %get-tuple-element.46), channel_id=1, source_target_pairs={{0,3},{1,2},{2,1},{3,0},{4,7},{5,6},{6,5},{7,4},{8,11},{9,10},{10,... | collective-permute-start | bytes 196616 | tf_op jit(solution)/shard_map/ppermute | solution.py:206

commit v2 on v0

--- a/solution.py
+++ b/solution.py
@@ -1,19 +1,340 @@
+import functools
 import math
 
 import jax
 import jax.numpy as jnp
 from jax import lax
+from jax.experimental import pallas as pl
+from jax.experimental.pallas import tpu as pltpu
 from jax.sharding import PartitionSpec as P
 
 HEAD = 128
 BLOCK = 256
+GROUPS = 4
+BF = jnp.bfloat16
+F32 = jnp.float32
 
 
 def ein(form, left, right):
     return jnp.einsum(form, left, right, preferred_element_type=jnp.float32)
 
 
-def per_device(queries, key_vecs, value_vecs, out_grad, out_weight):
+def nn(a, b):
+    return lax.dot_general(a, b, (((1,), (0,)), ((), ())), preferred_element_type=F32)
+
+
+def nt(a, b):
+    return lax.dot_general(a, b, (((1,), (1,)), ((), ())), preferred_element_type=F32)
+
+
+def tn(a, b):
+    return lax.dot_general(a, b, (((0,), (0,)), ((), ())), preferred_element_type=F32)
+
+
+def cols(index):
+    return pl.ds(pl.multiple_of(index * HEAD, HEAD), HEAD)
+
+
+def causal_mask():
+    t = lax.broadcasted_iota(jnp.int32, (BLOCK, BLOCK), 0)
+    s = lax.broadcasted_iota(jnp.int32, (BLOCK, BLOCK), 1)
+    return t >= s
+
+
+def place():
+    me = lax.axis_index("ctx")
+    return lax.rem(me, 2), lax.div(me, 2)
+
+
+def local_call(kernel, outs, *args, after=(), in_place=0, scratch=(), limit=24, micros=0):
+    vmem = pl.BlockSpec(memory_space=pltpu.VMEM)
+    hbm = pl.BlockSpec(memory_space=pltpu.HBM)
+    anywhere = pl.BlockSpec(memory_space=pl.ANY)
+    count = len(args)
+
+    def body(*refs):
+        kernel(*refs[:count], *refs[count + len(after) :])
+
+    return pl.pallas_call(
+        body,
+        out_shape=[jax.ShapeDtypeStruct(s, d) for s, d in outs],
+        in_specs=[vmem] * (count - in_place) + [hbm] * in_place + [anywhere] * len(after),
+        out_specs=[vmem] * len(outs),
+        scratch_shapes=scratch,
+        compiler_params=pltpu.CompilerParams(vmem_limit_bytes=limit << 20),
+        cost_estimate=pl.CostEstimate(
+            flops=0, bytes_accessed=micros * 3_600_000, transcendentals=0
+        ),
+    )(*args, *after)
+
+
+def kv_kernel(kv_o, kv_r, w_o, w_again, kvsel, psum, psum_sent):
+    par, _ = place()
+    later = par.astype(F32)
+    for j in range(GROUPS):
+        c = cols(2 * j + par)
+        own = tn(kv_o[0, :, c], kv_o[1, :, c])
+        other = tn(kv_r[0, :, c], kv_r[1, :, c])
+        kvsel[j] = other * later + own * (1.0 - later)
+        psum[j] = own + other
+        psum_sent[j] = (own + other).astype(BF)
+    w_again[...] = w_o[...]
+
+
+def total_kernel(psum, received, total):
+    total[...] = (psum[...] + received[...].astype(F32)).astype(BF)
+
+
+def intra_kernel(qg_o, kv_o, qg_r, kv_r, intra):
+    par, _ = place()
+    mask = causal_mask()
+    for i, (qg, kv) in enumerate(((qg_o, kv_o), (qg_r, kv_r))):
+        for j in range(GROUPS):
+            c = cols(2 * j + par)
+            scores = jnp.where(mask, nt(qg[0, :, c], kv[0, :, c]), 0.0).astype(BF)
+            intra[i, :, j * HEAD : (j + 1) * HEAD] = nn(scores, kv[1, :, c])
+
+
+def attend_kernel(
+    att_scale, inv_root, qg_o, qg_r, intra, kvsel, kv_x, kv_y,
+    to_x, to_y, keep, forward, state_o, state_r,
+):
+    par, chip = place()
+    later = par.astype(F32)
+    x_later = lax.rem(chip, 2).astype(F32)
+    half = qg_o.shape[2] // 2
+    for m in (3, 1, 2, 0):
+        j = lax.bitwise_xor(chip, m)
+        earlier = kv_x[j].astype(F32) * x_later + kv_y[j].astype(F32)
+        sel = kvsel[j]
+        s_o = (earlier + later * sel).astype(BF)
+        s_r = (earlier + (1.0 - later) * sel).astype(BF)
+        state_o[j] = s_o
+        state_r[j] = s_r
+        c = cols(2 * j + par)
+        a_o = (att_scale * (intra[0, :, cols(j)] + nn(qg_o[0, :, c], s_o))).astype(BF)
+        a_r = (att_scale * (intra[1, :, cols(j)] + nn(qg_r[0, :, c], s_r))).astype(BF)
+        term = (tn(a_o, qg_o[1]) + tn(a_r, qg_r[1])) * inv_root
+        first, second = term[:, :half], term[:, half:]
+        if m == 3:
+            to_x[1], to_y[1] = first.astype(BF), second.astype(BF)
+        elif m == 1:
+            to_x[0], forward[1] = first.astype(BF), second
+        elif m == 2:
+            forward[0], to_y[0] = first, second.astype(BF)
+        else:
+            keep[...] = term
+
+
+def forward_kernel(side, forward, received, total):
+    total[...] = (forward[side] + received[1].astype(F32)).astype(BF)
+
+
+def fold_kernel(n_dp, keep, from_x, from_y, last_y, last_x, own, *send):
+    rows = own.shape[0]
+    half = keep.shape[1] // 2
+    d = lax.axis_index("dp")
+    for m in range(n_dp):
+        at = pl.ds(pl.multiple_of(lax.bitwise_xor(d, m) * rows, rows), rows)
+        for side, (one, two) in enumerate(((from_x, last_y), (from_y, last_x))):
+            c = slice(side * half, (side + 1) * half)
+            total = keep[at, c] + one[0, at, :].astype(F32) + two[at, :].astype(F32)
+            if m == 0:
+                own[:, c] = total
+            else:
+                send[m - 1][:, c] = total.astype(BF)
+
+
+def sum_kernel(own, *rest):
+    parts, (total, done) = rest[:-2], rest[-2:]
+    done[...] = jnp.zeros_like(done)
+    total[...] = own[...] + sum(part[...].astype(F32) for part in parts)
+
+
+def order_kernel(n_dp, first, *refs):
+    parts, full = refs[:-1], refs[-1]
+    rows = full.shape[0] // n_dp
+    d = lax.axis_index("dp")
+    if first:
+        full[...] = parts[0][...]
+        parts = parts[1:]
+    for m, part in enumerate(parts, first):
+        at = pl.multiple_of(lax.bitwise_xor(d, m) * rows, rows)
+        full[pl.ds(at, rows), :] = part[...]
+
+
+def att_grad_kernel(qg_o, qg_r, w_0, w_x, w_y, w_d0, w_d1, ag_o, ag_r, qdsel, psum, psum_sent):
+    par, chip = place()
+    later = par.astype(F32)
+    for m, weight in enumerate((w_0, w_x, w_y, None)):
+        j = lax.bitwise_xor(chip, m)
+        if weight is None:
+            a_o, a_r = (
+                jnp.concatenate([nt(g[1], w_d0[...]), nt(g[1], w_d1[...])], axis=1).astype(BF)
+                for g in (qg_o, qg_r)
+            )
+        else:
+            a_o, a_r = (nt(g[1], weight[...]).astype(BF) for g in (qg_o, qg_r))
+        ag_o[:, cols(j)] = a_o
+        ag_r[:, cols(j)] = a_r
+        c = cols(2 * j + par)
+        own = tn(a_o, qg_o[0, :, c])
+        other = tn(a_r, qg_r[0, :, c])
+        qdsel[j] = own * later + other * (1.0 - later)
+        psum[j] = own + other
+        psum_sent[j] = (own + other).astype(BF)
+
+
+def block_kernel(att_scale, qg_o, kv_o, ag_o, ag_p, st_o, st_p, dq, dk_in, dv_in):
+    par, _ = place()
+    mask = causal_mask()
+    for side, (ag, st) in enumerate(((ag_o, st_o), (ag_p, st_p))):
+        parity = par if side == 0 else 1 - par
+        for j in range(GROUPS):
+            c = cols(2 * j + parity)
+            q, k, v = qg_o[0, :, c], kv_o[0, :, c], kv_o[1, :, c]
+            a = ag[:, j * HEAD : (j + 1) * HEAD]
+            dscores = jnp.where(mask, nt(a, v), 0.0).astype(BF)
+            scores = jnp.where(mask, nt(q, k), 0.0).astype(BF)
+            dq[:, c] = (att_scale * (nn(dscores, k) + nt(a, st[j]))).astype(BF)
+            dk_in[:, c] = tn(dscores, q)
+            dv_in[:, c] = tn(scores, a)
+
+
+def carried_kernel(qdsel, qd_x, qd_y, car_o, car_r):
+    par, chip = place()
+    later = par.astype(F32)
+    x_earlier = (1 - lax.rem(chip, 2)).astype(F32)
+    for j in range(GROUPS):
+        total = qd_x[j].astype(F32) * x_earlier + qd_y[j].astype(F32)
+        sel = qdsel[j]
+        car_o[j] = (total + (1.0 - later) * sel).astype(BF)
+        car_r[j] = (total + later * sel).astype(BF)
+
+
+def finish_kernel(att_scale, kv_o, car_o, car_p, dk_in, dv_in, dk, dv):
+    par, _ = place()
+    for side, car in enumerate((car_o, car_p)):
+        parity = par if side == 0 else 1 - par
+        for j in range(GROUPS):
+            c = cols(2 * j + parity)
+            carried = car[j]
+            dk[:, c] = (att_scale * (dk_in[:, c] + nn(kv_o[1, :, c], carried))).astype(BF)
+            dv[:, c] = (att_scale * (dv_in[:, c] + nt(kv_o[0, :, c], carried))).astype(BF)
+
+
+def per_device(n_ctx, n_dp, queries, key_vecs, value_vecs, out_grad, out_weight):
+    tok_count, width = queries.shape[1:]
+    att_scale = 1.0 / math.sqrt(HEAD * tok_count * n_ctx)
+    inv_root = 1.0 / math.sqrt(n_dp * tok_count * n_ctx)
+
+    def along(bit, keep=lambda i: True):
+        return [(i, i ^ bit) for i in range(n_ctx) if keep(i)]
+
+    def core(x):
+        return lax.ppermute(x, "ctx", along(1))
+
+    def over_x(x):
+        return lax.ppermute(x, "ctx", along(2))
+
+    def over_y(x):
+        return lax.ppermute(x, "ctx", along(4))
+
+    def along_dp(x, m):
+        return lax.ppermute(x, "dp", [(i, i ^ m) for i in range(n_dp)])
+
+    state = (GROUPS, HEAD, HEAD)
+    half = width // 2
+    rows = HEAD // n_dp
+    kv_o = jnp.concatenate([key_vecs, value_vecs])
+    qg_o = jnp.concatenate([queries, out_grad])
+    kv_r = core(kv_o)
+    w_parts = [along_dp(out_weight, 1)]
+    w_again, kvsel, kv_own, kv_sent = local_call(
+        kv_kernel,
+        [((rows, width), BF), (state, F32), (state, F32), (state, BF)],
+        kv_o, kv_r, out_weight,
+    )
+    kv_x = over_x(kv_sent)
+    w_parts += [along_dp(w_again, m) for m in range(2, n_dp)]
+    qg_r = core(qg_o)
+    (w_two,) = local_call(
+        functools.partial(order_kernel, n_dp, 0), [((HEAD, width), BF)], w_again, w_parts[0],
+        micros=10,
+    )
+    (intra,) = local_call(
+        intra_kernel, [((2, BLOCK, half), F32)], qg_o, kv_o, qg_r, kv_r, after=(w_two,)
+    )
+    (kv_total,) = local_call(total_kernel, [(state, BF)], kv_own, kv_x, after=(intra,))
+    kv_y = lax.ppermute(kv_total, "ctx", along(4, lambda i: i < i ^ 4))
+    (w_0,) = local_call(
+        functools.partial(order_kernel, n_dp, 2),
+        [((HEAD, width), BF)], w_two, *w_parts[1:], after=(kv_total,),
+    )
+    w_x, w_y = over_x(w_0), over_y(w_0)
+    w_d0, w_d1 = over_y(w_x[: HEAD // 2]), over_x(w_y[HEAD // 2 :])
+    to_x, to_y, keep, forward, state_o, state_r = local_call(
+        functools.partial(attend_kernel, att_scale, inv_root),
+        [
+            ((2, HEAD, half), BF),
+            ((2, HEAD, half), BF),
+            ((HEAD, width), F32),
+            ((2, HEAD, half), F32),
+            (state, BF),
+            (state, BF),
+        ],
+        qg_o, qg_r, intra, kvsel, kv_x, kv_y,
+        after=(w_0,),
+    )
+    from_x, from_y = over_x(to_x), over_y(to_y)
+    state_p = core(state_r)
+    (pass_y,) = local_call(
+        functools.partial(forward_kernel, 0), [((HEAD, half), BF)], forward, from_x
+    )
+    (pass_x,) = local_call(
+        functools.partial(forward_kernel, 1), [((HEAD, half), BF)], forward, from_y,
+        after=(pass_y,),
+    )
+    last_y, last_x = over_y(pass_y), over_x(pass_x)
+    ag_o, ag_r, qdsel, qd_own, qd_sent = local_call(
+        att_grad_kernel,
+        [((BLOCK, half), BF), ((BLOCK, half), BF), (state, F32), (state, F32), (state, BF)],
+        qg_o, qg_r, w_0, w_x, w_y, w_d0, w_d1,
+        after=(pass_y, pass_x),
+    )
+    qd_x = over_x(qd_sent)
+    ag_p = core(ag_r)
+    own, *send = local_call(
+        functools.partial(fold_kernel, n_dp),
+        [((rows, width), F32)] + [((rows, width), BF)] * (n_dp - 1),
+        keep, from_x, from_y, last_y, last_x,
+        after=(qd_sent,),
+    )
+    got = [along_dp(send[m - 1], m) for m in range(1, n_dp)]
+    (qd_total,) = local_call(total_kernel, [(state, BF)], qd_own, qd_x, after=(send[0],))
+    qd_y = lax.ppermute(qd_total, "ctx", along(4, lambda i: i > i ^ 4))
+    dq, dk_in, dv_in = local_call(
+        functools.partial(block_kernel, att_scale),
+        [((BLOCK, width), BF), ((BLOCK, width), F32), ((BLOCK, width), F32)],
+        qg_o, kv_o, ag_o, ag_p, state_o, state_p,
+        after=(qd_total,),
+    )
+    weight_grad, summed = local_call(
+        sum_kernel, [((rows, width), F32), ((8, HEAD), F32)], own, *got, after=(dk_in,)
+    )
+    car_o, car_r = local_call(
+        carried_kernel, [(state, BF), (state, BF)], qdsel, qd_x, qd_y, after=(summed,)
+    )
+    car_p = core(car_r)
+    dk, dv = local_call(
+        functools.partial(finish_kernel, att_scale),
+        [((BLOCK, width), BF), ((BLOCK, width), BF)],
+        kv_o, car_o, car_p, dk_in, dv_in,
+    )
+    return dq[None], dk[None], dv[None], weight_grad
+
+
+def general_per_device(queries, key_vecs, value_vecs, out_grad, out_weight):
     qry_rows = queries[0]
     tok_count = qry_rows.shape[0]
     width = qry_rows.shape[1]
@@ -105,8 +426,17 @@
         P("dp", "ctx", None),
         P(("ctx", "dp"), None),
     )
+    n_ctx, n_dp = mesh.shape["ctx"], mesh.shape["dp"]
+
+    def chosen(queries, key_vecs, value_vecs, out_grad, out_weight):
+        local = (queries, key_vecs, value_vecs, out_grad, out_weight)
+        one_head = out_weight.shape[0] * n_dp == HEAD and n_ctx == 2 * GROUPS
+        if one_head and n_dp in (2, 4, 8) and queries.shape[:2] == (1, BLOCK):
+            return per_device(n_ctx, n_dp, *local)
+        return general_per_device(*local)
+
     return jax.shard_map(
-        per_device,
+        chosen,
         mesh=mesh,
         in_specs=placed,
         out_specs=(

time: 228 us -> 59.8 us (0.26)
  waiting for transfers between devices: 159 us -> 16.9 us
  matrix products: 21.6 us -> 0 us
  between operations: 14.2 us -> 0.81 us
  starting transfers between devices: 17 us -> 28.7 us
  Pallas kernels: 0 us -> 11.2 us
  local copies, waits for them, and re-layouts: 9.72 us -> 1.92 us
  other arithmetic: 6.19 us -> 0 us
    reduce_scatter x1 -> x0, waiting for transfers between devices: 104 us -> none  [per_device(): lax.psum_scatter(lax.dot_general(attended, flat_grad, (((0,), (0,)), ((),...]
    all_to_all x4 -> x0, waiting for transfers between devices: 29.6 us -> none  [the longest x1 10 us: per_device(): lax.all_to_all(local_kv.reshape(n_ctx, rows_each, HEAD), 'ctx', split_axi...]
    ppermute x0 -> x23, starting transfers between devices: none -> 28.7 us  [the longest x6 8.84 us: along_dp(): return lax.ppermute(x, 'dp', [(i, i ^ m) for i in range(n_dp)])]
    all_gather x1 -> x0, waiting for transfers between devices: 24 us -> none  [per_device(): lax.all_gather(out_weight, ('ctx', 'dp'), axis=0, tiled=True)]
    dot_general x14 -> x0, matrix products: 21.6 us -> none  [the longest x12 16.6 us: ein(): return jnp.einsum(form, left, right, preferred_element_type=jnp.float32)]
    all_to_all x4 -> x0, starting transfers between devices: 17 us -> none  [the longest x1 5.18 us: per_device(): lax.all_to_all(local_kv.reshape(n_ctx, rows_each, HEAD), 'ctx', split_axi...]
    ppermute x0 -> x23, waiting for transfers between devices: none -> 16.9 us  [the longest x6 8.62 us: over_x(): return lax.ppermute(x, 'ctx', along(2))]
    pallas_call x0 -> x15, Pallas kernels: none -> 11.2 us  [local_call(): pl.pallas_call(body, out_shape=[jax.ShapeDtypeStruct(s, d) for s, d in ou...]
  transfers between devices with their start and end apart: 6 -> 23, of which waited for: 6 -> 11; matrix products, arithmetic and copies ran while one was open for 16% -> 0% of each run, Pallas kernels for 0% -> 12%
where the time goes in v2:
time: 59.8 us; the launch traced here: 59.5 us
  starting transfers between devices  28.7 us (48%)
  waiting for transfers between devices  16.9 us (28%)
  Pallas kernels  11.2 us (19%)
  local copies, waits for them, and re-layouts  1.92 us (3%)
  between operations  0.81 us (1%)
    pallas_call x15, Pallas kernels, local_call(): pl.pallas_call(body, out_shape=[jax.ShapeDtypeStruct(s, d) for s, d in ou...  11.2 us
    ppermute x6, starting transfers between devices, along_dp(): return lax.ppermute(x, 'dp', [(i, i ^ m) for i in range(n_dp)])  8.84 us
    ppermute x6, starting transfers between devices, over_x(): return lax.ppermute(x, 'ctx', along(2))  8.64 us
    ppermute x6, waiting for transfers between devices, over_x(): return lax.ppermute(x, 'ctx', along(2))  8.62 us
    ppermute x4, starting transfers between devices, over_y(): return lax.ppermute(x, 'ctx', along(4))  5.29 us
    ppermute x1, starting transfers between devices, per_device(): kv_y = lax.ppermute(kv_total, 'ctx', along(4, lambda i: i < i ^ 4))  3.43 us
    ppermute x6, waiting for transfers between devices, along_dp(): return lax.ppermute(x, 'dp', [(i, i ^ m) for i in range(n_dp)])  3.09 us
    ppermute x4, waiting for transfers between devices, over_y(): return lax.ppermute(x, 'ctx', along(4))  2.74 us
  transfers between devices with their start and end apart: 23, of which 11 were waited for; matrix products, arithmetic and copies ran while one was open for 0% of the time, Pallas kernels for 12%

profile of v2, /device:TPU:0, one launch (start us, length us, event | category | flops | bytes accessed | tf_op | source)
XLA Modules:
  0.0 59.5 jit_solution(15152593794663476135)
XLA Ops:
  0.6 0.0 copy-start.1
  0.6 1.1 %constant_dynamic-update-slice_fusion.3 = bf16[2,256,1024]{2,1,0:T(8,128)(2,1)S(1)} fusion(bf16[1,256,1024]{2,1,0:T(8,128)(2,1)} %param.6), kind=kLoop, calls=%fused_computation.3 | loop fusion | bytes 1048576
  1.8 0.1 copy-done.1
  1.8 0.0 copy-start.2
  1.9 0.0 copy-start.3
  1.9 0.5 collective-permute-start.1
  2.4 0.5 copy-done.2
  2.9 0.1 copy-done.3
  3.0 0.0 copy-start
  3.1 0.5 collective-permute-start
  3.6 1.1 %collective-permute-done.1.refs_1_.refs_3_ = bf16[2,256,1024]{2,1,0:T(8,128)(2,1)S(1)} collective-permute-done((bf16[2,256,1024]{2,1,0:T(8,128)(2,1)S(1)}, bf16[2,256,1024]{2,1,0:T(8,128)(2,1)S(1)}, u32[]{:S(2)}, u32[]{:S(2)}) %collective-permute-start.1) | collective-permute-done | bytes 1048608 | tf_op jit(solution)/shard_map/ppermute | solution.py:235
  4.7 0.0 copy-done
  4.7 0.5 shard_map.84
  5.2 2.9 %collective-permute-start.5 = (bf16[4,128,128]{2,1,0:T(8,128)(2,1)S(1)}, bf16[4,128,128]{2,1,0:T(8,128)(2,1)S(1)}, u32[]{:S(2)}, u32[]{:S(2)}) collective-permute-start(bf16[4,128,128]{2,1,0:T(8,128)(2,1)S(1)} %get-tuple-element.34), channel_id=1, source_target_pairs={{0,8},{4,12},{8,0},{12,4},{16,24},{20,28},{24,16},{28,20},{1,9},{5... | collective-permute-start | bytes 393224 | tf_op jit(solution)/shard_map/ppermute | solution.py:238
  8.1 1.6 %collective-permute-start.2 = (bf16[32,1024]{1,0:T(8,128)(2,1)S(1)}, bf16[32,1024]{1,0:T(8,128)(2,1)S(1)}, u32[]{:S(2)}, u32[]{:S(2)}) collective-permute-start(bf16[32,1024]{1,0:T(8,128)(2,1)S(1)} %copy-done), channel_id=1, source_target_pairs={{0,1},{1,0},{2,3},{3,2},{4,5},{5,4},{6,7},{7,6},{8,9},{9,8},{10,11... | collective-permute-start | bytes 196616 | tf_op jit(solution)/shard_map/ppermute | solution.py:244
  9.7 2.6 %collective-permute-start.3 = (bf16[32,1024]{1,0:T(8,128)(2,1)S(1)}, bf16[32,1024]{1,0:T(8,128)(2,1)S(1)}, u32[]{:S(2)}, u32[]{:S(2)}) collective-permute-start(bf16[32,1024]{1,0:T(8,128)(2,1)S(1)} %get-tuple-element.32.refs_0_), channel_id=1, source_target_pairs={{0,2},{1,3},{2,0},{3,1},{4,6},{5,7},{6,4},{7,5},{8,10},{9,11},{10,... | collective-permute-start | bytes 196616 | tf_op jit(solution)/shard_map/ppermute | solution.py:244
  12.3 0.2 collective-permute-start.4
  12.5 0.0 collective-permute-done.2.refs_1_
  12.5 0.0 collective-permute-done.refs_2_.refs_1_
  12.5 0.9 %shard_map.86.refs_2_ = f32[2,256,512]{2,1,0:T(8,128)S(1)} custom-call(bf16[2,256,1024]{2,1,0:T(8,128)(2,1)S(1)} %constant_dynamic-update-slice_fusion.refs_0_, bf16[2,256,1024]{2,1,0:T(8,128)(2,1)S(1)} %constant_dynamic-update-slice_fusion.2.refs_0_.refs_1_, bf16[2,256,1024]{2,1,0:T(8,128)(2,1)S(1)} %collective-permute-done.refs_2_.refs_1_, ...), custom_call_target="tpu_custom_call" | custom-call | tf_op jit(solution)/shard_map/pallas_call | solution.py:58
  13.5 0.0 collective-permute-done.5.refs_1_.refs_4_
  13.5 3.4 %collective-permute-start.10 = (bf16[4,128,128]{2,1,0:T(8,128)(2,1)S(1)}, bf16[4,128,128]{2,1,0:T(8,128)(2,1)S(1)}, u32[]{:S(2)}, u32[]{:S(2)}) collective-permute-start(bf16[4,128,128]{2,1,0:T(8,128)(2,1)S(1)} %shard_map.87.refs_3_), channel_id=1, source_target_pairs={{0,16},{4,20},{8,24},{12,28},{1,17},{5,21},{9,25},{13,29},{2,18},{... | collective-permute-start | bytes 393224 | tf_op jit(solution)/shard_map/ppermute | solution.py:269
  17.0 0.0 collective-permute-done.3.refs_1_
  17.0 1.4 %collective-permute-done.4.refs_2_ = bf16[32,1024]{1,0:T(8,128)(2,1)S(1)} collective-permute-done((bf16[32,1024]{1,0:T(8,128)(2,1)S(1)}, bf16[32,1024]{1,0:T(8,128)(2,1)S(1)}, u32[]{:S(2)}, u32[]{:S(2)}) %collective-permute-start.4) | collective-permute-done | bytes 65568 | tf_op jit(solution)/shard_map/ppermute | solution.py:244
  18.4 0.6 %collective-permute-start.6 = (bf16[128,1024]{1,0:T(8,128)(2,1)S(1)}, bf16[128,1024]{1,0:T(8,128)(2,1)S(1)}, u32[]{:S(2)}, u32[]{:S(2)}) collective-permute-start(bf16[128,1024]{1,0:T(8,128)(2,1)S(1)} %shard_map.88.refs_6_.refs_2_), channel_id=1, source_target_pairs={{0,8},{4,12},{8,0},{12,4},{16,24},{20,28},{24,16},{28,20},{1,9},{5... | collective-permute-start | bytes 786440 | tf_op jit(solution)/shard_map/ppermute | solution.py:238
  19.0 1.5 %collective-permute-start.7 = (bf16[128,1024]{1,0:T(8,128)(2,1)S(1)}, bf16[128,1024]{1,0:T(8,128)(2,1)S(1)}, u32[]{:S(2)}, u32[]{:S(2)}) collective-permute-start(bf16[128,1024]{1,0:T(8,128)(2,1)S(1)} %shard_map.88.refs_6_.refs_2_), channel_id=1, source_target_pairs={{0,16},{4,20},{8,24},{12,28},{16,0},{20,4},{24,8},{28,12},{1,17},{... | collective-permute-start | bytes 786440 | tf_op jit(solution)/shard_map/ppermute | solution.py:241
  20.5 0.0 collective-permute-done.10.refs_5_
  20.5 1.6 %shard_map.89 = (bf16[2,128,512]{2,1,0:T(8,128)(2,1)S(1)}, bf16[2,128,512]{2,1,0:T(8,128)(2,1)S(1)}, f32[128,1024]{1,0:T(8,128)S(1)}, f32[2,128,512]{2,1,0:T(8,1...) custom-call(bf16[2,256,1024]{2,1,0:T(8,128)(2,1)S(1)} %constant_dynamic-update-slice_fusion.refs_0_, ...), custom_call_target="tpu_custom_call" | custom-call | tf_op jit(solution)/shard_map/pallas_call | solution.py:58
  22.1 1.6 %collective-permute-start.11 = (bf16[2,128,512]{2,1,0:T(8,128)(2,1)S(1)}, bf16[2,128,512]{2,1,0:T(8,128)(2,1)S(1)}, u32[]{:S(2)}, u32[]{:S(2)}) collective-permute-start(bf16[2,128,512]{2,1,0:T(8,128)(2,1)S(1)} %get-tuple-element.37), channel_id=1, source_target_pairs={{0,8},{4,12},{8,0},{12,4},{16,24},{20,28},{24,16},{28,20},{1,9},{5... | collective-permute-start | bytes 786440 | tf_op jit(solution)/shard_map/ppermute | solution.py:238
  23.7 0.9 %collective-permute-start.12 = (bf16[2,128,512]{2,1,0:T(8,128)(2,1)S(1)}, bf16[2,128,512]{2,1,0:T(8,128)(2,1)S(1)}, u32[]{:S(2)}, u32[]{:S(2)}) collective-permute-start(bf16[2,128,512]{2,1,0:T(8,128)(2,1)S(1)} %get-tuple-element.38), channel_id=1, source_target_pairs={{0,16},{4,20},{8,24},{12,28},{16,0},{20,4},{24,8},{28,12},{1,17},{... | collective-permute-start | bytes 786440 | tf_op jit(solution)/shard_map/ppermute | solution.py:241
  24.6 2.8 %collective-permute-done.6.refs_3_ = bf16[128,1024]{1,0:T(8,128)(2,1)S(1)} collective-permute-done((bf16[128,1024]{1,0:T(8,128)(2,1)S(1)}, bf16[128,1024]{1,0:T(8,128)(2,1)S(1)}, u32[]{:S(2)}, u32[]{:S(2)}) %collective-permute-start.6) | collective-permute-done | bytes 262176 | tf_op jit(solution)/shard_map/ppermute | solution.py:238
  27.4 1.4 %collective-permute-start.8 = (bf16[64,1024]{1,0:T(8,128)(2,1)S(1)}, bf16[64,1024]{1,0:T(8,128)(2,1)S(1)}, u32[]{:S(2)}, u32[]{:S(2)}) collective-permute-start(bf16[64,1024]{1,0:T(8,128)(2,1)S(1)} %slice.8), channel_id=1, source_target_pairs={{0,16},{4,20},{8,24},{12,28},{16,0},{20,4},{24,8},{28,12},{1,17},{... | collective-permute-start | bytes 393224 | tf_op jit(solution)/shard_map/ppermute | solution.py:241
  28.7 0.0 collective-permute-done.7.refs_4_
  28.7 0.8 %collective-permute-start.9 = (bf16[64,1024]{1,0:T(8,128)(2,1)S(1)}, bf16[64,1024]{1,0:T(8,128)(2,1)S(1)}, u32[]{:S(2)}, u32[]{:S(2)}) collective-permute-start(bf16[64,1024]{1,0:T(8,128)(2,1)S(1)} %slice.9), channel_id=1, source_target_pairs={{0,8},{4,12},{8,0},{12,4},{16,24},{20,28},{24,16},{28,20},{1,9},{5... | collective-permute-start | bytes 393224 | tf_op jit(solution)/shard_map/ppermute | solution.py:238
  29.6 2.3 %collective-permute-done.11.refs_1_ = bf16[2,128,512]{2,1,0:T(8,128)(2,1)S(1)} collective-permute-done((bf16[2,128,512]{2,1,0:T(8,128)(2,1)S(1)}, bf16[2,128,512]{2,1,0:T(8,128)(2,1)S(1)}, u32[]{:S(2)}, u32[]{:S(2)}) %collective-permute-start.11) | collective-permute-done | bytes 262176 | tf_op jit(solution)/shard_map/ppermute | solution.py:238
  31.9 0.5 collective-permute-done.12.refs_1_.refs_2_
  32.4 1.4 %collective-permute-done.8.refs_5_ = bf16[64,1024]{1,0:T(8,128)(2,1)S(1)} collective-permute-done((bf16[64,1024]{1,0:T(8,128)(2,1)S(1)}, bf16[64,1024]{1,0:T(8,128)(2,1)S(1)}, u32[]{:S(2)}, u32[]{:S(2)}) %collective-permute-start.8) | collective-permute-done | bytes 131104 | tf_op jit(solution)/shard_map/ppermute | solution.py:241
  33.8 0.0 collective-permute-done.9.refs_6_
  33.8 2.4 %shard_map.92 = (bf16[256,512]{1,0:T(8,128)(2,1)S(1)}, bf16[256,512]{1,0:T(8,128)(2,1)S(1)}, f32[4,128,128]{2,1,0:T(8,128)S(1)}, f32[4,128,128]{2,1,0:T(8,128)S(1)}, bf16[4,128,128]{2,1,0:T(8,128)(2,1)S(1)}) custom-call(bf16[2,256,1024]{2,1,0:T(8,128)(2,1)S(1)} %constant_dynamic-update-slice_fusion.refs_0_, ...), custom_call_target="tpu_custom_call" | custom-call | tf_op jit(solution)/shard_map/pallas_call | solution.py:58
  36.2 0.1 collective-permute-start.13
  36.3 1.5 %collective-permute-start.17 = (bf16[128,512]{1,0:T(8,128)(2,1)S(1)}, bf16[128,512]{1,0:T(8,128)(2,1)S(1)}, u32[]{:S(2)}, u32[]{:S(2)}) collective-permute-start(bf16[128,512]{1,0:T(8,128)(2,1)S(1)} %shard_map.91.refs_8_), channel_id=1, source_target_pairs={{0,8},{4,12},{8,0},{12,4},{16,24},{20,28},{24,16},{28,20},{1,9},{5... | collective-permute-start | bytes 393224 | tf_op jit(solution)/shard_map/ppermute | solution.py:238
  37.8 1.5 %collective-permute-start.16 = (bf16[128,512]{1,0:T(8,128)(2,1)S(1)}, bf16[128,512]{1,0:T(8,128)(2,1)S(1)}, u32[]{:S(2)}, u32[]{:S(2)}) collective-permute-start(bf16[128,512]{1,0:T(8,128)(2,1)S(1)} %shard_map.90.refs_2_.refs_7_), channel_id=1, source_target_pairs={{0,16},{4,20},{8,24},{12,28},{16,0},{20,4},{24,8},{28,12},{1,17},{... | collective-permute-start | bytes 393224 | tf_op jit(solution)/shard_map/ppermute | solution.py:241
  39.3 1.2 %collective-permute-start.15 = (bf16[4,128,128]{2,1,0:T(8,128)(2,1)S(1)}, bf16[4,128,128]{2,1,0:T(8,128)(2,1)S(1)}, u32[]{:S(2)}, u32[]{:S(2)}) collective-permute-start(bf16[4,128,128]{2,1,0:T(8,128)(2,1)S(1)} %get-tuple-element.44.refs_5_), channel_id=1, source_target_pairs={{0,8},{4,12},{8,0},{12,4},{16,24},{20,28},{24,16},{28,20},{1,9},{5... | collective-permute-start | bytes 393224 | tf_op jit(solution)/shard_map/ppermute | solution.py:238
  40.5 0.0 collective-permute-start.14
  40.5 2.0 %collective-permute-done.17.refs_4_ = bf16[128,512]{1,0:T(8,128)(2,1)S(1)} collective-permute-done((bf16[128,512]{1,0:T(8,128)(2,1)S(1)}, bf16[128,512]{1,0:T(8,128)(2,1)S(1)}, u32[]{:S(2)}, u32[]{:S(2)}) %collective-permute-start.17) | collective-permute-done | bytes 131104 | tf_op jit(solution)/shard_map/ppermute | solution.py:238
  42.5 0.9 %collective-permute-done.16.refs_3_ = bf16[128,512]{1,0:T(8,128)(2,1)S(1)} collective-permute-done((bf16[128,512]{1,0:T(8,128)(2,1)S(1)}, bf16[128,512]{1,0:T(8,128)(2,1)S(1)}, u32[]{:S(2)}, u32[]{:S(2)}) %collective-permute-start.16) | collective-permute-done | bytes 131104 | tf_op jit(solution)/shard_map/ppermute | solution.py:241
  43.4 0.1 shard_map.93
  43.5 1.5 %collective-permute-done.15.refs_1_ = bf16[4,128,128]{2,1,0:T(8,128)(2,1)S(1)} collective-permute-done((bf16[4,128,128]{2,1,0:T(8,128)(2,1)S(1)}, bf16[4,128,128]{2,1,0:T(8,128)(2,1)S(1)}, u32[]{:S(2)}, u32[]{:S(2)}) %collective-permute-start.15) | collective-permute-done | bytes 131104 | tf_op jit(solution)/shard_map/ppermute | solution.py:238
  45.0 1.3 %collective-permute-start.18 = (bf16[4,128,128]{2,1,0:T(8,128)(2,1)S(1)}, bf16[4,128,128]{2,1,0:T(8,128)(2,1)S(1)}, u32[]{:S(2)}, u32[]{:S(2)}) collective-permute-start(bf16[4,128,128]{2,1,0:T(8,128)(2,1)S(1)} %shard_map.94.refs_6_), channel_id=1, source_target_pairs={{16,0},{20,4},{24,8},{28,12},{17,1},{21,5},{25,9},{29,13},{18,2},{... | collective-permute-start | bytes 393224 | tf_op jit(solution)/shard_map/ppermute | solution.py:315
  46.3 1.0 %collective-permute-start.19 = (bf16[32,1024]{1,0:T(8,128)(2,1)S(1)}, bf16[32,1024]{1,0:T(8,128)(2,1)S(1)}, u32[]{:S(2)}, u32[]{:S(2)}) collective-permute-start(bf16[32,1024]{1,0:T(8,128)(2,1)S(1)} %get-tuple-element.46.refs_2_), channel_id=1, source_target_pairs={{0,1},{1,0},{2,3},{3,2},{4,5},{5,4},{6,7},{7,6},{8,9},{9,8},{10,11... | collective-permute-start | bytes 196616 | tf_op jit(solution)/shard_map/ppermute | solution.py:244
  47.3 2.4 %collective-permute-start.20 = (bf16[32,1024]{1,0:T(8,128)(2,1)S(1)}, bf16[32,1024]{1,0:T(8,128)(2,1)S(1)}, u32[]{:S(2)}, u32[]{:S(2)}) collective-permute-start(bf16[32,1024]{1,0:T(8,128)(2,1)S(1)} %get-tuple-element.50), channel_id=1, source_target_pairs={{0,2},{1,3},{2,0},{3,1},{4,6},{5,7},{6,4},{7,5},{8,10},{9,11},{10,... | collective-permute-start | bytes 196616 | tf_op jit(solution)/shard_map/ppermute | solution.py:244
  49.7 0.0 collective-permute-done.14.refs_5_
  49.7 1.1 %collective-permute-start.21 = (bf16[32,1024]{1,0:T(8,128)(2,1)S(1)}, bf16[32,1024]{1,0:T(8,128)(2,1)S(1)}, u32[]{:S(2)}, u32[]{:S(2)}) collective-permute-start(bf16[32,1024]{1,0:T(8,128)(2,1)S(1)} %get-tuple-element.51), channel_id=1, source_target_pairs={{0,3},{1,2},{2,1},{3,0},{4,7},{5,6},{6,5},{7,4},{8,11},{9,10},{10,... | collective-permute-start | bytes 196616 | tf_op jit(solution)/shard_map/ppermute | solution.py:244
  50.8 0.0 collective-permute-done.13.refs_3_
  50.8 3.3 %shard_map.95 = (bf16[256,1024]{1,0:T(8,128)(2,1)}, f32[256,1024]{1,0:T(8,128)S(1)}, f32[256,1024]{1,0:T(8,128)S(1)}) custom-call(bf16[2,256,1024]{2,1,0:T(8,128)(2,1)S(1)} %constant_dynamic-update-slice_fusion.refs_0_, bf16[2,256,1024]{2,1,0:T(8,128)(2,1)S(1)} %constant_dynamic-update-slice_fusion.2.refs_0_.refs_1_, ...), custom_call_target="tpu_custom_call" | custom-call | tf_op jit(solution)/shard_map/pallas_call | solution.py:58
  54.1 0.0 collective-permute-done.19.refs_1_
  54.1 0.0 collective-permute-done.20.refs_2_
  54.1 1.7 %collective-permute-done.21.refs_3_ = bf16[32,1024]{1,0:T(8,128)(2,1)S(1)} collective-permute-done((bf16[32,1024]{1,0:T(8,128)(2,1)S(1)}, bf16[32,1024]{1,0:T(8,128)(2,1)S(1)}, u32[]{:S(2)}, u32[]{:S(2)}) %collective-permute-start.21) | collective-permute-done | bytes 65568 | tf_op jit(solution)/shard_map/ppermute | solution.py:244
  55.8 0.7 %shard_map.96 = (f32[32,1024]{1,0:T(8,128)}, f32[8,128]{1,0:T(8,128)S(1)}) custom-call(f32[32,1024]{1,0:T(8,128)S(1)} %get-tuple-element.49.refs_0_, bf16[32,1024]{1,0:T(8,128)(2,1)S(1)} %collective-permute-done.19.refs_1_, bf16[32,1024]{1,0:T(8,128)(2,1)S(1)} %collective-permute-done.20.refs_2_, bf16[32,1024]{1,0:T(8,128)(2,1)S(1)} %collective-permute-done.21.refs_3_, ...), custom_call_target="tpu_custom_call" | custom-call | tf_op jit(solution)/shard_map/pallas_call | solution.py:58
  56.5 0.0 collective-permute-done.18.refs_2_
  56.5 0.1 shard_map.97
  56.6 0.1 collective-permute-start.22
  56.6 1.3 %collective-permute-done.22.refs_2_ = bf16[4,128,128]{2,1,0:T(8,128)(2,1)S(1)} collective-permute-done((bf16[4,128,128]{2,1,0:T(8,128)(2,1)S(1)}, bf16[4,128,128]{2,1,0:T(8,128)(2,1)S(1)}, u32[]{:S(2)}, u32[]{:S(2)}) %collective-permute-start.22) | collective-permute-done | bytes 131104 | tf_op jit(solution)/shard_map/ppermute | solution.py:235
  58.0 1.6 %shard_map.98 = (bf16[256,1024]{1,0:T(8,128)(2,1)}, bf16[256,1024]{1,0:T(8,128)(2,1)}) custom-call(bf16[2,256,1024]{2,1,0:T(8,128)(2,1)S(1)} %constant_dynamic-update-slice_fusion.2.refs_0_.refs_1_, bf16[4,128,128]{2,1,0:T(8,128)(2,1)S(1)} %get-tuple-element.54.refs_1_, bf16[4,128,128]{2,1,0:T(8,128)(2,1)S(1)} %collective-permute-done.22.refs_2_, ...), custom_call_target="tpu_custom_call" | custom-call | tf_op jit(solution)/shard_map/pallas_call | solution.py:58
  (11 shorter events, 0.3 us)
Async XLA Ops:
  0.6 1.2 %copy-start.1 = (bf16[1,256,1024]{2,1,0:T(8,128)(2,1)S(1)}, bf16[1,256,1024]{2,1,0:T(8,128)(2,1)}, u32[]{:S(2)}) copy-start(bf16[1,256,1024]{2,1,0:T(8,128)(2,1)} %param.7) | copy-start | bytes 1572868
  1.8 1.0 %copy-start.2 = (bf16[1,256,1024]{2,1,0:T(8,128)(2,1)S(1)}, bf16[1,256,1024]{2,1,0:T(8,128)(2,1)}, u32[]{:S(2)}) copy-start(bf16[1,256,1024]{2,1,0:T(8,128)(2,1)} %param.5) | copy-start | bytes 1572868
  1.9 1.2 %copy-start.3 = (bf16[1,256,1024]{2,1,0:T(8,128)(2,1)S(1)}, bf16[1,256,1024]{2,1,0:T(8,128)(2,1)}, u32[]{:S(2)}) copy-start(bf16[1,256,1024]{2,1,0:T(8,128)(2,1)} %param.8) | copy-start | bytes 1572868
  1.9 2.8 %collective-permute-start.1 = (bf16[2,256,1024]{2,1,0:T(8,128)(2,1)S(1)}, bf16[2,256,1024]{2,1,0:T(8,128)(2,1)S(1)}, u32[]{:S(2)}, u32[]{:S(2)}) collective-permute-start(bf16[2,256,1024]{2,1,0:T(8,128)(2,1)S(1)} %constant_dynamic-update-slice_fusion.2.refs_0_.refs_1_), channel_id=1, source_target_pairs={{0,4},{4,0},{8,12},{12,8},{16,20},{20,16},{24,28},{28,24},{1,5},{5... | collective-permute-start | bytes 3145736 | tf_op jit(solution)/shard_map/ppermute | solution.py:235
  3.0 1.6 %copy-start = (bf16[32,1024]{1,0:T(8,128)(2,1)S(1)}, bf16[32,1024]{1,0:T(8,128)(2,1)}, u32[]{:S(2)}) copy-start(bf16[32,1024]{1,0:T(8,128)(2,1)} %refs_2_.1) | copy-start | bytes 196612
  3.1 9.4 %collective-permute-start = (bf16[2,256,1024]{2,1,0:T(8,128)(2,1)S(1)}, bf16[2,256,1024]{2,1,0:T(8,128)(2,1)S(1)}, u32[]{:S(2)}, u32[]{:S(2)}) collective-permute-start(bf16[2,256,1024]{2,1,0:T(8,128)(2,1)S(1)} %constant_dynamic-update-slice_fusion.refs_0_), channel_id=1, source_target_pairs={{0,4},{4,0},{8,12},{12,8},{16,20},{20,16},{24,28},{28,24},{1,5},{5... | collective-permute-start | bytes 3145736 | tf_op jit(solution)/shard_map/ppermute | solution.py:235
  5.2 8.3 %collective-permute-start.5 = (bf16[4,128,128]{2,1,0:T(8,128)(2,1)S(1)}, bf16[4,128,128]{2,1,0:T(8,128)(2,1)S(1)}, u32[]{:S(2)}, u32[]{:S(2)}) collective-permute-start(bf16[4,128,128]{2,1,0:T(8,128)(2,1)S(1)} %get-tuple-element.34), channel_id=1, source_target_pairs={{0,8},{4,12},{8,0},{12,4},{16,24},{20,28},{24,16},{28,20},{1,9},{5... | collective-permute-start | bytes 393224 | tf_op jit(solution)/shard_map/ppermute | solution.py:238
  8.1 4.4 %collective-permute-start.2 = (bf16[32,1024]{1,0:T(8,128)(2,1)S(1)}, bf16[32,1024]{1,0:T(8,128)(2,1)S(1)}, u32[]{:S(2)}, u32[]{:S(2)}) collective-permute-start(bf16[32,1024]{1,0:T(8,128)(2,1)S(1)} %copy-done), channel_id=1, source_target_pairs={{0,1},{1,0},{2,3},{3,2},{4,5},{5,4},{6,7},{7,6},{8,9},{9,8},{10,11... | collective-permute-start | bytes 196616 | tf_op jit(solution)/shard_map/ppermute | solution.py:244
  9.7 7.3 %collective-permute-start.3 = (bf16[32,1024]{1,0:T(8,128)(2,1)S(1)}, bf16[32,1024]{1,0:T(8,128)(2,1)S(1)}, u32[]{:S(2)}, u32[]{:S(2)}) collective-permute-start(bf16[32,1024]{1,0:T(8,128)(2,1)S(1)} %get-tuple-element.32.refs_0_), channel_id=1, source_target_pairs={{0,2},{1,3},{2,0},{3,1},{4,6},{5,7},{6,4},{7,5},{8,10},{9,11},{10,... | collective-permute-start | bytes 196616 | tf_op jit(solution)/shard_map/ppermute | solution.py:244
  12.3 6.1 %collective-permute-start.4 = (bf16[32,1024]{1,0:T(8,128)(2,1)S(1)}, bf16[32,1024]{1,0:T(8,128)(2,1)S(1)}, u32[]{:S(2)}, u32[]{:S(2)}) collective-permute-start(bf16[32,1024]{1,0:T(8,128)(2,1)S(1)} %get-tuple-element.32.refs_0_), channel_id=1, source_target_pairs={{0,3},{1,2},{2,1},{3,0},{4,7},{5,6},{6,5},{7,4},{8,11},{9,10},{10,... | collective-permute-start | bytes 196616 | tf_op jit(solution)/shard_map/ppermute | solution.py:244
  13.5 7.0 %collective-permute-start.10 = (bf16[4,128,128]{2,1,0:T(8,128)(2,1)S(1)}, bf16[4,128,128]{2,1,0:T(8,128)(2,1)S(1)}, u32[]{:S(2)}, u32[]{:S(2)}) collective-permute-start(bf16[4,128,128]{2,1,0:T(8,128)(2,1)S(1)} %shard_map.87.refs_3_), channel_id=1, source_target_pairs={{0,16},{4,20},{8,24},{12,28},{1,17},{5,21},{9,25},{13,29},{2,18},{... | collective-permute-start | bytes 393224 | tf_op jit(solution)/shard_map/ppermute | solution.py:269
  18.4 9.0 %collective-permute-start.6 = (bf16[128,1024]{1,0:T(8,128)(2,1)S(1)}, bf16[128,1024]{1,0:T(8,128)(2,1)S(1)}, u32[]{:S(2)}, u32[]{:S(2)}) collective-permute-start(bf16[128,1024]{1,0:T(8,128)(2,1)S(1)} %shard_map.88.refs_6_.refs_2_), channel_id=1, source_target_pairs={{0,8},{4,12},{8,0},{12,4},{16,24},{20,28},{24,16},{28,20},{1,9},{5... | collective-permute-start | bytes 786440 | tf_op jit(solution)/shard_map/ppermute | solution.py:238
  19.0 9.7 %collective-permute-start.7 = (bf16[128,1024]{1,0:T(8,128)(2,1)S(1)}, bf16[128,1024]{1,0:T(8,128)(2,1)S(1)}, u32[]{:S(2)}, u32[]{:S(2)}) collective-permute-start(bf16[128,1024]{1,0:T(8,128)(2,1)S(1)} %shard_map.88.refs_6_.refs_2_), channel_id=1, source_target_pairs={{0,16},{4,20},{8,24},{12,28},{16,0},{20,4},{24,8},{28,12},{1,17},{... | collective-permute-start | bytes 786440 | tf_op jit(solution)/shard_map/ppermute | solution.py:241
  22.1 9.8 %collective-permute-start.11 = (bf16[2,128,512]{2,1,0:T(8,128)(2,1)S(1)}, bf16[2,128,512]{2,1,0:T(8,128)(2,1)S(1)}, u32[]{:S(2)}, u32[]{:S(2)}) collective-permute-start(bf16[2,128,512]{2,1,0:T(8,128)(2,1)S(1)} %get-tuple-element.37), channel_id=1, source_target_pairs={{0,8},{4,12},{8,0},{12,4},{16,24},{20,28},{24,16},{28,20},{1,9},{5... | collective-permute-start | bytes 786440 | tf_op jit(solution)/shard_map/ppermute | solution.py:238
  23.7 8.7 %collective-permute-start.12 = (bf16[2,128,512]{2,1,0:T(8,128)(2,1)S(1)}, bf16[2,128,512]{2,1,0:T(8,128)(2,1)S(1)}, u32[]{:S(2)}, u32[]{:S(2)}) collective-permute-start(bf16[2,128,512]{2,1,0:T(8,128)(2,1)S(1)} %get-tuple-element.38), channel_id=1, source_target_pairs={{0,16},{4,20},{8,24},{12,28},{16,0},{20,4},{24,8},{28,12},{1,17},{... | collective-permute-start | bytes 786440 | tf_op jit(solution)/shard_map/ppermute | solution.py:241
  27.4 6.4 %collective-permute-start.8 = (bf16[64,1024]{1,0:T(8,128)(2,1)S(1)}, bf16[64,1024]{1,0:T(8,128)(2,1)S(1)}, u32[]{:S(2)}, u32[]{:S(2)}) collective-permute-start(bf16[64,1024]{1,0:T(8,128)(2,1)S(1)} %slice.8), channel_id=1, source_target_pairs={{0,16},{4,20},{8,24},{12,28},{16,0},{20,4},{24,8},{28,12},{1,17},{... | collective-permute-start | bytes 393224 | tf_op jit(solution)/shard_map/ppermute | solution.py:241
  28.7 5.1 %collective-permute-start.9 = (bf16[64,1024]{1,0:T(8,128)(2,1)S(1)}, bf16[64,1024]{1,0:T(8,128)(2,1)S(1)}, u32[]{:S(2)}, u32[]{:S(2)}) collective-permute-start(bf16[64,1024]{1,0:T(8,128)(2,1)S(1)} %slice.9), channel_id=1, source_target_pairs={{0,8},{4,12},{8,0},{12,4},{16,24},{20,28},{24,16},{28,20},{1,9},{5... | collective-permute-start | bytes 393224 | tf_op jit(solution)/shard_map/ppermute | solution.py:238
  36.2 14.6 %collective-permute-start.13 = (bf16[256,512]{1,0:T(8,128)(2,1)S(1)}, bf16[256,512]{1,0:T(8,128)(2,1)S(1)}, u32[]{:S(2)}, u32[]{:S(2)}) collective-permute-start(bf16[256,512]{1,0:T(8,128)(2,1)S(1)} %get-tuple-element.40), channel_id=1, source_target_pairs={{0,4},{4,0},{8,12},{12,8},{16,20},{20,16},{24,28},{28,24},{1,5},{5... | collective-permute-start | bytes 786440 | tf_op jit(solution)/shard_map/ppermute | solution.py:235
  36.3 6.2 %collective-permute-start.17 = (bf16[128,512]{1,0:T(8,128)(2,1)S(1)}, bf16[128,512]{1,0:T(8,128)(2,1)S(1)}, u32[]{:S(2)}, u32[]{:S(2)}) collective-permute-start(bf16[128,512]{1,0:T(8,128)(2,1)S(1)} %shard_map.91.refs_8_), channel_id=1, source_target_pairs={{0,8},{4,12},{8,0},{12,4},{16,24},{20,28},{24,16},{28,20},{1,9},{5... | collective-permute-start | bytes 393224 | tf_op jit(solution)/shard_map/ppermute | solution.py:238
  37.8 5.6 %collective-permute-start.16 = (bf16[128,512]{1,0:T(8,128)(2,1)S(1)}, bf16[128,512]{1,0:T(8,128)(2,1)S(1)}, u32[]{:S(2)}, u32[]{:S(2)}) collective-permute-start(bf16[128,512]{1,0:T(8,128)(2,1)S(1)} %shard_map.90.refs_2_.refs_7_), channel_id=1, source_target_pairs={{0,16},{4,20},{8,24},{12,28},{16,0},{20,4},{24,8},{28,12},{1,17},{... | collective-permute-start | bytes 393224 | tf_op jit(solution)/shard_map/ppermute | solution.py:241
  39.3 5.7 %collective-permute-start.15 = (bf16[4,128,128]{2,1,0:T(8,128)(2,1)S(1)}, bf16[4,128,128]{2,1,0:T(8,128)(2,1)S(1)}, u32[]{:S(2)}, u32[]{:S(2)}) collective-permute-start(bf16[4,128,128]{2,1,0:T(8,128)(2,1)S(1)} %get-tuple-element.44.refs_5_), channel_id=1, source_target_pairs={{0,8},{4,12},{8,0},{12,4},{16,24},{20,28},{24,16},{28,20},{1,9},{5... | collective-permute-start | bytes 393224 | tf_op jit(solution)/shard_map/ppermute | solution.py:238
  40.5 9.2 %collective-permute-start.14 = (bf16[4,128,128]{2,1,0:T(8,128)(2,1)S(1)}, bf16[4,128,128]{2,1,0:T(8,128)(2,1)S(1)}, u32[]{:S(2)}, u32[]{:S(2)}) collective-permute-start(bf16[4,128,128]{2,1,0:T(8,128)(2,1)S(1)} %get-tuple-element.42), channel_id=1, source_target_pairs={{0,4},{4,0},{8,12},{12,8},{16,20},{20,16},{24,28},{28,24},{1,5},{5... | collective-permute-start | bytes 393224 | tf_op jit(solution)/shard_map/ppermute | solution.py:235
  45.0 11.4 %collective-permute-start.18 = (bf16[4,128,128]{2,1,0:T(8,128)(2,1)S(1)}, bf16[4,128,128]{2,1,0:T(8,128)(2,1)S(1)}, u32[]{:S(2)}, u32[]{:S(2)}) collective-permute-start(bf16[4,128,128]{2,1,0:T(8,128)(2,1)S(1)} %shard_map.94.refs_6_), channel_id=1, source_target_pairs={{16,0},{20,4},{24,8},{28,12},{17,1},{21,5},{25,9},{29,13},{18,2},{... | collective-permute-start | bytes 393224 | tf_op jit(solution)/shard_map/ppermute | solution.py:315
  46.3 7.8 %collective-permute-start.19 = (bf16[32,1024]{1,0:T(8,128)(2,1)S(1)}, bf16[32,1024]{1,0:T(8,128)(2,1)S(1)}, u32[]{:S(2)}, u32[]{:S(2)}) collective-permute-start(bf16[32,1024]{1,0:T(8,128)(2,1)S(1)} %get-tuple-element.46.refs_2_), channel_id=1, source_target_pairs={{0,1},{1,0},{2,3},{3,2},{4,5},{5,4},{6,7},{7,6},{8,9},{9,8},{10,11... | collective-permute-start | bytes 196616 | tf_op jit(solution)/shard_map/ppermute | solution.py:244
  47.3 6.8 %collective-permute-start.20 = (bf16[32,1024]{1,0:T(8,128)(2,1)S(1)}, bf16[32,1024]{1,0:T(8,128)(2,1)S(1)}, u32[]{:S(2)}, u32[]{:S(2)}) collective-permute-start(bf16[32,1024]{1,0:T(8,128)(2,1)S(1)} %get-tuple-element.50), channel_id=1, source_target_pairs={{0,2},{1,3},{2,0},{3,1},{4,6},{5,7},{6,4},{7,5},{8,10},{9,11},{10,... | collective-permute-start | bytes 196616 | tf_op jit(solution)/shard_map/ppermute | solution.py:244
  49.7 6.1 %collective-permute-start.21 = (bf16[32,1024]{1,0:T(8,128)(2,1)S(1)}, bf16[32,1024]{1,0:T(8,128)(2,1)S(1)}, u32[]{:S(2)}, u32[]{:S(2)}) collective-permute-start(bf16[32,1024]{1,0:T(8,128)(2,1)S(1)} %get-tuple-element.51), channel_id=1, source_target_pairs={{0,3},{1,2},{2,1},{3,0},{4,7},{5,6},{6,5},{7,4},{8,11},{9,10},{10,... | collective-permute-start | bytes 196616 | tf_op jit(solution)/shard_map/ppermute | solution.py:244
  56.6 1.4 %collective-permute-start.22 = (bf16[4,128,128]{2,1,0:T(8,128)(2,1)S(1)}, bf16[4,128,128]{2,1,0:T(8,128)(2,1)S(1)}, u32[]{:S(2)}, u32[]{:S(2)}) collective-permute-start(bf16[4,128,128]{2,1,0:T(8,128)(2,1)S(1)} %get-tuple-element.55), channel_id=1, source_target_pairs={{0,4},{4,0},{8,12},{12,8},{16,20},{20,16},{24,28},{28,24},{1,5},{5... | collective-permute-start | bytes 393224 | tf_op jit(solution)/shard_map/ppermute | solution.py:235

commit v3 on v2

--- a/solution.py
+++ b/solution.py
@@ -46,9 +46,8 @@
     return lax.rem(me, 2), lax.div(me, 2)
 
 
-def local_call(kernel, outs, *args, after=(), in_place=0, scratch=(), limit=24, micros=0):
+def local_call(kernel, outs, *args, after=(), scratch=(), streamed=False, micros=0.0):
     vmem = pl.BlockSpec(memory_space=pltpu.VMEM)
-    hbm = pl.BlockSpec(memory_space=pltpu.HBM)
     anywhere = pl.BlockSpec(memory_space=pl.ANY)
     count = len(args)
 
@@ -58,54 +57,55 @@
     return pl.pallas_call(
         body,
         out_shape=[jax.ShapeDtypeStruct(s, d) for s, d in outs],
-        in_specs=[vmem] * (count - in_place) + [hbm] * in_place + [anywhere] * len(after),
-        out_specs=[vmem] * len(outs),
+        in_specs=[vmem] * count + [anywhere] * len(after),
+        out_specs=[anywhere if streamed else vmem] * len(outs),
         scratch_shapes=scratch,
-        compiler_params=pltpu.CompilerParams(vmem_limit_bytes=limit << 20),
+        compiler_params=pltpu.CompilerParams(vmem_limit_bytes=24 << 20),
         cost_estimate=pl.CostEstimate(
-            flops=0, bytes_accessed=micros * 3_600_000, transcendentals=0
+            flops=int(micros * 1e9), bytes_accessed=int(micros * 3.6e6), transcendentals=0
         ),
     )(*args, *after)
 
 
-def kv_kernel(kv_o, kv_r, w_o, w_again, kvsel, psum, psum_sent):
+def kv_kernel(kv_o, k_r, v_r, kvsel, psum_sent):
     par, _ = place()
     later = par.astype(F32)
     for j in range(GROUPS):
         c = cols(2 * j + par)
         own = tn(kv_o[0, :, c], kv_o[1, :, c])
-        other = tn(kv_r[0, :, c], kv_r[1, :, c])
+        other = tn(k_r[:, c], v_r[:, c])
         kvsel[j] = other * later + own * (1.0 - later)
-        psum[j] = own + other
         psum_sent[j] = (own + other).astype(BF)
-    w_again[...] = w_o[...]
-
-
-def total_kernel(psum, received, total):
-    total[...] = (psum[...] + received[...].astype(F32)).astype(BF)
-
-
-def intra_kernel(qg_o, kv_o, qg_r, kv_r, intra):
+
+
+def pack_kernel(first, second, both):
+    both[0], both[1] = first[...], second[...]
+
+
+def intra_kernel(qg_o, kv_o, qg_r, k_r, v_r, intra):
     par, _ = place()
     mask = causal_mask()
-    for i, (qg, kv) in enumerate(((qg_o, kv_o), (qg_r, kv_r))):
+    kv_both = ((kv_o.at[0], kv_o.at[1]), (k_r, v_r))
+    for i, (qg, (k, v)) in enumerate(zip((qg_o, qg_r), kv_both)):
         for j in range(GROUPS):
             c = cols(2 * j + par)
-            scores = jnp.where(mask, nt(qg[0, :, c], kv[0, :, c]), 0.0).astype(BF)
-            intra[i, :, j * HEAD : (j + 1) * HEAD] = nn(scores, kv[1, :, c])
+            scores = jnp.where(mask, nt(qg[0, :, c], k[:, c]), 0.0).astype(BF)
+            intra[i, :, j * HEAD : (j + 1) * HEAD] = nn(scores, v[:, c])
 
 
 def attend_kernel(
-    att_scale, inv_root, qg_o, qg_r, intra, kvsel, kv_x, kv_y,
+    att_scale, inv_root, qg_o, qg_r, intra, kvsel, kv_x, kv_y, kv_d,
     to_x, to_y, keep, forward, state_o, state_r,
 ):
     par, chip = place()
     later = par.astype(F32)
     x_later = lax.rem(chip, 2).astype(F32)
+    y_later = lax.div(chip, 2).astype(F32)
     half = qg_o.shape[2] // 2
     for m in (3, 1, 2, 0):
         j = lax.bitwise_xor(chip, m)
-        earlier = kv_x[j].astype(F32) * x_later + kv_y[j].astype(F32)
+        earlier = kv_x[j].astype(F32) * x_later
+        earlier += (kv_y[j].astype(F32) + kv_d[j].astype(F32)) * y_later
         sel = kvsel[j]
         s_o = (earlier + later * sel).astype(BF)
         s_r = (earlier + (1.0 - later) * sel).astype(BF)
@@ -146,43 +146,46 @@
 
 
 def sum_kernel(own, *rest):
-    parts, (total, done) = rest[:-2], rest[-2:]
-    done[...] = jnp.zeros_like(done)
+    parts, total = rest[:-1], rest[-1]
     total[...] = own[...] + sum(part[...].astype(F32) for part in parts)
 
 
-def order_kernel(n_dp, first, *refs):
+def order_kernel(n_dp, *refs):
     parts, full = refs[:-1], refs[-1]
-    rows = full.shape[0] // n_dp
+    rows = parts[0].shape[0]
     d = lax.axis_index("dp")
-    if first:
-        full[...] = parts[0][...]
-        parts = parts[1:]
-    for m, part in enumerate(parts, first):
+    for m, part in enumerate(parts):
         at = pl.multiple_of(lax.bitwise_xor(d, m) * rows, rows)
         full[pl.ds(at, rows), :] = part[...]
 
 
-def att_grad_kernel(qg_o, qg_r, w_0, w_x, w_y, w_d0, w_d1, ag_o, ag_r, qdsel, psum, psum_sent):
+def head_grad(m, weights, qg_o, qg_r, ag_o, ag_r, qdsel, psum_sent):
     par, chip = place()
     later = par.astype(F32)
-    for m, weight in enumerate((w_0, w_x, w_y, None)):
-        j = lax.bitwise_xor(chip, m)
-        if weight is None:
-            a_o, a_r = (
-                jnp.concatenate([nt(g[1], w_d0[...]), nt(g[1], w_d1[...])], axis=1).astype(BF)
-                for g in (qg_o, qg_r)
-            )
-        else:
-            a_o, a_r = (nt(g[1], weight[...]).astype(BF) for g in (qg_o, qg_r))
-        ag_o[:, cols(j)] = a_o
-        ag_r[:, cols(j)] = a_r
-        c = cols(2 * j + par)
-        own = tn(a_o, qg_o[0, :, c])
-        other = tn(a_r, qg_r[0, :, c])
-        qdsel[j] = own * later + other * (1.0 - later)
-        psum[j] = own + other
-        psum_sent[j] = (own + other).astype(BF)
+    j = lax.bitwise_xor(chip, m)
+    c = cols(2 * j + par)
+    a_o, a_r = (
+        jnp.concatenate([nt(qg[1], w[...]) for w in weights], axis=1).astype(BF)
+        for qg in (qg_o, qg_r)
+    )
+    ag_o[:, cols(j)] = a_o
+    ag_r[:, cols(j)] = a_r
+    own = tn(a_o, qg_o[0, :, c])
+    other = tn(a_r, qg_r[0, :, c])
+    qdsel[j] = own * later + other * (1.0 - later)
+    psum_sent[j] = (own + other).astype(BF)
+
+
+def near_grad_kernel(qg_o, qg_r, w_0, w_x, w_y, *outs):
+    for m, weight in enumerate((w_0, w_x, w_y)):
+        head_grad(m, (weight,), qg_o, qg_r, *outs)
+
+
+def far_grad_kernel(qg_o, qg_r, w_d0, w_d1, *rest):
+    near, outs = rest[: len(rest) // 2], rest[len(rest) // 2 :]
+    for src, dst in zip(near, outs):
+        dst[...] = src[...]
+    head_grad(3, (w_d0, w_d1), qg_o, qg_r, *outs)
 
 
 def block_kernel(att_scale, qg_o, kv_o, ag_o, ag_p, st_o, st_p, dq, dk_in, dv_in):
@@ -201,26 +204,38 @@
             dv_in[:, c] = tn(scores, a)
 
 
-def carried_kernel(qdsel, qd_x, qd_y, car_o, car_r):
+def carried_kernel(qdsel, qd_x, qd_y, qd_d, car_o, car_r):
     par, chip = place()
     later = par.astype(F32)
     x_earlier = (1 - lax.rem(chip, 2)).astype(F32)
+    y_earlier = (1 - lax.div(chip, 2)).astype(F32)
     for j in range(GROUPS):
-        total = qd_x[j].astype(F32) * x_earlier + qd_y[j].astype(F32)
+        total = qd_x[j].astype(F32) * x_earlier
+        total += (qd_y[j].astype(F32) + qd_d[j].astype(F32)) * y_earlier
         sel = qdsel[j]
         car_o[j] = (total + (1.0 - later) * sel).astype(BF)
         car_r[j] = (total + later * sel).astype(BF)
 
 
-def finish_kernel(att_scale, kv_o, car_o, car_p, dk_in, dv_in, dk, dv):
+def finish_kernel(
+    att_scale, kv_o, car_o, car_p, dk_in, dv_in, summed, dk, dv, weight_grad, dk_here, dv_here, sems
+):
     par, _ = place()
+    copies = [pltpu.make_async_copy(summed, weight_grad, sems.at[4 * GROUPS])]
+    copies[0].start()
     for side, car in enumerate((car_o, car_p)):
         parity = par if side == 0 else 1 - par
         for j in range(GROUPS):
             c = cols(2 * j + parity)
             carried = car[j]
-            dk[:, c] = (att_scale * (dk_in[:, c] + nn(kv_o[1, :, c], carried))).astype(BF)
-            dv[:, c] = (att_scale * (dv_in[:, c] + nt(kv_o[0, :, c], carried))).astype(BF)
+            dk_here[:, c] = (att_scale * (dk_in[:, c] + nn(kv_o[1, :, c], carried))).astype(BF)
+            dv_here[:, c] = (att_scale * (dv_in[:, c] + nt(kv_o[0, :, c], carried))).astype(BF)
+            for here, out in ((dk_here, dk), (dv_here, dv)):
+                sem = sems.at[len(copies) - 1]
+                copies.append(pltpu.make_async_copy(here.at[:, c], out.at[:, c], sem))
+                copies[-1].start()
+    for copy in copies:
+        copy.wait()
 
 
 def per_device(n_ctx, n_dp, queries, key_vecs, value_vecs, out_grad, out_weight):
@@ -228,8 +243,8 @@
     att_scale = 1.0 / math.sqrt(HEAD * tok_count * n_ctx)
     inv_root = 1.0 / math.sqrt(n_dp * tok_count * n_ctx)
 
-    def along(bit, keep=lambda i: True):
-        return [(i, i ^ bit) for i in range(n_ctx) if keep(i)]
+    def along(bit):
+        return [(i, i ^ bit) for i in range(n_ctx)]
 
     def core(x):
         return lax.ppermute(x, "ctx", along(1))
@@ -239,6 +254,9 @@
 
     def over_y(x):
         return lax.ppermute(x, "ctx", along(4))
+
+    def over_both(x):
+        return lax.ppermute(x, "ctx", along(6))
 
     def along_dp(x, m):
         return lax.ppermute(x, "dp", [(i, i ^ m) for i in range(n_dp)])
@@ -246,30 +264,26 @@
     state = (GROUPS, HEAD, HEAD)
     half = width // 2
     rows = HEAD // n_dp
+    k_r, v_r = core(key_vecs[0]), core(value_vecs[0])
     kv_o = jnp.concatenate([key_vecs, value_vecs])
-    qg_o = jnp.concatenate([queries, out_grad])
-    kv_r = core(kv_o)
-    w_parts = [along_dp(out_weight, 1)]
-    w_again, kvsel, kv_own, kv_sent = local_call(
+    w_parts = [along_dp(out_weight, m) for m in range(1, n_dp)]
+    kvsel, kv_sent = local_call(
         kv_kernel,
-        [((rows, width), BF), (state, F32), (state, F32), (state, BF)],
-        kv_o, kv_r, out_weight,
-    )
-    kv_x = over_x(kv_sent)
-    w_parts += [along_dp(w_again, m) for m in range(2, n_dp)]
+        [(state, F32), (state, BF)],
+        kv_o, k_r, v_r,
+    )
+    (qg_o,) = local_call(
+        pack_kernel, [((2, BLOCK, width), BF)], queries[0], out_grad[0], after=(kv_sent,)
+    )
+    kv_x, kv_y, kv_d = over_x(kv_sent), over_y(kv_sent), over_both(kv_sent)
     qg_r = core(qg_o)
-    (w_two,) = local_call(
-        functools.partial(order_kernel, n_dp, 0), [((HEAD, width), BF)], w_again, w_parts[0],
-        micros=10,
+    (w_0,) = local_call(
+        functools.partial(order_kernel, n_dp),
+        [((HEAD, width), BF)], out_weight, *w_parts, after=(qg_o,), micros=20,
     )
     (intra,) = local_call(
-        intra_kernel, [((2, BLOCK, half), F32)], qg_o, kv_o, qg_r, kv_r, after=(w_two,)
-    )
-    (kv_total,) = local_call(total_kernel, [(state, BF)], kv_own, kv_x, after=(intra,))
-    kv_y = lax.ppermute(kv_total, "ctx", along(4, lambda i: i < i ^ 4))
-    (w_0,) = local_call(
-        functools.partial(order_kernel, n_dp, 2),
-        [((HEAD, width), BF)], w_two, *w_parts[1:], after=(kv_total,),
+        intra_kernel,
+        [((2, BLOCK, half), F32)], qg_o, kv_o, qg_r, k_r, v_r, after=(w_0,),
     )
     w_x, w_y = over_x(w_0), over_y(w_0)
     w_d0, w_d1 = over_y(w_x[: HEAD // 2]), over_x(w_y[HEAD // 2 :])
@@ -283,53 +297,56 @@
             (state, BF),
             (state, BF),
         ],
-        qg_o, qg_r, intra, kvsel, kv_x, kv_y,
-        after=(w_0,),
+        qg_o, qg_r, intra, kvsel, kv_x, kv_y, kv_d,
     )
     from_x, from_y = over_x(to_x), over_y(to_y)
     state_p = core(state_r)
+    grads = [((BLOCK, half), BF), ((BLOCK, half), BF), (state, F32), (state, BF)]
+    near = local_call(near_grad_kernel, grads, qg_o, qg_r, w_0, w_x, w_y, after=(to_x,))
     (pass_y,) = local_call(
-        functools.partial(forward_kernel, 0), [((HEAD, half), BF)], forward, from_x
+        functools.partial(forward_kernel, 0), [((HEAD, half), BF)], forward, from_x,
+        after=(near[3],),
     )
     (pass_x,) = local_call(
         functools.partial(forward_kernel, 1), [((HEAD, half), BF)], forward, from_y,
         after=(pass_y,),
     )
     last_y, last_x = over_y(pass_y), over_x(pass_x)
-    ag_o, ag_r, qdsel, qd_own, qd_sent = local_call(
-        att_grad_kernel,
-        [((BLOCK, half), BF), ((BLOCK, half), BF), (state, F32), (state, F32), (state, BF)],
-        qg_o, qg_r, w_0, w_x, w_y, w_d0, w_d1,
-        after=(pass_y, pass_x),
-    )
-    qd_x = over_x(qd_sent)
+    ag_o, ag_r, qdsel, qd_sent = local_call(
+        far_grad_kernel, grads, qg_o, qg_r, w_d0, w_d1, *near, after=(pass_x,)
+    )
+    qd_x, qd_y, qd_d = over_x(qd_sent), over_y(qd_sent), over_both(qd_sent)
     ag_p = core(ag_r)
     own, *send = local_call(
         functools.partial(fold_kernel, n_dp),
         [((rows, width), F32)] + [((rows, width), BF)] * (n_dp - 1),
         keep, from_x, from_y, last_y, last_x,
-        after=(qd_sent,),
+        after=(qd_sent,), micros=20,
     )
     got = [along_dp(send[m - 1], m) for m in range(1, n_dp)]
-    (qd_total,) = local_call(total_kernel, [(state, BF)], qd_own, qd_x, after=(send[0],))
-    qd_y = lax.ppermute(qd_total, "ctx", along(4, lambda i: i > i ^ 4))
     dq, dk_in, dv_in = local_call(
         functools.partial(block_kernel, att_scale),
         [((BLOCK, width), BF), ((BLOCK, width), F32), ((BLOCK, width), F32)],
         qg_o, kv_o, ag_o, ag_p, state_o, state_p,
-        after=(qd_total,),
-    )
-    weight_grad, summed = local_call(
-        sum_kernel, [((rows, width), F32), ((8, HEAD), F32)], own, *got, after=(dk_in,)
+        after=(send[0],),
     )
     car_o, car_r = local_call(
-        carried_kernel, [(state, BF), (state, BF)], qdsel, qd_x, qd_y, after=(summed,)
+        carried_kernel, [(state, BF), (state, BF)], qdsel, qd_x, qd_y, qd_d, after=(dk_in,)
     )
     car_p = core(car_r)
-    dk, dv = local_call(
+    (summed,) = local_call(
+        sum_kernel, [((rows, width), F32)], own, *got, after=(car_r,), micros=20
+    )
+    dk, dv, weight_grad = local_call(
         functools.partial(finish_kernel, att_scale),
-        [((BLOCK, width), BF), ((BLOCK, width), BF)],
-        kv_o, car_o, car_p, dk_in, dv_in,
+        [((BLOCK, width), BF), ((BLOCK, width), BF), ((rows, width), F32)],
+        kv_o, car_o, car_p, dk_in, dv_in, summed,
+        streamed=True,
+        scratch=[
+            pltpu.VMEM((BLOCK, width), BF),
+            pltpu.VMEM((BLOCK, width), BF),
+            pltpu.SemaphoreType.DMA((4 * GROUPS + 1,)),
+        ],
     )
     return dq[None], dk[None], dv[None], weight_grad
 

time: 59.8 us -> 50.3 us (0.84)
  waiting for transfers between devices: 16.9 us -> 9.8 us
  starting transfers between devices: 28.7 us -> 27.7 us
  local copies, waits for them, and re-layouts: 1.92 us -> 1.15 us
    ppermute x6, waiting for transfers between devices: 8.62 us -> 4.82 us  [over_x(): return lax.ppermute(x, 'ctx', along(2))]
    ppermute x2, starting transfers between devices: 4.72 us -> 1.81 us  [over_both(): return lax.ppermute(x, 'ctx', along(6))]
    ppermute x4 -> x6, starting transfers between devices: 5.29 us -> 7.95 us  [over_y(): return lax.ppermute(x, 'ctx', along(4))]
    ppermute x5 -> x6, waiting for transfers between devices: 2.43 us -> 0.7 us  [core(): return lax.ppermute(x, 'ctx', along(1))]
    ppermute x4 -> x6, waiting for transfers between devices: 2.74 us -> 1.14 us  [over_y(): return lax.ppermute(x, 'ctx', along(4))]
    ppermute x2, waiting for transfers between devices: 0.01 us -> 1.47 us  [over_both(): return lax.ppermute(x, 'ctx', along(6))]
    ppermute x6, waiting for transfers between devices: 3.09 us -> 1.67 us  [along_dp(): return lax.ppermute(x, 'dp', [(i, i ^ m) for i in range(n_dp)])]
    ppermute x6, starting transfers between devices: 8.64 us -> 7.35 us  [over_x(): return lax.ppermute(x, 'ctx', along(2))]
  transfers between devices with their start and end apart: 23 -> 26, of which waited for: 11 -> 9; matrix products, arithmetic and copies ran while one was open for 0% -> 2% of each run, Pallas kernels for 12% -> 18%
where the time goes in v3:
time: 50.3 us; the launch traced here: 50.2 us
  starting transfers between devices  27.7 us (55%)
  Pallas kernels  10.7 us (21%)
  waiting for transfers between devices  9.8 us (19%)
  local copies, waits for them, and re-layouts  1.15 us (2%)
  between operations  0.84 us (2%)
    pallas_call x14, Pallas kernels, local_call(): pl.pallas_call(body, out_shape=[jax.ShapeDtypeStruct(s, d) for s, d in ou...  10.7 us
    ppermute x6, starting transfers between devices, along_dp(): return lax.ppermute(x, 'dp', [(i, i ^ m) for i in range(n_dp)])  9.93 us
    ppermute x6, starting transfers between devices, over_y(): return lax.ppermute(x, 'ctx', along(4))  7.95 us
    ppermute x6, starting transfers between devices, over_x(): return lax.ppermute(x, 'ctx', along(2))  7.35 us
    ppermute x6, waiting for transfers between devices, over_x(): return lax.ppermute(x, 'ctx', along(2))  4.82 us
    ppermute x2, starting transfers between devices, over_both(): return lax.ppermute(x, 'ctx', along(6))  1.81 us
    ppermute x6, waiting for transfers between devices, along_dp(): return lax.ppermute(x, 'dp', [(i, i ^ m) for i in range(n_dp)])  1.67 us
    ppermute x2, waiting for transfers between devices, over_both(): return lax.ppermute(x, 'ctx', along(6))  1.47 us
  transfers between devices with their start and end apart: 26, of which 9 were waited for; matrix products, arithmetic and copies ran while one was open for 2% of the time, Pallas kernels for 18%

profile of v3, /device:TPU:0, one launch (start us, length us, event | category | flops | bytes accessed | tf_op | source)
XLA Modules:
  0.0 50.2 jit_solution(6384790325084557885)
XLA Ops:
  0.6 0.5 %collective-permute-start = (bf16[256,1024]{1,0:T(8,128)(2,1)}, bf16[256,1024]{1,0:T(8,128)(2,1)S(1)}, u32[]{:S(2)}, u32[]{:S(2)}) collective-permute-start(bf16[256,1024]{1,0:T(8,128)(2,1)} %bitcast.9), channel_id=1, source_target_pairs={{0,4},{4,0},{8,12},{12,8},{16,20},{20,16},{24,28},{28,24},{1,5},{5... | collective-permute-start | bytes 1572872 | tf_op jit(solution)/shard_map/ppermute | solution.py:250
  1.2 0.1 collective-permute-start.1
  1.2 3.0 %collective-permute-start.3 = (bf16[32,1024]{1,0:T(8,128)(2,1)}, bf16[32,1024]{1,0:T(8,128)(2,1)S(1)}, u32[]{:S(2)}, u32[]{:S(2)}) collective-permute-start(bf16[32,1024]{1,0:T(8,128)(2,1)} %refs_0_.1), channel_id=1, source_target_pairs={{0,1},{1,0},{2,3},{3,2},{4,5},{5,4},{6,7},{7,6},{8,9},{9,8},{10,11... | collective-permute-start | bytes 196616 | tf_op jit(solution)/shard_map/ppermute | solution.py:262
  4.2 2.6 %collective-permute-start.4 = (bf16[32,1024]{1,0:T(8,128)(2,1)}, bf16[32,1024]{1,0:T(8,128)(2,1)S(1)}, u32[]{:S(2)}, u32[]{:S(2)}) collective-permute-start(bf16[32,1024]{1,0:T(8,128)(2,1)} %refs_0_.1), channel_id=1, source_target_pairs={{0,2},{1,3},{2,0},{3,1},{4,6},{5,7},{6,4},{7,5},{8,10},{9,11},{10,... | collective-permute-start | bytes 196616 | tf_op jit(solution)/shard_map/ppermute | solution.py:262
  6.8 0.0 collective-permute-start.5
  6.8 1.1 %constant_dynamic-update-slice_fusion.1 = bf16[2,256,1024]{2,1,0:T(8,128)(2,1)S(1)} fusion(bf16[1,256,1024]{2,1,0:T(8,128)(2,1)} %param.6), kind=kLoop, calls=%fused_computation.1 | loop fusion | bytes 1048576
  8.0 0.0 copy-start
  8.0 0.0 copy-start.1
  8.0 0.0 collective-permute-done.refs_1_.refs_3_
  8.0 0.0 collective-permute-done.1.refs_2_.refs_4_
  8.0 0.5 shard_map.84
  8.5 1.8 %collective-permute-start.10 = (bf16[4,128,128]{2,1,0:T(8,128)(2,1)S(1)}, bf16[4,128,128]{2,1,0:T(8,128)(2,1)S(1)}, u32[]{:S(2)}, u32[]{:S(2)}) collective-permute-start(bf16[4,128,128]{2,1,0:T(8,128)(2,1)S(1)} %get-tuple-element.32.refs_2_), channel_id=1, source_target_pairs={{0,8},{4,12},{8,0},{12,4},{16,24},{20,28},{24,16},{28,20},{1,9},{5... | collective-permute-start | bytes 393224 | tf_op jit(solution)/shard_map/ppermute | solution.py:253
  10.3 1.5 %collective-permute-start.11 = (bf16[4,128,128]{2,1,0:T(8,128)(2,1)S(1)}, bf16[4,128,128]{2,1,0:T(8,128)(2,1)S(1)}, u32[]{:S(2)}, u32[]{:S(2)}) collective-permute-start(bf16[4,128,128]{2,1,0:T(8,128)(2,1)S(1)} %get-tuple-element.32.refs_2_), channel_id=1, source_target_pairs={{0,16},{4,20},{8,24},{12,28},{16,0},{20,4},{24,8},{28,12},{1,17},{... | collective-permute-start | bytes 393224 | tf_op jit(solution)/shard_map/ppermute | solution.py:256
  11.8 0.1 shard_map.85.refs_4_.refs_0_
  11.9 0.0 collective-permute-done.3.refs_1_
  11.9 0.3 collective-permute-start.12
  12.2 0.0 collective-permute-done.4.refs_2_
  12.2 0.0 collective-permute-start.2
  12.2 1.0 %collective-permute-done.5.refs_3_ = bf16[32,1024]{1,0:T(8,128)(2,1)S(1)} collective-permute-done((bf16[32,1024]{1,0:T(8,128)(2,1)}, bf16[32,1024]{1,0:T(8,128)(2,1)S(1)}, u32[]{:S(2)}, u32[]{:S(2)}) %collective-permute-start.5) | collective-permute-done | bytes 65568 | tf_op jit(solution)/shard_map/ppermute | solution.py:262
  13.2 1.6 %collective-permute-start.6 = (bf16[128,1024]{1,0:T(8,128)(2,1)S(1)}, bf16[128,1024]{1,0:T(8,128)(2,1)S(1)}, u32[]{:S(2)}, u32[]{:S(2)}) collective-permute-start(bf16[128,1024]{1,0:T(8,128)(2,1)S(1)} %shard_map.86.refs_5_.refs_2_), channel_id=1, source_target_pairs={{0,8},{4,12},{8,0},{12,4},{16,24},{20,28},{24,16},{28,20},{1,9},{5... | collective-permute-start | bytes 786440 | tf_op jit(solution)/shard_map/ppermute | solution.py:253
  14.8 0.1 collective-permute-done.2.refs_2_.refs_1_
  14.9 1.7 %collective-permute-start.8 = (bf16[128,1024]{1,0:T(8,128)(2,1)S(1)}, bf16[128,1024]{1,0:T(8,128)(2,1)S(1)}, u32[]{:S(2)}, u32[]{:S(2)}) collective-permute-start(bf16[128,1024]{1,0:T(8,128)(2,1)S(1)} %shard_map.86.refs_5_.refs_2_), channel_id=1, source_target_pairs={{0,16},{4,20},{8,24},{12,28},{16,0},{20,4},{24,8},{28,12},{1,17},{... | collective-permute-start | bytes 786440 | tf_op jit(solution)/shard_map/ppermute | solution.py:256
  16.6 0.9 %shard_map.87.refs_2_ = f32[2,256,512]{2,1,0:T(8,128)S(1)} custom-call(bf16[2,256,1024]{2,1,0:T(8,128)(2,1)S(1)} %shard_map.85.refs_4_.refs_0_, bf16[2,256,1024]{2,1,0:T(8,128)(2,1)S(1)} %constant_dynamic-update-slice_fusion.refs_0_.refs_1_, bf16[2,256,1024]{2,1,0:T(8,128)(2,1)S(1)} %collective-permute-done.2.refs_2_.refs_1_, ...), custom_call_target="tpu_custom_call" | custom-call | tf_op jit(solution)/shard_map/pallas_call | solution.py:57
  17.6 0.0 collective-permute-done.10.refs_4_
  17.6 0.0 collective-permute-done.11.refs_5_
  17.6 1.5 %collective-permute-done.12.refs_6_ = bf16[4,128,128]{2,1,0:T(8,128)(2,1)S(1)} collective-permute-done((bf16[4,128,128]{2,1,0:T(8,128)(2,1)S(1)}, bf16[4,128,128]{2,1,0:T(8,128)(2,1)S(1)}, u32[]{:S(2)}, u32[]{:S(2)}) %collective-permute-start.12) | collective-permute-done | bytes 131104 | tf_op jit(solution)/shard_map/ppermute | solution.py:259
  19.0 1.6 %shard_map.88 = (bf16[2,128,512]{2,1,0:T(8,128)(2,1)S(1)}, bf16[2,128,512]{2,1,0:T(8,128)(2,1)S(1)}, f32[128,1024]{1,0:T(8,128)S(1)}, f32[2,128,512]{2,1,0:T(8,1...) custom-call(bf16[2,256,1024]{2,1,0:T(8,128)(2,1)S(1)} %shard_map.85.refs_4_.refs_0_, ...), custom_call_target="tpu_custom_call" | custom-call | tf_op jit(solution)/shard_map/pallas_call | solution.py:57
  20.6 0.8 %collective-permute-start.14 = (bf16[2,128,512]{2,1,0:T(8,128)(2,1)S(1)}, bf16[2,128,512]{2,1,0:T(8,128)(2,1)S(1)}, u32[]{:S(2)}, u32[]{:S(2)}) collective-permute-start(bf16[2,128,512]{2,1,0:T(8,128)(2,1)S(1)} %get-tuple-element.34.refs_5_), channel_id=1, source_target_pairs={{0,8},{4,12},{8,0},{12,4},{16,24},{20,28},{24,16},{28,20},{1,9},{5... | collective-permute-start | bytes 786440 | tf_op jit(solution)/shard_map/ppermute | solution.py:253
  21.4 0.6 %collective-permute-start.13 = (bf16[2,128,512]{2,1,0:T(8,128)(2,1)S(1)}, bf16[2,128,512]{2,1,0:T(8,128)(2,1)S(1)}, u32[]{:S(2)}, u32[]{:S(2)}) collective-permute-start(bf16[2,128,512]{2,1,0:T(8,128)(2,1)S(1)} %get-tuple-element.40), channel_id=1, source_target_pairs={{0,16},{4,20},{8,24},{12,28},{16,0},{20,4},{24,8},{28,12},{1,17},{... | collective-permute-start | bytes 786440 | tf_op jit(solution)/shard_map/ppermute | solution.py:256
  22.0 1.1 %collective-permute-done.6.refs_3_ = bf16[128,1024]{1,0:T(8,128)(2,1)S(1)} collective-permute-done((bf16[128,1024]{1,0:T(8,128)(2,1)S(1)}, bf16[128,1024]{1,0:T(8,128)(2,1)S(1)}, u32[]{:S(2)}, u32[]{:S(2)}) %collective-permute-start.6) | collective-permute-done | bytes 262176 | tf_op jit(solution)/shard_map/ppermute | solution.py:253
  23.1 2.2 %collective-permute-start.7 = (bf16[64,1024]{1,0:T(8,128)(2,1)S(1)}, bf16[64,1024]{1,0:T(8,128)(2,1)S(1)}, u32[]{:S(2)}, u32[]{:S(2)}) collective-permute-start(bf16[64,1024]{1,0:T(8,128)(2,1)S(1)} %slice.8), channel_id=1, source_target_pairs={{0,16},{4,20},{8,24},{12,28},{16,0},{20,4},{24,8},{28,12},{1,17},{... | collective-permute-start | bytes 393224 | tf_op jit(solution)/shard_map/ppermute | solution.py:256
  25.3 0.0 collective-permute-done.8.refs_4_
  25.3 0.8 %collective-permute-start.9 = (bf16[64,1024]{1,0:T(8,128)(2,1)S(1)}, bf16[64,1024]{1,0:T(8,128)(2,1)S(1)}, u32[]{:S(2)}, u32[]{:S(2)}) collective-permute-start(bf16[64,1024]{1,0:T(8,128)(2,1)S(1)} %slice.9), channel_id=1, source_target_pairs={{0,8},{4,12},{8,0},{12,4},{16,24},{20,28},{24,16},{28,20},{1,9},{5... | collective-permute-start | bytes 393224 | tf_op jit(solution)/shard_map/ppermute | solution.py:253
  26.1 1.6 %shard_map.89 = (bf16[256,512]{1,0:T(8,128)(2,1)S(1)}, bf16[256,512]{1,0:T(8,128)(2,1)S(1)}, f32[4,128,128]{2,1,0:T(8,128)S(1)}, bf16[4,128,128]{2,1,0:T(8,128)(2,1)S(1)}) custom-call(bf16[2,256,1024]{2,1,0:T(8,128)(2,1)S(1)} %shard_map.85.refs_4_.refs_0_, bf16[2,256,1024]{2,1,0:T(8,128)(2,1)S(1)} %collective-permute-done.2.refs_2_.refs_1_, ...), custom_call_target="tpu_custom_call" | custom-call | tf_op jit(solution)/shard_map/pallas_call | solution.py:57
  27.7 1.8 %collective-permute-done.14.refs_1_ = bf16[2,128,512]{2,1,0:T(8,128)(2,1)S(1)} collective-permute-done((bf16[2,128,512]{2,1,0:T(8,128)(2,1)S(1)}, bf16[2,128,512]{2,1,0:T(8,128)(2,1)S(1)}, u32[]{:S(2)}, u32[]{:S(2)}) %collective-permute-start.14) | collective-permute-done | bytes 262176 | tf_op jit(solution)/shard_map/ppermute | solution.py:253
  29.5 1.1 %collective-permute-done.13.refs_1_.refs_2_ = bf16[2,128,512]{2,1,0:T(8,128)(2,1)S(1)} collective-permute-done((bf16[2,128,512]{2,1,0:T(8,128)(2,1)S(1)}, bf16[2,128,512]{2,1,0:T(8,128)(2,1)S(1)}, u32[]{:S(2)}, u32[]{:S(2)}) %collective-permute-start.13) | collective-permute-done | bytes 262176 | tf_op jit(solution)/shard_map/ppermute | solution.py:256
  30.7 1.4 %collective-permute-start.18 = (bf16[128,512]{1,0:T(8,128)(2,1)S(1)}, bf16[128,512]{1,0:T(8,128)(2,1)S(1)}, u32[]{:S(2)}, u32[]{:S(2)}) collective-permute-start(bf16[128,512]{1,0:T(8,128)(2,1)S(1)} %shard_map.91.refs_8_), channel_id=1, source_target_pairs={{0,8},{4,12},{8,0},{12,4},{16,24},{20,28},{24,16},{28,20},{1,9},{5... | collective-permute-start | bytes 393224 | tf_op jit(solution)/shard_map/ppermute | solution.py:253
  32.1 0.9 %collective-permute-start.17 = (bf16[128,512]{1,0:T(8,128)(2,1)S(1)}, bf16[128,512]{1,0:T(8,128)(2,1)S(1)}, u32[]{:S(2)}, u32[]{:S(2)}) collective-permute-start(bf16[128,512]{1,0:T(8,128)(2,1)S(1)} %shard_map.90.refs_2_), channel_id=1, source_target_pairs={{0,16},{4,20},{8,24},{12,28},{16,0},{20,4},{24,8},{28,12},{1,17},{... | collective-permute-start | bytes 393224 | tf_op jit(solution)/shard_map/ppermute | solution.py:256
  33.0 0.0 collective-permute-start.16
  33.0 0.0 collective-permute-done.7.refs_2_
  33.0 0.0 collective-permute-done.9.refs_3_
  33.0 1.0 %shard_map.92 = (bf16[256,512]{1,0:T(8,128)(2,1)S(1)}, bf16[256,512]{1,0:T(8,128)(2,1)S(1)}, f32[4,128,128]{2,1,0:T(8,128)S(1)}, bf16[4,128,128]{2,1,0:T(8,128)(2,1)S(1)}) custom-call(bf16[2,256,1024]{2,1,0:T(8,128)(2,1)S(1)} %shard_map.85.refs_4_.refs_0_, bf16[2,256,1024]{2,1,0:T(8,128)(2,1)S(1)} %collective-permute-done.2.refs_2_.refs_1_, ...), custom_call_target="tpu_custom_call" | custom-call | tf_op jit(solution)/shard_map/pallas_call | solution.py:57
  34.0 1.1 %collective-permute-start.19 = (bf16[4,128,128]{2,1,0:T(8,128)(2,1)S(1)}, bf16[4,128,128]{2,1,0:T(8,128)(2,1)S(1)}, u32[]{:S(2)}, u32[]{:S(2)}) collective-permute-start(bf16[4,128,128]{2,1,0:T(8,128)(2,1)S(1)} %get-tuple-element.46.refs_5_), channel_id=1, source_target_pairs={{0,8},{4,12},{8,0},{12,4},{16,24},{20,28},{24,16},{28,20},{1,9},{5... | collective-permute-start | bytes 393224 | tf_op jit(solution)/shard_map/ppermute | solution.py:253
  35.1 1.0 %collective-permute-start.20 = (bf16[4,128,128]{2,1,0:T(8,128)(2,1)S(1)}, bf16[4,128,128]{2,1,0:T(8,128)(2,1)S(1)}, u32[]{:S(2)}, u32[]{:S(2)}) collective-permute-start(bf16[4,128,128]{2,1,0:T(8,128)(2,1)S(1)} %get-tuple-element.46.refs_5_), channel_id=1, source_target_pairs={{0,16},{4,20},{8,24},{12,28},{16,0},{20,4},{24,8},{28,12},{1,17},{... | collective-permute-start | bytes 393224 | tf_op jit(solution)/shard_map/ppermute | solution.py:256
  36.0 0.0 collective-permute-done.18.refs_4_
  36.0 1.5 %collective-permute-start.21 = (bf16[4,128,128]{2,1,0:T(8,128)(2,1)S(1)}, bf16[4,128,128]{2,1,0:T(8,128)(2,1)S(1)}, u32[]{:S(2)}, u32[]{:S(2)}) collective-permute-start(bf16[4,128,128]{2,1,0:T(8,128)(2,1)S(1)} %get-tuple-element.46.refs_5_), channel_id=1, source_target_pairs={{0,24},{4,28},{8,16},{12,20},{16,8},{20,12},{24,0},{28,4},{1,25},{... | collective-permute-start | bytes 393224 | tf_op jit(solution)/shard_map/ppermute | solution.py:259
  37.5 0.0 collective-permute-done.17.refs_3_
  37.5 0.0 collective-permute-start.15
  37.5 0.1 shard_map.93
  37.6 0.0 collective-permute-done.16.refs_5_
  37.6 0.7 %collective-permute-start.23 = (bf16[32,1024]{1,0:T(8,128)(2,1)S(1)}, bf16[32,1024]{1,0:T(8,128)(2,1)S(1)}, u32[]{:S(2)}, u32[]{:S(2)}) collective-permute-start(bf16[32,1024]{1,0:T(8,128)(2,1)S(1)} %get-tuple-element.47.refs_6_), channel_id=1, source_target_pairs={{0,1},{1,0},{2,3},{3,2},{4,5},{5,4},{6,7},{7,6},{8,9},{9,8},{10,11... | collective-permute-start | bytes 196616 | tf_op jit(solution)/shard_map/ppermute | solution.py:262
  38.4 2.0 %collective-permute-done.19.refs_1_ = bf16[4,128,128]{2,1,0:T(8,128)(2,1)S(1)} collective-permute-done((bf16[4,128,128]{2,1,0:T(8,128)(2,1)S(1)}, bf16[4,128,128]{2,1,0:T(8,128)(2,1)S(1)}, u32[]{:S(2)}, u32[]{:S(2)}) %collective-permute-start.19) | collective-permute-done | bytes 131104 | tf_op jit(solution)/shard_map/ppermute | solution.py:253
  40.3 1.7 %collective-permute-start.24 = (bf16[32,1024]{1,0:T(8,128)(2,1)S(1)}, bf16[32,1024]{1,0:T(8,128)(2,1)S(1)}, u32[]{:S(2)}, u32[]{:S(2)}) collective-permute-start(bf16[32,1024]{1,0:T(8,128)(2,1)S(1)} %get-tuple-element.55), channel_id=1, source_target_pairs={{0,2},{1,3},{2,0},{3,1},{4,6},{5,7},{6,4},{7,5},{8,10},{9,11},{10,... | collective-permute-start | bytes 196616 | tf_op jit(solution)/shard_map/ppermute | solution.py:262
  42.0 0.0 collective-permute-done.15.refs_3_
  42.0 1.9 %collective-permute-start.25 = (bf16[32,1024]{1,0:T(8,128)(2,1)S(1)}, bf16[32,1024]{1,0:T(8,128)(2,1)S(1)}, u32[]{:S(2)}, u32[]{:S(2)}) collective-permute-start(bf16[32,1024]{1,0:T(8,128)(2,1)S(1)} %get-tuple-element.56), channel_id=1, source_target_pairs={{0,3},{1,2},{2,1},{3,0},{4,7},{5,6},{6,5},{7,4},{8,11},{9,10},{10,... | collective-permute-start | bytes 196616 | tf_op jit(solution)/shard_map/ppermute | solution.py:262
  43.9 3.3 %shard_map.94 = (bf16[256,1024]{1,0:T(8,128)(2,1)}, f32[256,1024]{1,0:T(8,128)S(1)}, f32[256,1024]{1,0:T(8,128)S(1)}) custom-call(bf16[2,256,1024]{2,1,0:T(8,128)(2,1)S(1)} %shard_map.85.refs_4_.refs_0_, bf16[2,256,1024]{2,1,0:T(8,128)(2,1)S(1)} %constant_dynamic-update-slice_fusion.refs_0_.refs_1_, bf16[256,512]{1,0:T(8,128)(2,1)S(1)} %get-tuple-element.41.refs_2_, ...), custom_call_target="tpu_custom_call" | custom-call | tf_op jit(solution)/shard_map/pallas_call | solution.py:57
  47.2 0.0 collective-permute-done.20.refs_2_
  47.2 0.0 collective-permute-done.21.refs_3_
  47.2 0.1 shard_map.95
  47.4 0.1 collective-permute-start.22
  47.4 0.0 collective-permute-done.23.refs_1_
  47.5 0.7 %collective-permute-done.25.refs_3_ = bf16[32,1024]{1,0:T(8,128)(2,1)S(1)} collective-permute-done((bf16[32,1024]{1,0:T(8,128)(2,1)S(1)}, bf16[32,1024]{1,0:T(8,128)(2,1)S(1)}, u32[]{:S(2)}, u32[]{:S(2)}) %collective-permute-start.25) | collective-permute-done | bytes 65568 | tf_op jit(solution)/shard_map/ppermute | solution.py:262
  48.2 0.6 %collective-permute-done.22.refs_2_ = bf16[4,128,128]{2,1,0:T(8,128)(2,1)S(1)} collective-permute-done((bf16[4,128,128]{2,1,0:T(8,128)(2,1)S(1)}, bf16[4,128,128]{2,1,0:T(8,128)(2,1)S(1)}, u32[]{:S(2)}, u32[]{:S(2)}) %collective-permute-start.22) | collective-permute-done | bytes 131104 | tf_op jit(solution)/shard_map/ppermute | solution.py:250
  48.8 1.4 %shard_map.97 = (bf16[256,1024]{1,0:T(8,128)(2,1)}, bf16[256,1024]{1,0:T(8,128)(2,1)}, f32[32,1024]{1,0:T(8,128)}) custom-call(bf16[2,256,1024]{2,1,0:T(8,128)(2,1)S(1)} %constant_dynamic-update-slice_fusion.refs_0_.refs_1_, bf16[4,128,128]{2,1,0:T(8,128)(2,1)S(1)} %get-tuple-element.51.refs_1_, bf16[4,128,128]{2,1,0:T(8,128)(2,1)S(1)} %collective-permute-done.22.refs_2_, ...), custom_call_target="tpu_custom_call" | custom-call | tf_op jit(solution)/shard_map/pallas_call | solution.py:57
  (14 shorter events, 0.2 us)
Async XLA Ops:
  0.6 7.4 %collective-permute-start = (bf16[256,1024]{1,0:T(8,128)(2,1)}, bf16[256,1024]{1,0:T(8,128)(2,1)S(1)}, u32[]{:S(2)}, u32[]{:S(2)}) collective-permute-start(bf16[256,1024]{1,0:T(8,128)(2,1)} %bitcast.9), channel_id=1, source_target_pairs={{0,4},{4,0},{8,12},{12,8},{16,20},{20,16},{24,28},{28,24},{1,5},{5... | collective-permute-start | bytes 1572872 | tf_op jit(solution)/shard_map/ppermute | solution.py:250
  1.1 6.8 %copy-start.3 = (bf16[1,256,1024]{2,1,0:T(8,128)(2,1)S(1)}, bf16[1,256,1024]{2,1,0:T(8,128)(2,1)}, u32[]{:S(2)}) copy-start(bf16[1,256,1024]{2,1,0:T(8,128)(2,1)} %param.7) | copy-start | bytes 1572868
  1.2 6.8 %collective-permute-start.1 = (bf16[256,1024]{1,0:T(8,128)(2,1)}, bf16[256,1024]{1,0:T(8,128)(2,1)S(1)}, u32[]{:S(2)}, u32[]{:S(2)}) collective-permute-start(bf16[256,1024]{1,0:T(8,128)(2,1)} %bitcast.10), channel_id=1, source_target_pairs={{0,4},{4,0},{8,12},{12,8},{16,20},{20,16},{24,28},{28,24},{1,5},{5... | collective-permute-start | bytes 1572872 | tf_op jit(solution)/shard_map/ppermute | solution.py:250
  1.2 10.6 %collective-permute-start.3 = (bf16[32,1024]{1,0:T(8,128)(2,1)}, bf16[32,1024]{1,0:T(8,128)(2,1)S(1)}, u32[]{:S(2)}, u32[]{:S(2)}) collective-permute-start(bf16[32,1024]{1,0:T(8,128)(2,1)} %refs_0_.1), channel_id=1, source_target_pairs={{0,1},{1,0},{2,3},{3,2},{4,5},{5,4},{6,7},{7,6},{8,9},{9,8},{10,11... | collective-permute-start | bytes 196616 | tf_op jit(solution)/shard_map/ppermute | solution.py:262
  4.2 8.0 %collective-permute-start.4 = (bf16[32,1024]{1,0:T(8,128)(2,1)}, bf16[32,1024]{1,0:T(8,128)(2,1)S(1)}, u32[]{:S(2)}, u32[]{:S(2)}) collective-permute-start(bf16[32,1024]{1,0:T(8,128)(2,1)} %refs_0_.1), channel_id=1, source_target_pairs={{0,2},{1,3},{2,0},{3,1},{4,6},{5,7},{6,4},{7,5},{8,10},{9,11},{10,... | collective-permute-start | bytes 196616 | tf_op jit(solution)/shard_map/ppermute | solution.py:262
  6.8 6.4 %collective-permute-start.5 = (bf16[32,1024]{1,0:T(8,128)(2,1)}, bf16[32,1024]{1,0:T(8,128)(2,1)S(1)}, u32[]{:S(2)}, u32[]{:S(2)}) collective-permute-start(bf16[32,1024]{1,0:T(8,128)(2,1)} %refs_0_.1), channel_id=1, source_target_pairs={{0,3},{1,2},{2,1},{3,0},{4,7},{5,6},{6,5},{7,4},{8,11},{9,10},{10,... | collective-permute-start | bytes 196616 | tf_op jit(solution)/shard_map/ppermute | solution.py:262
  8.0 3.8 %copy-start = (bf16[1,256,1024]{2,1,0:T(8,128)(2,1)S(1)}, bf16[1,256,1024]{2,1,0:T(8,128)(2,1)}, u32[]{:S(2)}) copy-start(bf16[1,256,1024]{2,1,0:T(8,128)(2,1)} %param.5) | copy-start | bytes 1572868
  8.0 3.8 %copy-start.1 = (bf16[1,256,1024]{2,1,0:T(8,128)(2,1)S(1)}, bf16[1,256,1024]{2,1,0:T(8,128)(2,1)}, u32[]{:S(2)}) copy-start(bf16[1,256,1024]{2,1,0:T(8,128)(2,1)} %param.8) | copy-start | bytes 1572868
  8.5 9.1 %collective-permute-start.10 = (bf16[4,128,128]{2,1,0:T(8,128)(2,1)S(1)}, bf16[4,128,128]{2,1,0:T(8,128)(2,1)S(1)}, u32[]{:S(2)}, u32[]{:S(2)}) collective-permute-start(bf16[4,128,128]{2,1,0:T(8,128)(2,1)S(1)} %get-tuple-element.32.refs_2_), channel_id=1, source_target_pairs={{0,8},{4,12},{8,0},{12,4},{16,24},{20,28},{24,16},{28,20},{1,9},{5... | collective-permute-start | bytes 393224 | tf_op jit(solution)/shard_map/ppermute | solution.py:253
  10.3 7.3 %collective-permute-start.11 = (bf16[4,128,128]{2,1,0:T(8,128)(2,1)S(1)}, bf16[4,128,128]{2,1,0:T(8,128)(2,1)S(1)}, u32[]{:S(2)}, u32[]{:S(2)}) collective-permute-start(bf16[4,128,128]{2,1,0:T(8,128)(2,1)S(1)} %get-tuple-element.32.refs_2_), channel_id=1, source_target_pairs={{0,16},{4,20},{8,24},{12,28},{16,0},{20,4},{24,8},{28,12},{1,17},{... | collective-permute-start | bytes 393224 | tf_op jit(solution)/shard_map/ppermute | solution.py:256
  11.8 1.4 %copy-start.2 = (bf16[32,1024]{1,0:T(8,128)(2,1)S(1)}, bf16[32,1024]{1,0:T(8,128)(2,1)}, u32[]{:S(2)}) copy-start(bf16[32,1024]{1,0:T(8,128)(2,1)} %refs_0_.1) | copy-start | bytes 196612
  11.9 7.2 %collective-permute-start.12 = (bf16[4,128,128]{2,1,0:T(8,128)(2,1)S(1)}, bf16[4,128,128]{2,1,0:T(8,128)(2,1)S(1)}, u32[]{:S(2)}, u32[]{:S(2)}) collective-permute-start(bf16[4,128,128]{2,1,0:T(8,128)(2,1)S(1)} %get-tuple-element.32.refs_2_), channel_id=1, source_target_pairs={{0,24},{4,28},{8,16},{12,20},{16,8},{20,12},{24,0},{28,4},{1,25},{... | collective-permute-start | bytes 393224 | tf_op jit(solution)/shard_map/ppermute | solution.py:259
  12.2 2.7 %collective-permute-start.2 = (bf16[2,256,1024]{2,1,0:T(8,128)(2,1)S(1)}, bf16[2,256,1024]{2,1,0:T(8,128)(2,1)S(1)}, u32[]{:S(2)}, u32[]{:S(2)}) collective-permute-start(bf16[2,256,1024]{2,1,0:T(8,128)(2,1)S(1)} %shard_map.85.refs_4_.refs_0_), channel_id=1, source_target_pairs={{0,4},{4,0},{8,12},{12,8},{16,20},{20,16},{24,28},{28,24},{1,5},{5... | collective-permute-start | bytes 3145736 | tf_op jit(solution)/shard_map/ppermute | solution.py:250
  13.2 9.9 %collective-permute-start.6 = (bf16[128,1024]{1,0:T(8,128)(2,1)S(1)}, bf16[128,1024]{1,0:T(8,128)(2,1)S(1)}, u32[]{:S(2)}, u32[]{:S(2)}) collective-permute-start(bf16[128,1024]{1,0:T(8,128)(2,1)S(1)} %shard_map.86.refs_5_.refs_2_), channel_id=1, source_target_pairs={{0,8},{4,12},{8,0},{12,4},{16,24},{20,28},{24,16},{28,20},{1,9},{5... | collective-permute-start | bytes 786440 | tf_op jit(solution)/shard_map/ppermute | solution.py:253
  14.9 10.4 %collective-permute-start.8 = (bf16[128,1024]{1,0:T(8,128)(2,1)S(1)}, bf16[128,1024]{1,0:T(8,128)(2,1)S(1)}, u32[]{:S(2)}, u32[]{:S(2)}) collective-permute-start(bf16[128,1024]{1,0:T(8,128)(2,1)S(1)} %shard_map.86.refs_5_.refs_2_), channel_id=1, source_target_pairs={{0,16},{4,20},{8,24},{12,28},{16,0},{20,4},{24,8},{28,12},{1,17},{... | collective-permute-start | bytes 786440 | tf_op jit(solution)/shard_map/ppermute | solution.py:256
  20.6 8.8 %collective-permute-start.14 = (bf16[2,128,512]{2,1,0:T(8,128)(2,1)S(1)}, bf16[2,128,512]{2,1,0:T(8,128)(2,1)S(1)}, u32[]{:S(2)}, u32[]{:S(2)}) collective-permute-start(bf16[2,128,512]{2,1,0:T(8,128)(2,1)S(1)} %get-tuple-element.34.refs_5_), channel_id=1, source_target_pairs={{0,8},{4,12},{8,0},{12,4},{16,24},{20,28},{24,16},{28,20},{1,9},{5... | collective-permute-start | bytes 786440 | tf_op jit(solution)/shard_map/ppermute | solution.py:253
  21.4 9.2 %collective-permute-start.13 = (bf16[2,128,512]{2,1,0:T(8,128)(2,1)S(1)}, bf16[2,128,512]{2,1,0:T(8,128)(2,1)S(1)}, u32[]{:S(2)}, u32[]{:S(2)}) collective-permute-start(bf16[2,128,512]{2,1,0:T(8,128)(2,1)S(1)} %get-tuple-element.40), channel_id=1, source_target_pairs={{0,16},{4,20},{8,24},{12,28},{16,0},{20,4},{24,8},{28,12},{1,17},{... | collective-permute-start | bytes 786440 | tf_op jit(solution)/shard_map/ppermute | solution.py:256
  23.1 9.8 %collective-permute-start.7 = (bf16[64,1024]{1,0:T(8,128)(2,1)S(1)}, bf16[64,1024]{1,0:T(8,128)(2,1)S(1)}, u32[]{:S(2)}, u32[]{:S(2)}) collective-permute-start(bf16[64,1024]{1,0:T(8,128)(2,1)S(1)} %slice.8), channel_id=1, source_target_pairs={{0,16},{4,20},{8,24},{12,28},{16,0},{20,4},{24,8},{28,12},{1,17},{... | collective-permute-start | bytes 393224 | tf_op jit(solution)/shard_map/ppermute | solution.py:256
  25.3 7.7 %collective-permute-start.9 = (bf16[64,1024]{1,0:T(8,128)(2,1)S(1)}, bf16[64,1024]{1,0:T(8,128)(2,1)S(1)}, u32[]{:S(2)}, u32[]{:S(2)}) collective-permute-start(bf16[64,1024]{1,0:T(8,128)(2,1)S(1)} %slice.9), channel_id=1, source_target_pairs={{0,8},{4,12},{8,0},{12,4},{16,24},{20,28},{24,16},{28,20},{1,9},{5... | collective-permute-start | bytes 393224 | tf_op jit(solution)/shard_map/ppermute | solution.py:253
  30.7 5.4 %collective-permute-start.18 = (bf16[128,512]{1,0:T(8,128)(2,1)S(1)}, bf16[128,512]{1,0:T(8,128)(2,1)S(1)}, u32[]{:S(2)}, u32[]{:S(2)}) collective-permute-start(bf16[128,512]{1,0:T(8,128)(2,1)S(1)} %shard_map.91.refs_8_), channel_id=1, source_target_pairs={{0,8},{4,12},{8,0},{12,4},{16,24},{20,28},{24,16},{28,20},{1,9},{5... | collective-permute-start | bytes 393224 | tf_op jit(solution)/shard_map/ppermute | solution.py:253
  32.1 5.5 %collective-permute-start.17 = (bf16[128,512]{1,0:T(8,128)(2,1)S(1)}, bf16[128,512]{1,0:T(8,128)(2,1)S(1)}, u32[]{:S(2)}, u32[]{:S(2)}) collective-permute-start(bf16[128,512]{1,0:T(8,128)(2,1)S(1)} %shard_map.90.refs_2_), channel_id=1, source_target_pairs={{0,16},{4,20},{8,24},{12,28},{16,0},{20,4},{24,8},{28,12},{1,17},{... | collective-permute-start | bytes 393224 | tf_op jit(solution)/shard_map/ppermute | solution.py:256
  33.0 4.6 %collective-permute-start.16 = (bf16[4,128,128]{2,1,0:T(8,128)(2,1)S(1)}, bf16[4,128,128]{2,1,0:T(8,128)(2,1)S(1)}, u32[]{:S(2)}, u32[]{:S(2)}) collective-permute-start(bf16[4,128,128]{2,1,0:T(8,128)(2,1)S(1)} %get-tuple-element.44), channel_id=1, source_target_pairs={{0,4},{4,0},{8,12},{12,8},{16,20},{20,16},{24,28},{28,24},{1,5},{5... | collective-permute-start | bytes 393224 | tf_op jit(solution)/shard_map/ppermute | solution.py:250
  34.0 6.4 %collective-permute-start.19 = (bf16[4,128,128]{2,1,0:T(8,128)(2,1)S(1)}, bf16[4,128,128]{2,1,0:T(8,128)(2,1)S(1)}, u32[]{:S(2)}, u32[]{:S(2)}) collective-permute-start(bf16[4,128,128]{2,1,0:T(8,128)(2,1)S(1)} %get-tuple-element.46.refs_5_), channel_id=1, source_target_pairs={{0,8},{4,12},{8,0},{12,4},{16,24},{20,28},{24,16},{28,20},{1,9},{5... | collective-permute-start | bytes 393224 | tf_op jit(solution)/shard_map/ppermute | solution.py:253
  35.1 12.2 %collective-permute-start.20 = (bf16[4,128,128]{2,1,0:T(8,128)(2,1)S(1)}, bf16[4,128,128]{2,1,0:T(8,128)(2,1)S(1)}, u32[]{:S(2)}, u32[]{:S(2)}) collective-permute-start(bf16[4,128,128]{2,1,0:T(8,128)(2,1)S(1)} %get-tuple-element.46.refs_5_), channel_id=1, source_target_pairs={{0,16},{4,20},{8,24},{12,28},{16,0},{20,4},{24,8},{28,12},{1,17},{... | collective-permute-start | bytes 393224 | tf_op jit(solution)/shard_map/ppermute | solution.py:256
  36.0 11.2 %collective-permute-start.21 = (bf16[4,128,128]{2,1,0:T(8,128)(2,1)S(1)}, bf16[4,128,128]{2,1,0:T(8,128)(2,1)S(1)}, u32[]{:S(2)}, u32[]{:S(2)}) collective-permute-start(bf16[4,128,128]{2,1,0:T(8,128)(2,1)S(1)} %get-tuple-element.46.refs_5_), channel_id=1, source_target_pairs={{0,24},{4,28},{8,16},{12,20},{16,8},{20,12},{24,0},{28,4},{1,25},{... | collective-permute-start | bytes 393224 | tf_op jit(solution)/shard_map/ppermute | solution.py:259
  37.5 4.5 %collective-permute-start.15 = (bf16[256,512]{1,0:T(8,128)(2,1)S(1)}, bf16[256,512]{1,0:T(8,128)(2,1)S(1)}, u32[]{:S(2)}, u32[]{:S(2)}) collective-permute-start(bf16[256,512]{1,0:T(8,128)(2,1)S(1)} %get-tuple-element.42), channel_id=1, source_target_pairs={{0,4},{4,0},{8,12},{12,8},{16,20},{20,16},{24,28},{28,24},{1,5},{5... | collective-permute-start | bytes 786440 | tf_op jit(solution)/shard_map/ppermute | solution.py:250
  37.6 9.8 %collective-permute-start.23 = (bf16[32,1024]{1,0:T(8,128)(2,1)S(1)}, bf16[32,1024]{1,0:T(8,128)(2,1)S(1)}, u32[]{:S(2)}, u32[]{:S(2)}) collective-permute-start(bf16[32,1024]{1,0:T(8,128)(2,1)S(1)} %get-tuple-element.47.refs_6_), channel_id=1, source_target_pairs={{0,1},{1,0},{2,3},{3,2},{4,5},{5,4},{6,7},{7,6},{8,9},{9,8},{10,11... | collective-permute-start | bytes 196616 | tf_op jit(solution)/shard_map/ppermute | solution.py:262
  40.3 7.1 %collective-permute-start.24 = (bf16[32,1024]{1,0:T(8,128)(2,1)S(1)}, bf16[32,1024]{1,0:T(8,128)(2,1)S(1)}, u32[]{:S(2)}, u32[]{:S(2)}) collective-permute-start(bf16[32,1024]{1,0:T(8,128)(2,1)S(1)} %get-tuple-element.55), channel_id=1, source_target_pairs={{0,2},{1,3},{2,0},{3,1},{4,6},{5,7},{6,4},{7,5},{8,10},{9,11},{10,... | collective-permute-start | bytes 196616 | tf_op jit(solution)/shard_map/ppermute | solution.py:262
  42.0 6.1 %collective-permute-start.25 = (bf16[32,1024]{1,0:T(8,128)(2,1)S(1)}, bf16[32,1024]{1,0:T(8,128)(2,1)S(1)}, u32[]{:S(2)}, u32[]{:S(2)}) collective-permute-start(bf16[32,1024]{1,0:T(8,128)(2,1)S(1)} %get-tuple-element.56), channel_id=1, source_target_pairs={{0,3},{1,2},{2,1},{3,0},{4,7},{5,6},{6,5},{7,4},{8,11},{9,10},{10,... | collective-permute-start | bytes 196616 | tf_op jit(solution)/shard_map/ppermute | solution.py:262
  47.4 1.4 %collective-permute-start.22 = (bf16[4,128,128]{2,1,0:T(8,128)(2,1)S(1)}, bf16[4,128,128]{2,1,0:T(8,128)(2,1)S(1)}, u32[]{:S(2)}, u32[]{:S(2)}) collective-permute-start(bf16[4,128,128]{2,1,0:T(8,128)(2,1)S(1)} %get-tuple-element.52.refs_4_), channel_id=1, source_target_pairs={{0,4},{4,0},{8,12},{12,8},{16,20},{20,16},{24,28},{28,24},{1,5},{5... | collective-permute-start | bytes 393224 | tf_op jit(solution)/shard_map/ppermute | solution.py:250

commit v4 on v3

--- a/solution.py
+++ b/solution.py
@@ -38,7 +38,7 @@
 def causal_mask():
     t = lax.broadcasted_iota(jnp.int32, (BLOCK, BLOCK), 0)
     s = lax.broadcasted_iota(jnp.int32, (BLOCK, BLOCK), 1)
-    return t >= s
+    return t >= s, s >= t
 
 
 def place():
@@ -46,7 +46,7 @@
     return lax.rem(me, 2), lax.div(me, 2)
 
 
-def local_call(kernel, outs, *args, after=(), scratch=(), streamed=False, micros=0.0):
+def local_call(kernel, outs, *args, after=(), scratch=(), streamed=0, aliases=None, micros=0.0):
     vmem = pl.BlockSpec(memory_space=pltpu.VMEM)
     anywhere = pl.BlockSpec(memory_space=pl.ANY)
     count = len(args)
@@ -58,8 +58,9 @@
         body,
         out_shape=[jax.ShapeDtypeStruct(s, d) for s, d in outs],
         in_specs=[vmem] * count + [anywhere] * len(after),
-        out_specs=[anywhere if streamed else vmem] * len(outs),
+        out_specs=[anywhere] * streamed + [vmem] * (len(outs) - streamed),
         scratch_shapes=scratch,
+        input_output_aliases=aliases or {},
         compiler_params=pltpu.CompilerParams(vmem_limit_bytes=24 << 20),
         cost_estimate=pl.CostEstimate(
             flops=int(micros * 1e9), bytes_accessed=int(micros * 3.6e6), transcendentals=0
@@ -78,30 +79,26 @@
         psum_sent[j] = (own + other).astype(BF)
 
 
-def pack_kernel(first, second, both):
-    both[0], both[1] = first[...], second[...]
-
-
-def intra_kernel(qg_o, kv_o, qg_r, k_r, v_r, intra):
+def intra_kernel(q_o, kv_o, q_r, k_r, v_r, intra):
     par, _ = place()
-    mask = causal_mask()
+    mask, _ = causal_mask()
     kv_both = ((kv_o.at[0], kv_o.at[1]), (k_r, v_r))
-    for i, (qg, (k, v)) in enumerate(zip((qg_o, qg_r), kv_both)):
+    for i, (q, (k, v)) in enumerate(zip((q_o, q_r), kv_both)):
         for j in range(GROUPS):
             c = cols(2 * j + par)
-            scores = jnp.where(mask, nt(qg[0, :, c], k[:, c]), 0.0).astype(BF)
+            scores = jnp.where(mask, nt(q[:, c], k[:, c]), 0.0).astype(BF)
             intra[i, :, j * HEAD : (j + 1) * HEAD] = nn(scores, v[:, c])
 
 
 def attend_kernel(
-    att_scale, inv_root, qg_o, qg_r, intra, kvsel, kv_x, kv_y, kv_d,
+    att_scale, inv_root, q_o, q_r, g_o, g_r, intra, kvsel, kv_x, kv_y, kv_d,
     to_x, to_y, keep, forward, state_o, state_r,
 ):
     par, chip = place()
     later = par.astype(F32)
     x_later = lax.rem(chip, 2).astype(F32)
     y_later = lax.div(chip, 2).astype(F32)
-    half = qg_o.shape[2] // 2
+    half = g_o.shape[1] // 2
     for m in (3, 1, 2, 0):
         j = lax.bitwise_xor(chip, m)
         earlier = kv_x[j].astype(F32) * x_later
@@ -112,9 +109,9 @@
         state_o[j] = s_o
         state_r[j] = s_r
         c = cols(2 * j + par)
-        a_o = (att_scale * (intra[0, :, cols(j)] + nn(qg_o[0, :, c], s_o))).astype(BF)
-        a_r = (att_scale * (intra[1, :, cols(j)] + nn(qg_r[0, :, c], s_r))).astype(BF)
-        term = (tn(a_o, qg_o[1]) + tn(a_r, qg_r[1])) * inv_root
+        a_o = (att_scale * (intra[0, :, cols(j)] + nn(q_o[:, c], s_o))).astype(BF)
+        a_r = (att_scale * (intra[1, :, cols(j)] + nn(q_r[:, c], s_r))).astype(BF)
+        term = (tn(a_o, g_o[...]) + tn(a_r, g_r[...])) * inv_root
         first, second = term[:, :half], term[:, half:]
         if m == 3:
             to_x[1], to_y[1] = first.astype(BF), second.astype(BF)
@@ -159,49 +156,74 @@
         full[pl.ds(at, rows), :] = part[...]
 
 
-def head_grad(m, weights, qg_o, qg_r, ag_o, ag_r, qdsel, psum_sent):
+def head_grad(m, at, weights, q_o, q_r, g_o, g_r, ag_o, ag_r, qdsel, psum_sent):
     par, chip = place()
     later = par.astype(F32)
     j = lax.bitwise_xor(chip, m)
     c = cols(2 * j + par)
     a_o, a_r = (
-        jnp.concatenate([nt(qg[1], w[...]) for w in weights], axis=1).astype(BF)
-        for qg in (qg_o, qg_r)
-    )
-    ag_o[:, cols(j)] = a_o
-    ag_r[:, cols(j)] = a_r
-    own = tn(a_o, qg_o[0, :, c])
-    other = tn(a_r, qg_r[0, :, c])
+        jnp.concatenate([nt(g[...], w[...]) for w in weights], axis=1).astype(BF)
+        for g in (g_o, g_r)
+    )
+    ag_o[:, at * HEAD : (at + 1) * HEAD] = a_o
+    ag_r[:, at * HEAD : (at + 1) * HEAD] = a_r
+    own = tn(a_o, q_o[:, c])
+    other = tn(a_r, q_r[:, c])
     qdsel[j] = own * later + other * (1.0 - later)
     psum_sent[j] = (own + other).astype(BF)
 
 
-def near_grad_kernel(qg_o, qg_r, w_0, w_x, w_y, *outs):
+def near_grad_kernel(q_o, q_r, g_o, g_r, w_0, w_x, w_y, *outs):
     for m, weight in enumerate((w_0, w_x, w_y)):
-        head_grad(m, (weight,), qg_o, qg_r, *outs)
-
-
-def far_grad_kernel(qg_o, qg_r, w_d0, w_d1, *rest):
-    near, outs = rest[: len(rest) // 2], rest[len(rest) // 2 :]
-    for src, dst in zip(near, outs):
-        dst[...] = src[...]
-    head_grad(3, (w_d0, w_d1), qg_o, qg_r, *outs)
-
-
-def block_kernel(att_scale, qg_o, kv_o, ag_o, ag_p, st_o, st_p, dq, dk_in, dv_in):
-    par, _ = place()
-    mask = causal_mask()
-    for side, (ag, st) in enumerate(((ag_o, st_o), (ag_p, st_p))):
-        parity = par if side == 0 else 1 - par
-        for j in range(GROUPS):
-            c = cols(2 * j + parity)
-            q, k, v = qg_o[0, :, c], kv_o[0, :, c], kv_o[1, :, c]
-            a = ag[:, j * HEAD : (j + 1) * HEAD]
-            dscores = jnp.where(mask, nt(a, v), 0.0).astype(BF)
-            scores = jnp.where(mask, nt(q, k), 0.0).astype(BF)
-            dq[:, c] = (att_scale * (nn(dscores, k) + nt(a, st[j]))).astype(BF)
-            dk_in[:, c] = tn(dscores, q)
-            dv_in[:, c] = tn(scores, a)
+        head_grad(m, m, (weight,), q_o, q_r, g_o, g_r, *outs)
+
+
+def far_grad_kernel(
+    q_o, q_r, g_o, g_r, w_d0, w_d1, near_sel, near_sent, ag_o, ag_r, qdsel, psum_sent
+):
+    qdsel[...] = near_sel[...]
+    psum_sent[...] = near_sent[...]
+    head_grad(3, 0, (w_d0, w_d1), q_o, q_r, g_o, g_r, ag_o, ag_r, qdsel, psum_sent)
+
+
+def head_block(att_scale, q, k, v, a, state):
+    mask, mask_t = causal_mask()
+    dscores = jnp.where(mask, nt(a, v), 0.0).astype(BF)
+    dscores_t = jnp.where(mask_t, nt(v, a), 0.0).astype(BF)
+    scores_t = jnp.where(mask_t, nt(k, q), 0.0).astype(BF)
+    dq = (att_scale * (nn(dscores, k) + nt(a, state))).astype(BF)
+    return dq, nn(dscores_t, q), nn(scores_t, a)
+
+
+def near_block_kernel(att_scale, q_o, kv_o, near_o, st_o, dq, dk_in, dv_in):
+    par, chip = place()
+    for m in range(GROUPS - 1):
+        j = lax.bitwise_xor(chip, m)
+        c, at = cols(2 * j + par), slice(m * HEAD, (m + 1) * HEAD)
+        dq[:, at], dk_in[:, at], dv_in[:, at] = head_block(
+            att_scale, q_o[:, c], kv_o[0, :, c], kv_o[1, :, c], near_o[:, at], st_o[j]
+        )
+
+
+def block_kernel(
+    att_scale, q_o, kv_o, far_o, near_p, far_p, st_o, st_p, *rest
+):
+    done, outs = rest[:3], rest[3:]
+    par, chip = place()
+    for m in range(GROUPS - 1):
+        c = cols(2 * lax.bitwise_xor(chip, m) + par)
+        for src, dst in zip(done, outs):
+            dst[:, c] = src[:, m * HEAD : (m + 1) * HEAD]
+    heads = [(par, GROUPS - 1, far_o[...], st_o)]
+    for m in range(GROUPS):
+        a = near_p[:, m * HEAD : (m + 1) * HEAD] if m < GROUPS - 1 else far_p[...]
+        heads.append((1 - par, m, a, st_p))
+    for parity, m, a, st in heads:
+        j = lax.bitwise_xor(chip, m)
+        c = cols(2 * j + parity)
+        results = head_block(att_scale, q_o[:, c], kv_o[0, :, c], kv_o[1, :, c], a, st[j])
+        for dst, result in zip(outs, results):
+            dst[:, c] = result
 
 
 def carried_kernel(qdsel, qd_x, qd_y, qd_d, car_o, car_r):
@@ -217,23 +239,25 @@
         car_r[j] = (total + later * sel).astype(BF)
 
 
-def finish_kernel(
-    att_scale, kv_o, car_o, car_p, dk_in, dv_in, summed, dk, dv, weight_grad, dk_here, dv_here, sems
-):
+def finish_kernel(att_scale, other, kv_o, car, dk_in, dv_in, *refs):
+    before, (dk, dv, last, dk_here, dv_here, sems) = refs[:-6], refs[-6:]
     par, _ = place()
-    copies = [pltpu.make_async_copy(summed, weight_grad, sems.at[4 * GROUPS])]
-    copies[0].start()
-    for side, car in enumerate((car_o, car_p)):
-        parity = par if side == 0 else 1 - par
-        for j in range(GROUPS):
-            c = cols(2 * j + parity)
-            carried = car[j]
-            dk_here[:, c] = (att_scale * (dk_in[:, c] + nn(kv_o[1, :, c], carried))).astype(BF)
-            dv_here[:, c] = (att_scale * (dv_in[:, c] + nt(kv_o[0, :, c], carried))).astype(BF)
-            for here, out in ((dk_here, dk), (dv_here, dv)):
-                sem = sems.at[len(copies) - 1]
-                copies.append(pltpu.make_async_copy(here.at[:, c], out.at[:, c], sem))
-                copies[-1].start()
+    parity = 1 - par if other else par
+    copies = []
+    if other:
+        copies.append(pltpu.make_async_copy(before[0], last, sems.at[2 * GROUPS]))
+        copies[0].start()
+    else:
+        last[...] = jnp.zeros_like(last)
+    for j in range(GROUPS):
+        c, at = cols(2 * j + parity), slice(j * HEAD, (j + 1) * HEAD)
+        carried = car[j]
+        dk_here[:, at] = (att_scale * (dk_in[:, c] + nn(kv_o[1, :, c], carried))).astype(BF)
+        dv_here[:, at] = (att_scale * (dv_in[:, c] + nt(kv_o[0, :, c], carried))).astype(BF)
+        for here, out in ((dk_here, dk), (dv_here, dv)):
+            sem = sems.at[len(copies) - other]
+            copies.append(pltpu.make_async_copy(here.at[:, at], out.at[:, c], sem))
+            copies[-1].start()
     for copy in copies:
         copy.wait()
 
@@ -264,26 +288,24 @@
     state = (GROUPS, HEAD, HEAD)
     half = width // 2
     rows = HEAD // n_dp
-    k_r, v_r = core(key_vecs[0]), core(value_vecs[0])
+    q_o, k_o, v_o, g_o = queries[0], key_vecs[0], value_vecs[0], out_grad[0]
+    k_r, v_r, q_r, g_r = core(k_o), core(v_o), core(q_o), core(g_o)
     kv_o = jnp.concatenate([key_vecs, value_vecs])
     w_parts = [along_dp(out_weight, m) for m in range(1, n_dp)]
     kvsel, kv_sent = local_call(
         kv_kernel,
         [(state, F32), (state, BF)],
         kv_o, k_r, v_r,
-    )
-    (qg_o,) = local_call(
-        pack_kernel, [((2, BLOCK, width), BF)], queries[0], out_grad[0], after=(kv_sent,)
+        after=(q_r, g_r),
     )
     kv_x, kv_y, kv_d = over_x(kv_sent), over_y(kv_sent), over_both(kv_sent)
-    qg_r = core(qg_o)
     (w_0,) = local_call(
         functools.partial(order_kernel, n_dp),
-        [((HEAD, width), BF)], out_weight, *w_parts, after=(qg_o,), micros=20,
+        [((HEAD, width), BF)], out_weight, *w_parts, after=(kv_sent,), micros=20,
     )
     (intra,) = local_call(
         intra_kernel,
-        [((2, BLOCK, half), F32)], qg_o, kv_o, qg_r, k_r, v_r, after=(w_0,),
+        [((2, BLOCK, half), F32)], q_o, kv_o, q_r, k_r, v_r, after=(w_0,),
     )
     w_x, w_y = over_x(w_0), over_y(w_0)
     w_d0, w_d1 = over_y(w_x[: HEAD // 2]), over_x(w_y[HEAD // 2 :])
@@ -297,56 +319,81 @@
             (state, BF),
             (state, BF),
         ],
-        qg_o, qg_r, intra, kvsel, kv_x, kv_y, kv_d,
+        q_o, q_r, g_o, g_r, intra, kvsel, kv_x, kv_y, kv_d,
     )
     from_x, from_y = over_x(to_x), over_y(to_y)
     state_p = core(state_r)
-    grads = [((BLOCK, half), BF), ((BLOCK, half), BF), (state, F32), (state, BF)]
-    near = local_call(near_grad_kernel, grads, qg_o, qg_r, w_0, w_x, w_y, after=(to_x,))
+    sums = [(state, F32), (state, BF)]
+    near_o, near_r, near_sel, near_sent = local_call(
+        near_grad_kernel,
+        [((BLOCK, half - HEAD), BF)] * 2 + sums,
+        q_o, q_r, g_o, g_r, w_0, w_x, w_y,
+        after=(state_p,),
+    )
+    near_p = core(near_r)
+    near_done = local_call(
+        functools.partial(near_block_kernel, att_scale),
+        [((BLOCK, half - HEAD), kind) for kind in (BF, F32, F32)],
+        q_o, kv_o, near_o, state_o,
+    )
     (pass_y,) = local_call(
         functools.partial(forward_kernel, 0), [((HEAD, half), BF)], forward, from_x,
-        after=(near[3],),
+        after=(near_done[0],),
     )
     (pass_x,) = local_call(
         functools.partial(forward_kernel, 1), [((HEAD, half), BF)], forward, from_y,
         after=(pass_y,),
     )
     last_y, last_x = over_y(pass_y), over_x(pass_x)
-    ag_o, ag_r, qdsel, qd_sent = local_call(
-        far_grad_kernel, grads, qg_o, qg_r, w_d0, w_d1, *near, after=(pass_x,)
+    far_o, far_r, qdsel, qd_sent = local_call(
+        far_grad_kernel,
+        [((BLOCK, HEAD), BF)] * 2 + sums,
+        q_o, q_r, g_o, g_r, w_d0, w_d1, near_sel, near_sent,
+        after=(pass_x,),
     )
     qd_x, qd_y, qd_d = over_x(qd_sent), over_y(qd_sent), over_both(qd_sent)
-    ag_p = core(ag_r)
+    far_p = core(far_r)
     own, *send = local_call(
         functools.partial(fold_kernel, n_dp),
         [((rows, width), F32)] + [((rows, width), BF)] * (n_dp - 1),
         keep, from_x, from_y, last_y, last_x,
-        after=(qd_sent,), micros=20,
+        after=(far_p, near_p), micros=20,
     )
     got = [along_dp(send[m - 1], m) for m in range(1, n_dp)]
     dq, dk_in, dv_in = local_call(
         functools.partial(block_kernel, att_scale),
         [((BLOCK, width), BF), ((BLOCK, width), F32), ((BLOCK, width), F32)],
-        qg_o, kv_o, ag_o, ag_p, state_o, state_p,
+        q_o, kv_o, far_o, near_p, far_p, state_o, state_p, *near_done,
         after=(send[0],),
     )
     car_o, car_r = local_call(
         carried_kernel, [(state, BF), (state, BF)], qdsel, qd_x, qd_y, qd_d, after=(dk_in,)
     )
     car_p = core(car_r)
+    grads = [((BLOCK, width), BF), ((BLOCK, width), BF)]
+    streams = [
+        pltpu.VMEM((BLOCK, half), BF),
+        pltpu.VMEM((BLOCK, half), BF),
+        pltpu.SemaphoreType.DMA((2 * GROUPS + 1,)),
+    ]
+    dk, dv, ended = local_call(
+        functools.partial(finish_kernel, att_scale, 0),
+        grads + [((8, HEAD), F32)],
+        kv_o, car_o, dk_in, dv_in,
+        streamed=2,
+        scratch=streams,
+    )
     (summed,) = local_call(
-        sum_kernel, [((rows, width), F32)], own, *got, after=(car_r,), micros=20
+        sum_kernel, [((rows, width), F32)], own, *got, after=(ended,), micros=20
     )
     dk, dv, weight_grad = local_call(
-        functools.partial(finish_kernel, att_scale),
-        [((BLOCK, width), BF), ((BLOCK, width), BF), ((rows, width), F32)],
-        kv_o, car_o, car_p, dk_in, dv_in, summed,
-        streamed=True,
-        scratch=[
-            pltpu.VMEM((BLOCK, width), BF),
-            pltpu.VMEM((BLOCK, width), BF),
-            pltpu.SemaphoreType.DMA((4 * GROUPS + 1,)),
-        ],
+        functools.partial(finish_kernel, att_scale, 1),
+        grads + [((rows, width), F32)],
+        kv_o, car_p, dk_in, dv_in, summed,
+        after=(dk, dv),
+        aliases={5: 0, 6: 1},
+        streamed=3,
+        scratch=streams,
     )
     return dq[None], dk[None], dv[None], weight_grad
 

time: 50.3 us -> 47.7 us (0.948)
  waiting for transfers between devices: 9.8 us -> 6.53 us
    ppermute x6, waiting for transfers between devices: 4.82 us -> 2.53 us  [over_x(): return lax.ppermute(x, 'ctx', along(2))]
    ppermute x6, starting transfers between devices: 7.95 us -> 5.68 us  [over_y(): return lax.ppermute(x, 'ctx', along(4))]
    ppermute x2, starting transfers between devices: 1.81 us -> 4.06 us  [over_both(): return lax.ppermute(x, 'ctx', along(6))]
    ppermute x6, waiting for transfers between devices: 1.67 us -> 2.87 us  [along_dp(): return lax.ppermute(x, 'dp', [(i, i ^ m) for i in range(n_dp)])]
    ppermute x2, waiting for transfers between devices: 1.47 us -> 0.3 us  [over_both(): return lax.ppermute(x, 'ctx', along(6))]
    ppermute x6 -> x8, waiting for transfers between devices: 0.7 us -> 0.02 us  [core(): return lax.ppermute(x, 'ctx', along(1))]
    ppermute x6 -> x8, starting transfers between devices: 0.68 us -> 1.32 us  [core(): return lax.ppermute(x, 'ctx', along(1))]
    pallas_call x14 -> x15, Pallas kernels: 10.7 us -> 11.1 us  [local_call(): pl.pallas_call(body, out_shape=[jax.ShapeDtypeStruct(s, d) for s, d in ou...]
  transfers between devices with their start and end apart: 26 -> 28, of which waited for: 9 -> 8; matrix products, arithmetic and copies ran while one was open for 2% -> 2% of each run, Pallas kernels for 18% -> 21%
where the time goes in v4:
time: 47.7 us; the launch traced here: 47.5 us
  starting transfers between devices  27.8 us (58%)
  Pallas kernels  11.1 us (23%)
  waiting for transfers between devices  6.53 us (14%)
  local copies, waits for them, and re-layouts  1.15 us (2%)
  between operations  0.85 us (2%)
    pallas_call x15, Pallas kernels, local_call(): pl.pallas_call(body, out_shape=[jax.ShapeDtypeStruct(s, d) for s, d in ou...  11.1 us
    ppermute x6, starting transfers between devices, along_dp(): return lax.ppermute(x, 'dp', [(i, i ^ m) for i in range(n_dp)])  9.46 us
    ppermute x6, starting transfers between devices, over_x(): return lax.ppermute(x, 'ctx', along(2))  7.32 us
    ppermute x6, starting transfers between devices, over_y(): return lax.ppermute(x, 'ctx', along(4))  5.68 us
    ppermute x2, starting transfers between devices, over_both(): return lax.ppermute(x, 'ctx', along(6))  4.06 us
    ppermute x6, waiting for transfers between devices, along_dp(): return lax.ppermute(x, 'dp', [(i, i ^ m) for i in range(n_dp)])  2.87 us
    ppermute x6, waiting for transfers between devices, over_x(): return lax.ppermute(x, 'ctx', along(2))  2.53 us
    ppermute x8, starting transfers between devices, core(): return lax.ppermute(x, 'ctx', along(1))  1.32 us
  transfers between devices with their start and end apart: 28, of which 8 were waited for; matrix products, arithmetic and copies ran while one was open for 2% of the time, Pallas kernels for 21%

profile of v4, /device:TPU:0, one launch (start us, length us, event | category | flops | bytes accessed | tf_op | source)
XLA Modules:
  0.0 47.5 jit_solution(15367489518168310349)
XLA Ops:
  0.6 0.5 %collective-permute-start = (bf16[256,1024]{1,0:T(8,128)(2,1)}, bf16[256,1024]{1,0:T(8,128)(2,1)S(1)}, u32[]{:S(2)}, u32[]{:S(2)}) collective-permute-start(bf16[256,1024]{1,0:T(8,128)(2,1)} %bitcast.7), channel_id=1, source_target_pairs={{0,4},{4,0},{8,12},{12,8},{16,20},{20,16},{24,28},{28,24},{1,5},{5... | collective-permute-start | bytes 1572872 | tf_op jit(solution)/shard_map/ppermute | solution.py:274
  1.1 0.1 collective-permute-start.1
  1.2 0.4 collective-permute-start.6
  1.7 0.1 collective-permute-start.5
  1.7 4.0 %collective-permute-start.3 = (bf16[32,1024]{1,0:T(8,128)(2,1)}, bf16[32,1024]{1,0:T(8,128)(2,1)S(1)}, u32[]{:S(2)}, u32[]{:S(2)}) collective-permute-start(bf16[32,1024]{1,0:T(8,128)(2,1)} %refs_0_.1), channel_id=1, source_target_pairs={{0,2},{1,3},{2,0},{3,1},{4,6},{5,7},{6,4},{7,5},{8,10},{9,11},{10,... | collective-permute-start | bytes 196616 | tf_op jit(solution)/shard_map/ppermute | solution.py:286
  5.8 1.1 %constant_dynamic-update-slice_fusion.1 = bf16[2,256,1024]{2,1,0:T(8,128)(2,1)S(1)} fusion(bf16[1,256,1024]{2,1,0:T(8,128)(2,1)} %param.6), kind=kLoop, calls=%fused_computation.1 | loop fusion | bytes 1048576
  6.8 0.0 collective-permute-done.refs_3_.refs_2_.refs_1_
  6.9 1.6 %collective-permute-start.2 = (bf16[32,1024]{1,0:T(8,128)(2,1)S(1)}, bf16[32,1024]{1,0:T(8,128)(2,1)S(1)}, u32[]{:S(2)}, u32[]{:S(2)}) collective-permute-start(bf16[32,1024]{1,0:T(8,128)(2,1)S(1)} %copy-done.2), channel_id=1, source_target_pairs={{0,1},{1,0},{2,3},{3,2},{4,5},{5,4},{6,7},{7,6},{8,9},{9,8},{10,11... | collective-permute-start | bytes 196616 | tf_op jit(solution)/shard_map/ppermute | solution.py:286
  8.5 0.0 collective-permute-done.1.refs_4_.refs_3_
  8.5 0.1 collective-permute-start.4
  8.7 0.0 collective-permute-done.6.refs_2_.refs_4_
  8.7 0.0 collective-permute-done.5.refs_1_.refs_3_
  8.7 0.5 %shard_map.84 = (f32[4,128,128]{2,1,0:T(8,128)S(1)}, bf16[4,128,128]{2,1,0:T(8,128)(2,1)S(1)}) custom-call(bf16[2,256,1024]{2,1,0:T(8,128)(2,1)S(1)} %constant_dynamic-update-slice_fusion.refs_0_.refs_1_, bf16[256,1024]{1,0:T(8,128)(2,1)S(1)} %collective-permute-done.5.refs_1_.refs_3_, bf16[256,1024]{1,0:T(8,128)(2,1)S(1)} %collective-permute-done.6.refs_2_.refs_4_, ...), custom_call_target="tpu_custom_call" | custom-call | tf_op jit(solution)/shard_map/pallas_call | solution.py:57
  9.2 0.0 copy-start
  9.2 2.6 %collective-permute-start.13 = (bf16[4,128,128]{2,1,0:T(8,128)(2,1)S(1)}, bf16[4,128,128]{2,1,0:T(8,128)(2,1)S(1)}, u32[]{:S(2)}, u32[]{:S(2)}) collective-permute-start(bf16[4,128,128]{2,1,0:T(8,128)(2,1)S(1)} %get-tuple-element.38.refs_4_), channel_id=1, source_target_pairs={{0,24},{4,28},{8,16},{12,20},{16,8},{20,12},{24,0},{28,4},{1,25},{... | collective-permute-start | bytes 393224 | tf_op jit(solution)/shard_map/ppermute | solution.py:283
  11.8 0.5 %collective-permute-start.12 = (bf16[4,128,128]{2,1,0:T(8,128)(2,1)S(1)}, bf16[4,128,128]{2,1,0:T(8,128)(2,1)S(1)}, u32[]{:S(2)}, u32[]{:S(2)}) collective-permute-start(bf16[4,128,128]{2,1,0:T(8,128)(2,1)S(1)} %get-tuple-element.38.refs_4_), channel_id=1, source_target_pairs={{0,16},{4,20},{8,24},{12,28},{16,0},{20,4},{24,8},{28,12},{1,17},{... | collective-permute-start | bytes 393224 | tf_op jit(solution)/shard_map/ppermute | solution.py:280
  12.3 0.4 collective-permute-start.11
  12.8 0.0 collective-permute-done.2.refs_1_
  12.8 1.8 %collective-permute-done.4.refs_3_ = bf16[32,1024]{1,0:T(8,128)(2,1)S(1)} collective-permute-done((bf16[32,1024]{1,0:T(8,128)(2,1)S(1)}, bf16[32,1024]{1,0:T(8,128)(2,1)S(1)}, u32[]{:S(2)}, u32[]{:S(2)}) %collective-permute-start.4) | collective-permute-done | bytes 65568 | tf_op jit(solution)/shard_map/ppermute | solution.py:286
  14.6 0.0 copy-start.1
  14.6 1.6 %collective-permute-start.9 = (bf16[128,1024]{1,0:T(8,128)(2,1)S(1)}, bf16[128,1024]{1,0:T(8,128)(2,1)S(1)}, u32[]{:S(2)}, u32[]{:S(2)}) collective-permute-start(bf16[128,1024]{1,0:T(8,128)(2,1)S(1)} %shard_map.85.refs_5_.refs_4_), channel_id=1, source_target_pairs={{0,16},{4,20},{8,24},{12,28},{16,0},{20,4},{24,8},{28,12},{1,17},{... | collective-permute-start | bytes 786440 | tf_op jit(solution)/shard_map/ppermute | solution.py:280
  16.2 1.5 %collective-permute-start.7 = (bf16[128,1024]{1,0:T(8,128)(2,1)S(1)}, bf16[128,1024]{1,0:T(8,128)(2,1)S(1)}, u32[]{:S(2)}, u32[]{:S(2)}) collective-permute-start(bf16[128,1024]{1,0:T(8,128)(2,1)S(1)} %shard_map.85.refs_5_.refs_4_), channel_id=1, source_target_pairs={{0,8},{4,12},{8,0},{12,4},{16,24},{20,28},{24,16},{28,20},{1,9},{5... | collective-permute-start | bytes 786440 | tf_op jit(solution)/shard_map/ppermute | solution.py:277
  17.7 0.9 %shard_map.86.refs_4_ = f32[2,256,512]{2,1,0:T(8,128)S(1)} custom-call(bf16[256,1024]{1,0:T(8,128)(2,1)S(1)} %bitcast.8, bf16[2,256,1024]{2,1,0:T(8,128)(2,1)S(1)} %constant_dynamic-update-slice_fusion.refs_0_.refs_1_, bf16[256,1024]{1,0:T(8,128)(2,1)S(1)} %collective-permute-done.refs_3_.refs_2_.refs_1_, ...), custom_call_target="tpu_custom_call" | custom-call | tf_op jit(solution)/shard_map/pallas_call | solution.py:57
  18.6 0.0 collective-permute-done.12.refs_7_
  18.6 0.9 %collective-permute-done.11.refs_6_ = bf16[4,128,128]{2,1,0:T(8,128)(2,1)S(1)} collective-permute-done((bf16[4,128,128]{2,1,0:T(8,128)(2,1)S(1)}, bf16[4,128,128]{2,1,0:T(8,128)(2,1)S(1)}, u32[]{:S(2)}, u32[]{:S(2)}) %collective-permute-start.11) | collective-permute-done | bytes 131104 | tf_op jit(solution)/shard_map/ppermute | solution.py:277
  19.5 1.6 %shard_map.87 = (bf16[2,128,512]{2,1,0:T(8,128)(2,1)S(1)}, bf16[2,128,512]{2,1,0:T(8,128)(2,1)S(1)}, f32[128,1024]{1,0:T(8,128)S(1)}, f32[2,128,512]{2,1,0:T(8,1...) custom-call(bf16[256,1024]{1,0:T(8,128)(2,1)S(1)} %bitcast.9, ...), custom_call_target="tpu_custom_call" | custom-call | tf_op jit(solution)/shard_map/pallas_call | solution.py:57
  21.1 1.6 %collective-permute-start.16 = (bf16[2,128,512]{2,1,0:T(8,128)(2,1)S(1)}, bf16[2,128,512]{2,1,0:T(8,128)(2,1)S(1)}, u32[]{:S(2)}, u32[]{:S(2)}) collective-permute-start(bf16[2,128,512]{2,1,0:T(8,128)(2,1)S(1)} %get-tuple-element.45), channel_id=1, source_target_pairs={{0,8},{4,12},{8,0},{12,4},{16,24},{20,28},{24,16},{28,20},{1,9},{5... | collective-permute-start | bytes 786440 | tf_op jit(solution)/shard_map/ppermute | solution.py:277
  22.7 0.5 %collective-permute-start.15 = (bf16[2,128,512]{2,1,0:T(8,128)(2,1)S(1)}, bf16[2,128,512]{2,1,0:T(8,128)(2,1)S(1)}, u32[]{:S(2)}, u32[]{:S(2)}) collective-permute-start(bf16[2,128,512]{2,1,0:T(8,128)(2,1)S(1)} %get-tuple-element.44), channel_id=1, source_target_pairs={{0,16},{4,20},{8,24},{12,28},{16,0},{20,4},{24,8},{28,12},{1,17},{... | collective-permute-start | bytes 786440 | tf_op jit(solution)/shard_map/ppermute | solution.py:280
  23.2 0.0 collective-permute-start.14
  23.2 0.8 %collective-permute-done.9.refs_6_ = bf16[128,1024]{1,0:T(8,128)(2,1)S(1)} collective-permute-done((bf16[128,1024]{1,0:T(8,128)(2,1)S(1)}, bf16[128,1024]{1,0:T(8,128)(2,1)S(1)}, u32[]{:S(2)}, u32[]{:S(2)}) %collective-permute-start.9) | collective-permute-done | bytes 262176 | tf_op jit(solution)/shard_map/ppermute | solution.py:280
  24.0 1.5 %collective-permute-start.10 = (bf16[64,1024]{1,0:T(8,128)(2,1)S(1)}, bf16[64,1024]{1,0:T(8,128)(2,1)S(1)}, u32[]{:S(2)}, u32[]{:S(2)}) collective-permute-start(bf16[64,1024]{1,0:T(8,128)(2,1)S(1)} %slice.9), channel_id=1, source_target_pairs={{0,8},{4,12},{8,0},{12,4},{16,24},{20,28},{24,16},{28,20},{1,9},{5... | collective-permute-start | bytes 393224 | tf_op jit(solution)/shard_map/ppermute | solution.py:277
  25.6 1.1 %collective-permute-start.8 = (bf16[64,1024]{1,0:T(8,128)(2,1)S(1)}, bf16[64,1024]{1,0:T(8,128)(2,1)S(1)}, u32[]{:S(2)}, u32[]{:S(2)}) collective-permute-start(bf16[64,1024]{1,0:T(8,128)(2,1)S(1)} %slice.8), channel_id=1, source_target_pairs={{0,16},{4,20},{8,24},{12,28},{16,0},{20,4},{24,8},{28,12},{1,17},{... | collective-permute-start | bytes 393224 | tf_op jit(solution)/shard_map/ppermute | solution.py:280
  26.6 1.6 %shard_map.88 = (bf16[256,384]{1,0:T(8,128)(2,1)S(1)}, bf16[256,384]{1,0:T(8,128)(2,1)S(1)}, f32[4,128,128]{2,1,0:T(8,128)S(1)}, bf16[4,128,128]{2,1,0:T(8,128)(2,1)S(1)}) custom-call(bf16[256,1024]{1,0:T(8,128)(2,1)S(1)} %bitcast.10, bf16[256,1024]{1,0:T(8,128)(2,1)S(1)} %collective-permute-done.refs_3_.refs_2_.refs_1_, bf16[256,1024]{1,0:T(8,128)(2,1)S(1)} %bitcast.16, ...), custom_call_target="tpu_custom_call" | custom-call | tf_op jit(solution)/shard_map/pallas_call | solution.py:57
  28.3 0.1 collective-permute-start.17
  28.4 0.9 %shard_map.89 = (bf16[256,384]{1,0:T(8,128)(2,1)S(1)}, f32[256,384]{1,0:T(8,128)S(1)}, f32[256,384]{1,0:T(8,128)S(1)}) custom-call(bf16[256,1024]{1,0:T(8,128)(2,1)S(1)} %bitcast.11, bf16[2,256,1024]{2,1,0:T(8,128)(2,1)S(1)} %constant_dynamic-update-slice_fusion.refs_0_.refs_1_, bf16[256,384]{1,0:T(8,128)(2,1)S(1)} %get-tuple-element.46.refs_2_, ...), custom_call_target="tpu_custom_call" | custom-call | tf_op jit(solution)/shard_map/pallas_call | solution.py:57
  29.3 1.6 %collective-permute-done.16.refs_1_ = bf16[2,128,512]{2,1,0:T(8,128)(2,1)S(1)} collective-permute-done((bf16[2,128,512]{2,1,0:T(8,128)(2,1)S(1)}, bf16[2,128,512]{2,1,0:T(8,128)(2,1)S(1)}, u32[]{:S(2)}, u32[]{:S(2)}) %collective-permute-start.16) | collective-permute-done | bytes 262176 | tf_op jit(solution)/shard_map/ppermute | solution.py:277
  31.0 1.6 %collective-permute-start.20 = (bf16[128,512]{1,0:T(8,128)(2,1)S(1)}, bf16[128,512]{1,0:T(8,128)(2,1)S(1)}, u32[]{:S(2)}, u32[]{:S(2)}) collective-permute-start(bf16[128,512]{1,0:T(8,128)(2,1)S(1)} %shard_map.91.refs_8_), channel_id=1, source_target_pairs={{0,8},{4,12},{8,0},{12,4},{16,24},{20,28},{24,16},{28,20},{1,9},{5... | collective-permute-start | bytes 393224 | tf_op jit(solution)/shard_map/ppermute | solution.py:277
  32.6 0.6 %collective-permute-start.19 = (bf16[128,512]{1,0:T(8,128)(2,1)S(1)}, bf16[128,512]{1,0:T(8,128)(2,1)S(1)}, u32[]{:S(2)}, u32[]{:S(2)}) collective-permute-start(bf16[128,512]{1,0:T(8,128)(2,1)S(1)} %shard_map.90.refs_2_), channel_id=1, source_target_pairs={{0,16},{4,20},{8,24},{12,28},{16,0},{20,4},{24,8},{28,12},{1,17},{... | collective-permute-start | bytes 393224 | tf_op jit(solution)/shard_map/ppermute | solution.py:280
  33.2 0.0 collective-permute-done.10.refs_5_
  33.2 0.0 collective-permute-done.8.refs_4_
  33.2 1.0 %shard_map.92 = (bf16[256,128]{1,0:T(8,128)(2,1)S(1)}, bf16[256,128]{1,0:T(8,128)(2,1)S(1)}, f32[4,128,128]{2,1,0:T(8,128)S(1)}, bf16[4,128,128]{2,1,0:T(8,128)(2,1)S(1)}) custom-call(bf16[256,1024]{1,0:T(8,128)(2,1)S(1)} %bitcast.12, bf16[256,1024]{1,0:T(8,128)(2,1)S(1)} %collective-permute-done.refs_3_.refs_2_.refs_1_, bf16[256,1024]{1,0:T(8,128)(2,1)S(1)} %bitcast.17, ...), custom_call_target="tpu_custom_call" | custom-call | tf_op jit(solution)/shard_map/pallas_call | solution.py:57
  34.1 0.1 collective-permute-start.18
  34.2 1.4 %collective-permute-start.23 = (bf16[4,128,128]{2,1,0:T(8,128)(2,1)S(1)}, bf16[4,128,128]{2,1,0:T(8,128)(2,1)S(1)}, u32[]{:S(2)}, u32[]{:S(2)}) collective-permute-start(bf16[4,128,128]{2,1,0:T(8,128)(2,1)S(1)} %get-tuple-element.58), channel_id=1, source_target_pairs={{0,24},{4,28},{8,16},{12,20},{16,8},{20,12},{24,0},{28,4},{1,25},{... | collective-permute-start | bytes 393224 | tf_op jit(solution)/shard_map/ppermute | solution.py:283
  35.6 0.0 collective-permute-done.17.refs_6_.refs_3_
  35.6 1.4 %collective-permute-start.22 = (bf16[4,128,128]{2,1,0:T(8,128)(2,1)S(1)}, bf16[4,128,128]{2,1,0:T(8,128)(2,1)S(1)}, u32[]{:S(2)}, u32[]{:S(2)}) collective-permute-start(bf16[4,128,128]{2,1,0:T(8,128)(2,1)S(1)} %get-tuple-element.58), channel_id=1, source_target_pairs={{0,16},{4,20},{8,24},{12,28},{16,0},{20,4},{24,8},{28,12},{1,17},{... | collective-permute-start | bytes 393224 | tf_op jit(solution)/shard_map/ppermute | solution.py:280
  37.1 0.7 %collective-permute-start.21 = (bf16[4,128,128]{2,1,0:T(8,128)(2,1)S(1)}, bf16[4,128,128]{2,1,0:T(8,128)(2,1)S(1)}, u32[]{:S(2)}, u32[]{:S(2)}) collective-permute-start(bf16[4,128,128]{2,1,0:T(8,128)(2,1)S(1)} %get-tuple-element.58), channel_id=1, source_target_pairs={{0,8},{4,12},{8,0},{12,4},{16,24},{20,28},{24,16},{28,20},{1,9},{5... | collective-permute-start | bytes 393224 | tf_op jit(solution)/shard_map/ppermute | solution.py:277
  37.8 0.0 collective-permute-done.20.refs_4_
  37.8 0.0 collective-permute-done.19.refs_3_
  37.8 0.1 shard_map.93
  37.9 1.4 %collective-permute-start.26 = (bf16[32,1024]{1,0:T(8,128)(2,1)S(1)}, bf16[32,1024]{1,0:T(8,128)(2,1)S(1)}, u32[]{:S(2)}, u32[]{:S(2)}) collective-permute-start(bf16[32,1024]{1,0:T(8,128)(2,1)S(1)} %get-tuple-element.63), channel_id=1, source_target_pairs={{0,2},{1,3},{2,0},{3,1},{4,6},{5,7},{6,4},{7,5},{8,10},{9,11},{10,... | collective-permute-start | bytes 196616 | tf_op jit(solution)/shard_map/ppermute | solution.py:286
  39.2 2.0 %collective-permute-start.27 = (bf16[32,1024]{1,0:T(8,128)(2,1)S(1)}, bf16[32,1024]{1,0:T(8,128)(2,1)S(1)}, u32[]{:S(2)}, u32[]{:S(2)}) collective-permute-start(bf16[32,1024]{1,0:T(8,128)(2,1)S(1)} %get-tuple-element.64), channel_id=1, source_target_pairs={{0,3},{1,2},{2,1},{3,0},{4,7},{5,6},{6,5},{7,4},{8,11},{9,10},{10,... | collective-permute-start | bytes 196616 | tf_op jit(solution)/shard_map/ppermute | solution.py:286
  41.2 0.3 collective-permute-done.23.refs_3_
  41.5 0.3 collective-permute-start.25
  41.9 2.2 %shard_map.94 = (bf16[256,1024]{1,0:T(8,128)(2,1)}, f32[256,1024]{1,0:T(8,128)S(1)}, f32[256,1024]{1,0:T(8,128)S(1)}) custom-call(bf16[256,1024]{1,0:T(8,128)(2,1)S(1)} %bitcast.13, bf16[2,256,1024]{2,1,0:T(8,128)(2,1)S(1)} %constant_dynamic-update-slice_fusion.refs_0_.refs_1_, bf16[256,128]{1,0:T(8,128)(2,1)S(1)} %get-tuple-element.49.refs_2_, ...), custom_call_target="tpu_custom_call" | custom-call | tf_op jit(solution)/shard_map/pallas_call | solution.py:57
  44.1 0.0 collective-permute-done.22.refs_2_
  44.1 0.0 collective-permute-done.21.refs_1_
  44.1 0.1 shard_map.95
  44.2 0.1 collective-permute-start.24
  44.3 1.1 %shard_map.96 = (bf16[256,1024]{1,0:T(8,128)(2,1)}, bf16[256,1024]{1,0:T(8,128)(2,1)}, f32[8,128]{1,0:T(8,128)S(1)}) custom-call(bf16[2,256,1024]{2,1,0:T(8,128)(2,1)S(1)} %constant_dynamic-update-slice_fusion.refs_0_.refs_1_, bf16[4,128,128]{2,1,0:T(8,128)(2,1)S(1)} %get-tuple-element.65.refs_1_, f32[256,1024]{1,0:T(8,128)S(1)} %get-tuple-element.59.refs_4_.refs_2_, ...), custom_call_target="tpu_custom_call" | custom-call | tf_op jit(solution)/shard_map/pallas_call | solution.py:57
  45.3 0.2 collective-permute-done.26.refs_2_
  45.6 0.2 collective-permute-done.27.refs_3_
  45.8 0.6 %collective-permute-done.25.refs_1_ = bf16[32,1024]{1,0:T(8,128)(2,1)S(1)} collective-permute-done((bf16[32,1024]{1,0:T(8,128)(2,1)S(1)}, bf16[32,1024]{1,0:T(8,128)(2,1)S(1)}, u32[]{:S(2)}, u32[]{:S(2)}) %collective-permute-start.25) | collective-permute-done | bytes 65568 | tf_op jit(solution)/shard_map/ppermute | solution.py:286
  46.4 0.0 collective-permute-done.24.refs_1_
  46.4 1.1 %shard_map.98 = (bf16[256,1024]{1,0:T(8,128)(2,1)}, bf16[256,1024]{1,0:T(8,128)(2,1)}, f32[32,1024]{1,0:T(8,128)}) custom-call(bf16[2,256,1024]{2,1,0:T(8,128)(2,1)S(1)} %constant_dynamic-update-slice_fusion.refs_0_.refs_1_, bf16[4,128,128]{2,1,0:T(8,128)(2,1)S(1)} %collective-permute-done.24.refs_1_, ...), custom_call_target="tpu_custom_call", output_to_operand_aliasing={{0}: (5, {}), {1}: (6, {})} | custom-call | tf_op jit(solution)/shard_map/pallas_call | solution.py:57
  (19 shorter events, 0.2 us)
Async XLA Ops:
  0.6 6.2 %collective-permute-start = (bf16[256,1024]{1,0:T(8,128)(2,1)}, bf16[256,1024]{1,0:T(8,128)(2,1)S(1)}, u32[]{:S(2)}, u32[]{:S(2)}) collective-permute-start(bf16[256,1024]{1,0:T(8,128)(2,1)} %bitcast.7), channel_id=1, source_target_pairs={{0,4},{4,0},{8,12},{12,8},{16,20},{20,16},{24,28},{28,24},{1,5},{5... | collective-permute-start | bytes 1572872 | tf_op jit(solution)/shard_map/ppermute | solution.py:274
  1.1 7.4 %collective-permute-start.1 = (bf16[256,1024]{1,0:T(8,128)(2,1)}, bf16[256,1024]{1,0:T(8,128)(2,1)S(1)}, u32[]{:S(2)}, u32[]{:S(2)}) collective-permute-start(bf16[256,1024]{1,0:T(8,128)(2,1)} %bitcast.14), channel_id=1, source_target_pairs={{0,4},{4,0},{8,12},{12,8},{16,20},{20,16},{24,28},{28,24},{1,5},{5... | collective-permute-start | bytes 1572872 | tf_op jit(solution)/shard_map/ppermute | solution.py:274
  1.2 7.4 %collective-permute-start.6 = (bf16[256,1024]{1,0:T(8,128)(2,1)}, bf16[256,1024]{1,0:T(8,128)(2,1)S(1)}, u32[]{:S(2)}, u32[]{:S(2)}) collective-permute-start(bf16[256,1024]{1,0:T(8,128)(2,1)} %bitcast.20), channel_id=1, source_target_pairs={{0,4},{4,0},{8,12},{12,8},{16,20},{20,16},{24,28},{28,24},{1,5},{5... | collective-permute-start | bytes 1572872 | tf_op jit(solution)/shard_map/ppermute | solution.py:274
  1.7 5.2 %copy-start.2 = (bf16[32,1024]{1,0:T(8,128)(2,1)S(1)}, bf16[32,1024]{1,0:T(8,128)(2,1)}, u32[]{:S(2)}) copy-start(bf16[32,1024]{1,0:T(8,128)(2,1)} %refs_0_.1) | copy-start | bytes 196612
  1.7 7.0 %copy-start.3 = (bf16[1,256,1024]{2,1,0:T(8,128)(2,1)S(1)}, bf16[1,256,1024]{2,1,0:T(8,128)(2,1)}, u32[]{:S(2)}) copy-start(bf16[1,256,1024]{2,1,0:T(8,128)(2,1)} %param.7) | copy-start | bytes 1572868
  1.7 7.0 %collective-permute-start.5 = (bf16[256,1024]{1,0:T(8,128)(2,1)}, bf16[256,1024]{1,0:T(8,128)(2,1)S(1)}, u32[]{:S(2)}, u32[]{:S(2)}) collective-permute-start(bf16[256,1024]{1,0:T(8,128)(2,1)} %bitcast.21), channel_id=1, source_target_pairs={{0,4},{4,0},{8,12},{12,8},{16,20},{20,16},{24,28},{28,24},{1,5},{5... | collective-permute-start | bytes 1572872 | tf_op jit(solution)/shard_map/ppermute | solution.py:274
  1.7 10.6 %collective-permute-start.3 = (bf16[32,1024]{1,0:T(8,128)(2,1)}, bf16[32,1024]{1,0:T(8,128)(2,1)S(1)}, u32[]{:S(2)}, u32[]{:S(2)}) collective-permute-start(bf16[32,1024]{1,0:T(8,128)(2,1)} %refs_0_.1), channel_id=1, source_target_pairs={{0,2},{1,3},{2,0},{3,1},{4,6},{5,7},{6,4},{7,5},{8,10},{9,11},{10,... | collective-permute-start | bytes 196616 | tf_op jit(solution)/shard_map/ppermute | solution.py:286
  6.9 5.9 %collective-permute-start.2 = (bf16[32,1024]{1,0:T(8,128)(2,1)S(1)}, bf16[32,1024]{1,0:T(8,128)(2,1)S(1)}, u32[]{:S(2)}, u32[]{:S(2)}) collective-permute-start(bf16[32,1024]{1,0:T(8,128)(2,1)S(1)} %copy-done.2), channel_id=1, source_target_pairs={{0,1},{1,0},{2,3},{3,2},{4,5},{5,4},{6,7},{7,6},{8,9},{9,8},{10,11... | collective-permute-start | bytes 196616 | tf_op jit(solution)/shard_map/ppermute | solution.py:286
  8.5 6.1 %collective-permute-start.4 = (bf16[32,1024]{1,0:T(8,128)(2,1)S(1)}, bf16[32,1024]{1,0:T(8,128)(2,1)S(1)}, u32[]{:S(2)}, u32[]{:S(2)}) collective-permute-start(bf16[32,1024]{1,0:T(8,128)(2,1)S(1)} %copy-done.2), channel_id=1, source_target_pairs={{0,3},{1,2},{2,1},{3,0},{4,7},{5,6},{6,5},{7,4},{8,11},{9,10},{10,... | collective-permute-start | bytes 196616 | tf_op jit(solution)/shard_map/ppermute | solution.py:286
  9.2 8.5 %copy-start = (bf16[1,256,1024]{2,1,0:T(8,128)(2,1)S(1)}, bf16[1,256,1024]{2,1,0:T(8,128)(2,1)}, u32[]{:S(2)}) copy-start(bf16[1,256,1024]{2,1,0:T(8,128)(2,1)} %param.5) | copy-start | bytes 1572868
  9.2 9.4 %collective-permute-start.13 = (bf16[4,128,128]{2,1,0:T(8,128)(2,1)S(1)}, bf16[4,128,128]{2,1,0:T(8,128)(2,1)S(1)}, u32[]{:S(2)}, u32[]{:S(2)}) collective-permute-start(bf16[4,128,128]{2,1,0:T(8,128)(2,1)S(1)} %get-tuple-element.38.refs_4_), channel_id=1, source_target_pairs={{0,24},{4,28},{8,16},{12,20},{16,8},{20,12},{24,0},{28,4},{1,25},{... | collective-permute-start | bytes 393224 | tf_op jit(solution)/shard_map/ppermute | solution.py:283
  11.8 6.8 %collective-permute-start.12 = (bf16[4,128,128]{2,1,0:T(8,128)(2,1)S(1)}, bf16[4,128,128]{2,1,0:T(8,128)(2,1)S(1)}, u32[]{:S(2)}, u32[]{:S(2)}) collective-permute-start(bf16[4,128,128]{2,1,0:T(8,128)(2,1)S(1)} %get-tuple-element.38.refs_4_), channel_id=1, source_target_pairs={{0,16},{4,20},{8,24},{12,28},{16,0},{20,4},{24,8},{28,12},{1,17},{... | collective-permute-start | bytes 393224 | tf_op jit(solution)/shard_map/ppermute | solution.py:280
  12.3 7.2 %collective-permute-start.11 = (bf16[4,128,128]{2,1,0:T(8,128)(2,1)S(1)}, bf16[4,128,128]{2,1,0:T(8,128)(2,1)S(1)}, u32[]{:S(2)}, u32[]{:S(2)}) collective-permute-start(bf16[4,128,128]{2,1,0:T(8,128)(2,1)S(1)} %get-tuple-element.38.refs_4_), channel_id=1, source_target_pairs={{0,8},{4,12},{8,0},{12,4},{16,24},{20,28},{24,16},{28,20},{1,9},{5... | collective-permute-start | bytes 393224 | tf_op jit(solution)/shard_map/ppermute | solution.py:277
  14.6 4.9 %copy-start.1 = (bf16[1,256,1024]{2,1,0:T(8,128)(2,1)S(1)}, bf16[1,256,1024]{2,1,0:T(8,128)(2,1)}, u32[]{:S(2)}) copy-start(bf16[1,256,1024]{2,1,0:T(8,128)(2,1)} %param.8) | copy-start | bytes 1572868
  14.6 9.4 %collective-permute-start.9 = (bf16[128,1024]{1,0:T(8,128)(2,1)S(1)}, bf16[128,1024]{1,0:T(8,128)(2,1)S(1)}, u32[]{:S(2)}, u32[]{:S(2)}) collective-permute-start(bf16[128,1024]{1,0:T(8,128)(2,1)S(1)} %shard_map.85.refs_5_.refs_4_), channel_id=1, source_target_pairs={{0,16},{4,20},{8,24},{12,28},{16,0},{20,4},{24,8},{28,12},{1,17},{... | collective-permute-start | bytes 786440 | tf_op jit(solution)/shard_map/ppermute | solution.py:280
  16.2 9.3 %collective-permute-start.7 = (bf16[128,1024]{1,0:T(8,128)(2,1)S(1)}, bf16[128,1024]{1,0:T(8,128)(2,1)S(1)}, u32[]{:S(2)}, u32[]{:S(2)}) collective-permute-start(bf16[128,1024]{1,0:T(8,128)(2,1)S(1)} %shard_map.85.refs_5_.refs_4_), channel_id=1, source_target_pairs={{0,8},{4,12},{8,0},{12,4},{16,24},{20,28},{24,16},{28,20},{1,9},{5... | collective-permute-start | bytes 786440 | tf_op jit(solution)/shard_map/ppermute | solution.py:277
  21.1 9.8 %collective-permute-start.16 = (bf16[2,128,512]{2,1,0:T(8,128)(2,1)S(1)}, bf16[2,128,512]{2,1,0:T(8,128)(2,1)S(1)}, u32[]{:S(2)}, u32[]{:S(2)}) collective-permute-start(bf16[2,128,512]{2,1,0:T(8,128)(2,1)S(1)} %get-tuple-element.45), channel_id=1, source_target_pairs={{0,8},{4,12},{8,0},{12,4},{16,24},{20,28},{24,16},{28,20},{1,9},{5... | collective-permute-start | bytes 786440 | tf_op jit(solution)/shard_map/ppermute | solution.py:277
  22.7 8.3 %collective-permute-start.15 = (bf16[2,128,512]{2,1,0:T(8,128)(2,1)S(1)}, bf16[2,128,512]{2,1,0:T(8,128)(2,1)S(1)}, u32[]{:S(2)}, u32[]{:S(2)}) collective-permute-start(bf16[2,128,512]{2,1,0:T(8,128)(2,1)S(1)} %get-tuple-element.44), channel_id=1, source_target_pairs={{0,16},{4,20},{8,24},{12,28},{16,0},{20,4},{24,8},{28,12},{1,17},{... | collective-permute-start | bytes 786440 | tf_op jit(solution)/shard_map/ppermute | solution.py:280
  23.2 3.5 %collective-permute-start.14 = (bf16[4,128,128]{2,1,0:T(8,128)(2,1)S(1)}, bf16[4,128,128]{2,1,0:T(8,128)(2,1)S(1)}, u32[]{:S(2)}, u32[]{:S(2)}) collective-permute-start(bf16[4,128,128]{2,1,0:T(8,128)(2,1)S(1)} %get-tuple-element.40), channel_id=1, source_target_pairs={{0,4},{4,0},{8,12},{12,8},{16,20},{20,16},{24,28},{28,24},{1,5},{5... | collective-permute-start | bytes 393224 | tf_op jit(solution)/shard_map/ppermute | solution.py:274
  24.0 9.2 %collective-permute-start.10 = (bf16[64,1024]{1,0:T(8,128)(2,1)S(1)}, bf16[64,1024]{1,0:T(8,128)(2,1)S(1)}, u32[]{:S(2)}, u32[]{:S(2)}) collective-permute-start(bf16[64,1024]{1,0:T(8,128)(2,1)S(1)} %slice.9), channel_id=1, source_target_pairs={{0,8},{4,12},{8,0},{12,4},{16,24},{20,28},{24,16},{28,20},{1,9},{5... | collective-permute-start | bytes 393224 | tf_op jit(solution)/shard_map/ppermute | solution.py:277
  25.6 7.6 %collective-permute-start.8 = (bf16[64,1024]{1,0:T(8,128)(2,1)S(1)}, bf16[64,1024]{1,0:T(8,128)(2,1)S(1)}, u32[]{:S(2)}, u32[]{:S(2)}) collective-permute-start(bf16[64,1024]{1,0:T(8,128)(2,1)S(1)} %slice.8), channel_id=1, source_target_pairs={{0,16},{4,20},{8,24},{12,28},{16,0},{20,4},{24,8},{28,12},{1,17},{... | collective-permute-start | bytes 393224 | tf_op jit(solution)/shard_map/ppermute | solution.py:280
  28.3 7.4 %collective-permute-start.17 = (bf16[256,384]{1,0:T(8,128)(2,1)S(1)}, bf16[256,384]{1,0:T(8,128)(2,1)S(1)}, u32[]{:S(2)}, u32[]{:S(2)}) collective-permute-start(bf16[256,384]{1,0:T(8,128)(2,1)S(1)} %get-tuple-element.50), channel_id=1, source_target_pairs={{0,4},{4,0},{8,12},{12,8},{16,20},{20,16},{24,28},{28,24},{1,5},{5... | collective-permute-start | bytes 589832 | tf_op jit(solution)/shard_map/ppermute | solution.py:274
  31.0 6.8 %collective-permute-start.20 = (bf16[128,512]{1,0:T(8,128)(2,1)S(1)}, bf16[128,512]{1,0:T(8,128)(2,1)S(1)}, u32[]{:S(2)}, u32[]{:S(2)}) collective-permute-start(bf16[128,512]{1,0:T(8,128)(2,1)S(1)} %shard_map.91.refs_8_), channel_id=1, source_target_pairs={{0,8},{4,12},{8,0},{12,4},{16,24},{20,28},{24,16},{28,20},{1,9},{5... | collective-permute-start | bytes 393224 | tf_op jit(solution)/shard_map/ppermute | solution.py:277
  32.6 5.2 %collective-permute-start.19 = (bf16[128,512]{1,0:T(8,128)(2,1)S(1)}, bf16[128,512]{1,0:T(8,128)(2,1)S(1)}, u32[]{:S(2)}, u32[]{:S(2)}) collective-permute-start(bf16[128,512]{1,0:T(8,128)(2,1)S(1)} %shard_map.90.refs_2_), channel_id=1, source_target_pairs={{0,16},{4,20},{8,24},{12,28},{16,0},{20,4},{24,8},{28,12},{1,17},{... | collective-permute-start | bytes 393224 | tf_op jit(solution)/shard_map/ppermute | solution.py:280
  34.1 3.0 %collective-permute-start.18 = (bf16[256,128]{1,0:T(8,128)(2,1)S(1)}, bf16[256,128]{1,0:T(8,128)(2,1)S(1)}, u32[]{:S(2)}, u32[]{:S(2)}) collective-permute-start(bf16[256,128]{1,0:T(8,128)(2,1)S(1)} %get-tuple-element.51), channel_id=1, source_target_pairs={{0,4},{4,0},{8,12},{12,8},{16,20},{20,16},{24,28},{28,24},{1,5},{5... | collective-permute-start | bytes 196616 | tf_op jit(solution)/shard_map/ppermute | solution.py:274
  34.2 7.3 %collective-permute-start.23 = (bf16[4,128,128]{2,1,0:T(8,128)(2,1)S(1)}, bf16[4,128,128]{2,1,0:T(8,128)(2,1)S(1)}, u32[]{:S(2)}, u32[]{:S(2)}) collective-permute-start(bf16[4,128,128]{2,1,0:T(8,128)(2,1)S(1)} %get-tuple-element.58), channel_id=1, source_target_pairs={{0,24},{4,28},{8,16},{12,20},{16,8},{20,12},{24,0},{28,4},{1,25},{... | collective-permute-start | bytes 393224 | tf_op jit(solution)/shard_map/ppermute | solution.py:283
  35.6 8.4 %collective-permute-start.22 = (bf16[4,128,128]{2,1,0:T(8,128)(2,1)S(1)}, bf16[4,128,128]{2,1,0:T(8,128)(2,1)S(1)}, u32[]{:S(2)}, u32[]{:S(2)}) collective-permute-start(bf16[4,128,128]{2,1,0:T(8,128)(2,1)S(1)} %get-tuple-element.58), channel_id=1, source_target_pairs={{0,16},{4,20},{8,24},{12,28},{16,0},{20,4},{24,8},{28,12},{1,17},{... | collective-permute-start | bytes 393224 | tf_op jit(solution)/shard_map/ppermute | solution.py:280
  37.1 7.0 %collective-permute-start.21 = (bf16[4,128,128]{2,1,0:T(8,128)(2,1)S(1)}, bf16[4,128,128]{2,1,0:T(8,128)(2,1)S(1)}, u32[]{:S(2)}, u32[]{:S(2)}) collective-permute-start(bf16[4,128,128]{2,1,0:T(8,128)(2,1)S(1)} %get-tuple-element.58), channel_id=1, source_target_pairs={{0,8},{4,12},{8,0},{12,4},{16,24},{20,28},{24,16},{28,20},{1,9},{5... | collective-permute-start | bytes 393224 | tf_op jit(solution)/shard_map/ppermute | solution.py:277
  37.9 7.7 %collective-permute-start.26 = (bf16[32,1024]{1,0:T(8,128)(2,1)S(1)}, bf16[32,1024]{1,0:T(8,128)(2,1)S(1)}, u32[]{:S(2)}, u32[]{:S(2)}) collective-permute-start(bf16[32,1024]{1,0:T(8,128)(2,1)S(1)} %get-tuple-element.63), channel_id=1, source_target_pairs={{0,2},{1,3},{2,0},{3,1},{4,6},{5,7},{6,4},{7,5},{8,10},{9,11},{10,... | collective-permute-start | bytes 196616 | tf_op jit(solution)/shard_map/ppermute | solution.py:286
  39.2 6.6 %collective-permute-start.27 = (bf16[32,1024]{1,0:T(8,128)(2,1)S(1)}, bf16[32,1024]{1,0:T(8,128)(2,1)S(1)}, u32[]{:S(2)}, u32[]{:S(2)}) collective-permute-start(bf16[32,1024]{1,0:T(8,128)(2,1)S(1)} %get-tuple-element.64), channel_id=1, source_target_pairs={{0,3},{1,2},{2,1},{3,0},{4,7},{5,6},{6,5},{7,4},{8,11},{9,10},{10,... | collective-permute-start | bytes 196616 | tf_op jit(solution)/shard_map/ppermute | solution.py:286
  41.5 4.9 %collective-permute-start.25 = (bf16[32,1024]{1,0:T(8,128)(2,1)S(1)}, bf16[32,1024]{1,0:T(8,128)(2,1)S(1)}, u32[]{:S(2)}, u32[]{:S(2)}) collective-permute-start(bf16[32,1024]{1,0:T(8,128)(2,1)S(1)} %get-tuple-element.55.refs_10_), channel_id=1, source_target_pairs={{0,1},{1,0},{2,3},{3,2},{4,5},{5,4},{6,7},{7,6},{8,9},{9,8},{10,11... | collective-permute-start | bytes 196616 | tf_op jit(solution)/shard_map/ppermute | solution.py:286
  44.2 2.2 %collective-permute-start.24 = (bf16[4,128,128]{2,1,0:T(8,128)(2,1)S(1)}, bf16[4,128,128]{2,1,0:T(8,128)(2,1)S(1)}, u32[]{:S(2)}, u32[]{:S(2)}) collective-permute-start(bf16[4,128,128]{2,1,0:T(8,128)(2,1)S(1)} %get-tuple-element.60), channel_id=1, source_target_pairs={{0,4},{4,0},{8,12},{12,8},{16,20},{20,16},{24,28},{28,24},{1,5},{5... | collective-permute-start | bytes 393224 | tf_op jit(solution)/shard_map/ppermute | solution.py:274

commit v5 on v4

--- a/solution.py
+++ b/solution.py
@@ -29,6 +29,10 @@
 
 def tn(a, b):
     return lax.dot_general(a, b, (((0,), (0,)), ((), ())), preferred_element_type=F32)
+
+
+def feature_rows(a, b):
+    return lax.dot_general(a, b, (((0,), (1,)), ((), ())), preferred_element_type=F32)
 
 
 def cols(index):
@@ -87,7 +91,7 @@
         for j in range(GROUPS):
             c = cols(2 * j + par)
             scores = jnp.where(mask, nt(q[:, c], k[:, c]), 0.0).astype(BF)
-            intra[i, :, j * HEAD : (j + 1) * HEAD] = nn(scores, v[:, c])
+            intra[i, j * HEAD : (j + 1) * HEAD, :] = feature_rows(v[:, c], scores)
 
 
 def attend_kernel(
@@ -109,9 +113,9 @@
         state_o[j] = s_o
         state_r[j] = s_r
         c = cols(2 * j + par)
-        a_o = (att_scale * (intra[0, :, cols(j)] + nn(q_o[:, c], s_o))).astype(BF)
-        a_r = (att_scale * (intra[1, :, cols(j)] + nn(q_r[:, c], s_r))).astype(BF)
-        term = (tn(a_o, g_o[...]) + tn(a_r, g_r[...])) * inv_root
+        a_o = (att_scale * (intra[0, cols(j), :] + feature_rows(s_o, q_o[:, c]))).astype(BF)
+        a_r = (att_scale * (intra[1, cols(j), :] + feature_rows(s_r, q_r[:, c]))).astype(BF)
+        term = (nn(a_o, g_o[...]) + nn(a_r, g_r[...])) * inv_root
         first, second = term[:, :half], term[:, half:]
         if m == 3:
             to_x[1], to_y[1] = first.astype(BF), second.astype(BF)
@@ -305,7 +309,7 @@
     )
     (intra,) = local_call(
         intra_kernel,
-        [((2, BLOCK, half), F32)], q_o, kv_o, q_r, k_r, v_r, after=(w_0,),
+        [((2, half, BLOCK), F32)], q_o, kv_o, q_r, k_r, v_r, after=(w_0,),
     )
     w_x, w_y = over_x(w_0), over_y(w_0)
     w_d0, w_d1 = over_y(w_x[: HEAD // 2]), over_x(w_y[HEAD // 2 :])

time: 47.7 us -> 47.5 us (level)
  no operation moved by 1% of the time
where the time goes in v5:
time: 47.5 us; the launch traced here: 47.3 us
  starting transfers between devices  28.2 us (59%)
  Pallas kernels  10.8 us (23%)
  waiting for transfers between devices  6.37 us (13%)
  local copies, waits for them, and re-layouts  1.15 us (2%)
  between operations  0.85 us (2%)
    pallas_call x15, Pallas kernels, local_call(): pl.pallas_call(body, out_shape=[jax.ShapeDtypeStruct(s, d) for s, d in ou...  10.8 us
    ppermute x6, starting transfers between devices, along_dp(): return lax.ppermute(x, 'dp', [(i, i ^ m) for i in range(n_dp)])  9.64 us
    ppermute x6, starting transfers between devices, over_x(): return lax.ppermute(x, 'ctx', along(2))  7.43 us
    ppermute x6, starting transfers between devices, over_y(): return lax.ppermute(x, 'ctx', along(4))  5.6 us
    ppermute x2, starting transfers between devices, over_both(): return lax.ppermute(x, 'ctx', along(6))  4.18 us
    ppermute x6, waiting for transfers between devices, along_dp(): return lax.ppermute(x, 'dp', [(i, i ^ m) for i in range(n_dp)])  2.68 us
    ppermute x6, waiting for transfers between devices, over_x(): return lax.ppermute(x, 'ctx', along(2))  2.38 us
    ppermute x8, starting transfers between devices, core(): return lax.ppermute(x, 'ctx', along(1))  1.32 us
  transfers between devices with their start and end apart: 28, of which 8 were waited for; matrix products, arithmetic and copies ran while one was open for 2% of the time, Pallas kernels for 21%

profile of v5, /device:TPU:0, one launch (start us, length us, event | category | flops | bytes accessed | tf_op | source)
XLA Modules:
  0.0 47.3 jit_solution(8065392074734372814)
XLA Ops:
  0.6 0.5 %collective-permute-start = (bf16[256,1024]{1,0:T(8,128)(2,1)}, bf16[256,1024]{1,0:T(8,128)(2,1)S(1)}, u32[]{:S(2)}, u32[]{:S(2)}) collective-permute-start(bf16[256,1024]{1,0:T(8,128)(2,1)} %bitcast.7), channel_id=1, source_target_pairs={{0,4},{4,0},{8,12},{12,8},{16,20},{20,16},{24,28},{28,24},{1,5},{5... | collective-permute-start | bytes 1572872 | tf_op jit(solution)/shard_map/ppermute | solution.py:278
  1.1 0.1 collective-permute-start.1
  1.2 0.4 collective-permute-start.6
  1.7 0.1 collective-permute-start.5
  1.7 4.0 %collective-permute-start.3 = (bf16[32,1024]{1,0:T(8,128)(2,1)}, bf16[32,1024]{1,0:T(8,128)(2,1)S(1)}, u32[]{:S(2)}, u32[]{:S(2)}) collective-permute-start(bf16[32,1024]{1,0:T(8,128)(2,1)} %refs_0_.1), channel_id=1, source_target_pairs={{0,2},{1,3},{2,0},{3,1},{4,6},{5,7},{6,4},{7,5},{8,10},{9,11},{10,... | collective-permute-start | bytes 196616 | tf_op jit(solution)/shard_map/ppermute | solution.py:290
  5.8 1.1 %constant_dynamic-update-slice_fusion.1 = bf16[2,256,1024]{2,1,0:T(8,128)(2,1)S(1)} fusion(bf16[1,256,1024]{2,1,0:T(8,128)(2,1)} %param.6), kind=kLoop, calls=%fused_computation.1 | loop fusion | bytes 1048576
  6.8 0.0 collective-permute-done.refs_3_.refs_2_.refs_1_
  6.9 1.6 %collective-permute-start.2 = (bf16[32,1024]{1,0:T(8,128)(2,1)S(1)}, bf16[32,1024]{1,0:T(8,128)(2,1)S(1)}, u32[]{:S(2)}, u32[]{:S(2)}) collective-permute-start(bf16[32,1024]{1,0:T(8,128)(2,1)S(1)} %copy-done.2), channel_id=1, source_target_pairs={{0,1},{1,0},{2,3},{3,2},{4,5},{5,4},{6,7},{7,6},{8,9},{9,8},{10,11... | collective-permute-start | bytes 196616 | tf_op jit(solution)/shard_map/ppermute | solution.py:290
  8.5 0.0 collective-permute-done.1.refs_4_.refs_3_
  8.5 0.1 collective-permute-start.4
  8.7 0.0 collective-permute-done.6.refs_2_.refs_4_
  8.7 0.0 collective-permute-done.5.refs_1_.refs_3_
  8.7 0.5 %shard_map.84 = (f32[4,128,128]{2,1,0:T(8,128)S(1)}, bf16[4,128,128]{2,1,0:T(8,128)(2,1)S(1)}) custom-call(bf16[2,256,1024]{2,1,0:T(8,128)(2,1)S(1)} %constant_dynamic-update-slice_fusion.refs_0_.refs_1_, bf16[256,1024]{1,0:T(8,128)(2,1)S(1)} %collective-permute-done.5.refs_1_.refs_3_, bf16[256,1024]{1,0:T(8,128)(2,1)S(1)} %collective-permute-done.6.refs_2_.refs_4_, ...), custom_call_target="tpu_custom_call" | custom-call | tf_op jit(solution)/shard_map/pallas_call | solution.py:61
  9.2 0.0 copy-start
  9.2 2.6 %collective-permute-start.13 = (bf16[4,128,128]{2,1,0:T(8,128)(2,1)S(1)}, bf16[4,128,128]{2,1,0:T(8,128)(2,1)S(1)}, u32[]{:S(2)}, u32[]{:S(2)}) collective-permute-start(bf16[4,128,128]{2,1,0:T(8,128)(2,1)S(1)} %get-tuple-element.38.refs_4_), channel_id=1, source_target_pairs={{0,24},{4,28},{8,16},{12,20},{16,8},{20,12},{24,0},{28,4},{1,25},{... | collective-permute-start | bytes 393224 | tf_op jit(solution)/shard_map/ppermute | solution.py:287
  11.8 0.5 %collective-permute-start.12 = (bf16[4,128,128]{2,1,0:T(8,128)(2,1)S(1)}, bf16[4,128,128]{2,1,0:T(8,128)(2,1)S(1)}, u32[]{:S(2)}, u32[]{:S(2)}) collective-permute-start(bf16[4,128,128]{2,1,0:T(8,128)(2,1)S(1)} %get-tuple-element.38.refs_4_), channel_id=1, source_target_pairs={{0,16},{4,20},{8,24},{12,28},{16,0},{20,4},{24,8},{28,12},{1,17},{... | collective-permute-start | bytes 393224 | tf_op jit(solution)/shard_map/ppermute | solution.py:284
  12.3 0.0 collective-permute-done.3.refs_2_
  12.3 0.4 collective-permute-start.11
  12.8 0.0 collective-permute-done.2.refs_1_
  12.8 1.8 %collective-permute-done.4.refs_3_ = bf16[32,1024]{1,0:T(8,128)(2,1)S(1)} collective-permute-done((bf16[32,1024]{1,0:T(8,128)(2,1)S(1)}, bf16[32,1024]{1,0:T(8,128)(2,1)S(1)}, u32[]{:S(2)}, u32[]{:S(2)}) %collective-permute-start.4) | collective-permute-done | bytes 65568 | tf_op jit(solution)/shard_map/ppermute | solution.py:290
  14.6 0.0 copy-start.1
  14.6 1.6 %collective-permute-start.9 = (bf16[128,1024]{1,0:T(8,128)(2,1)S(1)}, bf16[128,1024]{1,0:T(8,128)(2,1)S(1)}, u32[]{:S(2)}, u32[]{:S(2)}) collective-permute-start(bf16[128,1024]{1,0:T(8,128)(2,1)S(1)} %shard_map.85.refs_5_.refs_4_), channel_id=1, source_target_pairs={{0,16},{4,20},{8,24},{12,28},{16,0},{20,4},{24,8},{28,12},{1,17},{... | collective-permute-start | bytes 786440 | tf_op jit(solution)/shard_map/ppermute | solution.py:284
  16.2 1.5 %collective-permute-start.7 = (bf16[128,1024]{1,0:T(8,128)(2,1)S(1)}, bf16[128,1024]{1,0:T(8,128)(2,1)S(1)}, u32[]{:S(2)}, u32[]{:S(2)}) collective-permute-start(bf16[128,1024]{1,0:T(8,128)(2,1)S(1)} %shard_map.85.refs_5_.refs_4_), channel_id=1, source_target_pairs={{0,8},{4,12},{8,0},{12,4},{16,24},{20,28},{24,16},{28,20},{1,9},{5... | collective-permute-start | bytes 786440 | tf_op jit(solution)/shard_map/ppermute | solution.py:281
  17.7 0.9 %shard_map.86.refs_4_ = f32[2,512,256]{2,1,0:T(8,128)S(1)} custom-call(bf16[256,1024]{1,0:T(8,128)(2,1)S(1)} %bitcast.8, bf16[2,256,1024]{2,1,0:T(8,128)(2,1)S(1)} %constant_dynamic-update-slice_fusion.refs_0_.refs_1_, bf16[256,1024]{1,0:T(8,128)(2,1)S(1)} %collective-permute-done.refs_3_.refs_2_.refs_1_, ...), custom_call_target="tpu_custom_call" | custom-call | tf_op jit(solution)/shard_map/pallas_call | solution.py:61
  18.6 0.0 collective-permute-done.13.refs_8_
  18.6 0.0 collective-permute-done.12.refs_7_
  18.6 1.0 %collective-permute-done.11.refs_6_ = bf16[4,128,128]{2,1,0:T(8,128)(2,1)S(1)} collective-permute-done((bf16[4,128,128]{2,1,0:T(8,128)(2,1)S(1)}, bf16[4,128,128]{2,1,0:T(8,128)(2,1)S(1)}, u32[]{:S(2)}, u32[]{:S(2)}) %collective-permute-start.11) | collective-permute-done | bytes 131104 | tf_op jit(solution)/shard_map/ppermute | solution.py:281
  19.5 1.3 %shard_map.87 = (bf16[2,128,512]{2,1,0:T(8,128)(2,1)S(1)}, bf16[2,128,512]{2,1,0:T(8,128)(2,1)S(1)}, f32[128,1024]{1,0:T(8,128)S(1)}, f32[2,128,512]{2,1,0:T(8,1...) custom-call(bf16[256,1024]{1,0:T(8,128)(2,1)S(1)} %bitcast.9, ...), custom_call_target="tpu_custom_call" | custom-call | tf_op jit(solution)/shard_map/pallas_call | solution.py:61
  20.9 1.6 %collective-permute-start.16 = (bf16[2,128,512]{2,1,0:T(8,128)(2,1)S(1)}, bf16[2,128,512]{2,1,0:T(8,128)(2,1)S(1)}, u32[]{:S(2)}, u32[]{:S(2)}) collective-permute-start(bf16[2,128,512]{2,1,0:T(8,128)(2,1)S(1)} %get-tuple-element.45), channel_id=1, source_target_pairs={{0,8},{4,12},{8,0},{12,4},{16,24},{20,28},{24,16},{28,20},{1,9},{5... | collective-permute-start | bytes 786440 | tf_op jit(solution)/shard_map/ppermute | solution.py:281
  22.4 0.5 %collective-permute-start.15 = (bf16[2,128,512]{2,1,0:T(8,128)(2,1)S(1)}, bf16[2,128,512]{2,1,0:T(8,128)(2,1)S(1)}, u32[]{:S(2)}, u32[]{:S(2)}) collective-permute-start(bf16[2,128,512]{2,1,0:T(8,128)(2,1)S(1)} %get-tuple-element.44), channel_id=1, source_target_pairs={{0,16},{4,20},{8,24},{12,28},{16,0},{20,4},{24,8},{28,12},{1,17},{... | collective-permute-start | bytes 786440 | tf_op jit(solution)/shard_map/ppermute | solution.py:284
  22.9 1.1 %collective-permute-done.9.refs_6_ = bf16[128,1024]{1,0:T(8,128)(2,1)S(1)} collective-permute-done((bf16[128,1024]{1,0:T(8,128)(2,1)S(1)}, bf16[128,1024]{1,0:T(8,128)(2,1)S(1)}, u32[]{:S(2)}, u32[]{:S(2)}) %collective-permute-start.9) | collective-permute-done | bytes 262176 | tf_op jit(solution)/shard_map/ppermute | solution.py:284
  24.0 1.5 %collective-permute-start.10 = (bf16[64,1024]{1,0:T(8,128)(2,1)S(1)}, bf16[64,1024]{1,0:T(8,128)(2,1)S(1)}, u32[]{:S(2)}, u32[]{:S(2)}) collective-permute-start(bf16[64,1024]{1,0:T(8,128)(2,1)S(1)} %slice.9), channel_id=1, source_target_pairs={{0,8},{4,12},{8,0},{12,4},{16,24},{20,28},{24,16},{28,20},{1,9},{5... | collective-permute-start | bytes 393224 | tf_op jit(solution)/shard_map/ppermute | solution.py:281
  25.5 0.0 collective-permute-done.7.refs_5_
  25.6 1.4 %collective-permute-start.8 = (bf16[64,1024]{1,0:T(8,128)(2,1)S(1)}, bf16[64,1024]{1,0:T(8,128)(2,1)S(1)}, u32[]{:S(2)}, u32[]{:S(2)}) collective-permute-start(bf16[64,1024]{1,0:T(8,128)(2,1)S(1)} %slice.8), channel_id=1, source_target_pairs={{0,16},{4,20},{8,24},{12,28},{16,0},{20,4},{24,8},{28,12},{1,17},{... | collective-permute-start | bytes 393224 | tf_op jit(solution)/shard_map/ppermute | solution.py:284
  26.9 1.6 %shard_map.88 = (bf16[256,384]{1,0:T(8,128)(2,1)S(1)}, bf16[256,384]{1,0:T(8,128)(2,1)S(1)}, f32[4,128,128]{2,1,0:T(8,128)S(1)}, bf16[4,128,128]{2,1,0:T(8,128)(2,1)S(1)}) custom-call(bf16[256,1024]{1,0:T(8,128)(2,1)S(1)} %bitcast.10, bf16[256,1024]{1,0:T(8,128)(2,1)S(1)} %collective-permute-done.refs_3_.refs_2_.refs_1_, bf16[256,1024]{1,0:T(8,128)(2,1)S(1)} %bitcast.16, ...), custom_call_target="tpu_custom_call" | custom-call | tf_op jit(solution)/shard_map/pallas_call | solution.py:61
  28.5 0.1 collective-permute-start.17
  28.6 0.9 %shard_map.89 = (bf16[256,384]{1,0:T(8,128)(2,1)S(1)}, f32[256,384]{1,0:T(8,128)S(1)}, f32[256,384]{1,0:T(8,128)S(1)}) custom-call(bf16[256,1024]{1,0:T(8,128)(2,1)S(1)} %bitcast.11, bf16[2,256,1024]{2,1,0:T(8,128)(2,1)S(1)} %constant_dynamic-update-slice_fusion.refs_0_.refs_1_, bf16[256,384]{1,0:T(8,128)(2,1)S(1)} %get-tuple-element.46.refs_2_, ...), custom_call_target="tpu_custom_call" | custom-call | tf_op jit(solution)/shard_map/pallas_call | solution.py:61
  29.5 1.4 %collective-permute-done.16.refs_1_ = bf16[2,128,512]{2,1,0:T(8,128)(2,1)S(1)} collective-permute-done((bf16[2,128,512]{2,1,0:T(8,128)(2,1)S(1)}, bf16[2,128,512]{2,1,0:T(8,128)(2,1)S(1)}, u32[]{:S(2)}, u32[]{:S(2)}) %collective-permute-start.16) | collective-permute-done | bytes 262176 | tf_op jit(solution)/shard_map/ppermute | solution.py:281
  31.0 1.6 %collective-permute-start.20 = (bf16[128,512]{1,0:T(8,128)(2,1)S(1)}, bf16[128,512]{1,0:T(8,128)(2,1)S(1)}, u32[]{:S(2)}, u32[]{:S(2)}) collective-permute-start(bf16[128,512]{1,0:T(8,128)(2,1)S(1)} %shard_map.91.refs_8_), channel_id=1, source_target_pairs={{0,8},{4,12},{8,0},{12,4},{16,24},{20,28},{24,16},{28,20},{1,9},{5... | collective-permute-start | bytes 393224 | tf_op jit(solution)/shard_map/ppermute | solution.py:281
  32.6 0.5 collective-permute-start.19
  33.1 0.0 collective-permute-done.10.refs_5_
  33.1 0.0 collective-permute-done.8.refs_4_
  33.1 1.0 %shard_map.92 = (bf16[256,128]{1,0:T(8,128)(2,1)S(1)}, bf16[256,128]{1,0:T(8,128)(2,1)S(1)}, f32[4,128,128]{2,1,0:T(8,128)S(1)}, bf16[4,128,128]{2,1,0:T(8,128)(2,1)S(1)}) custom-call(bf16[256,1024]{1,0:T(8,128)(2,1)S(1)} %bitcast.12, bf16[256,1024]{1,0:T(8,128)(2,1)S(1)} %collective-permute-done.refs_3_.refs_2_.refs_1_, bf16[256,1024]{1,0:T(8,128)(2,1)S(1)} %bitcast.17, ...), custom_call_target="tpu_custom_call" | custom-call | tf_op jit(solution)/shard_map/pallas_call | solution.py:61
  34.0 0.1 collective-permute-start.18
  34.1 1.6 %collective-permute-start.23 = (bf16[4,128,128]{2,1,0:T(8,128)(2,1)S(1)}, bf16[4,128,128]{2,1,0:T(8,128)(2,1)S(1)}, u32[]{:S(2)}, u32[]{:S(2)}) collective-permute-start(bf16[4,128,128]{2,1,0:T(8,128)(2,1)S(1)} %get-tuple-element.58), channel_id=1, source_target_pairs={{0,24},{4,28},{8,16},{12,20},{16,8},{20,12},{24,0},{28,4},{1,25},{... | collective-permute-start | bytes 393224 | tf_op jit(solution)/shard_map/ppermute | solution.py:287
  35.7 1.2 %collective-permute-start.22 = (bf16[4,128,128]{2,1,0:T(8,128)(2,1)S(1)}, bf16[4,128,128]{2,1,0:T(8,128)(2,1)S(1)}, u32[]{:S(2)}, u32[]{:S(2)}) collective-permute-start(bf16[4,128,128]{2,1,0:T(8,128)(2,1)S(1)} %get-tuple-element.58), channel_id=1, source_target_pairs={{0,16},{4,20},{8,24},{12,28},{16,0},{20,4},{24,8},{28,12},{1,17},{... | collective-permute-start | bytes 393224 | tf_op jit(solution)/shard_map/ppermute | solution.py:284
  36.9 0.8 %collective-permute-start.21 = (bf16[4,128,128]{2,1,0:T(8,128)(2,1)S(1)}, bf16[4,128,128]{2,1,0:T(8,128)(2,1)S(1)}, u32[]{:S(2)}, u32[]{:S(2)}) collective-permute-start(bf16[4,128,128]{2,1,0:T(8,128)(2,1)S(1)} %get-tuple-element.58), channel_id=1, source_target_pairs={{0,8},{4,12},{8,0},{12,4},{16,24},{20,28},{24,16},{28,20},{1,9},{5... | collective-permute-start | bytes 393224 | tf_op jit(solution)/shard_map/ppermute | solution.py:281
  37.7 0.0 collective-permute-done.20.refs_4_
  37.7 0.0 collective-permute-done.19.refs_3_
  37.7 0.1 shard_map.93
  37.8 1.4 %collective-permute-start.26 = (bf16[32,1024]{1,0:T(8,128)(2,1)S(1)}, bf16[32,1024]{1,0:T(8,128)(2,1)S(1)}, u32[]{:S(2)}, u32[]{:S(2)}) collective-permute-start(bf16[32,1024]{1,0:T(8,128)(2,1)S(1)} %get-tuple-element.63), channel_id=1, source_target_pairs={{0,2},{1,3},{2,0},{3,1},{4,6},{5,7},{6,4},{7,5},{8,10},{9,11},{10,... | collective-permute-start | bytes 196616 | tf_op jit(solution)/shard_map/ppermute | solution.py:290
  39.1 2.1 %collective-permute-start.27 = (bf16[32,1024]{1,0:T(8,128)(2,1)S(1)}, bf16[32,1024]{1,0:T(8,128)(2,1)S(1)}, u32[]{:S(2)}, u32[]{:S(2)}) collective-permute-start(bf16[32,1024]{1,0:T(8,128)(2,1)S(1)} %get-tuple-element.64), channel_id=1, source_target_pairs={{0,3},{1,2},{2,1},{3,0},{4,7},{5,6},{6,5},{7,4},{8,11},{9,10},{10,... | collective-permute-start | bytes 196616 | tf_op jit(solution)/shard_map/ppermute | solution.py:290
  41.2 0.2 collective-permute-done.23.refs_3_
  41.4 0.4 collective-permute-start.25
  41.9 2.2 %shard_map.94 = (bf16[256,1024]{1,0:T(8,128)(2,1)}, f32[256,1024]{1,0:T(8,128)S(1)}, f32[256,1024]{1,0:T(8,128)S(1)}) custom-call(bf16[256,1024]{1,0:T(8,128)(2,1)S(1)} %bitcast.13, bf16[2,256,1024]{2,1,0:T(8,128)(2,1)S(1)} %constant_dynamic-update-slice_fusion.refs_0_.refs_1_, bf16[256,128]{1,0:T(8,128)(2,1)S(1)} %get-tuple-element.49.refs_2_, ...), custom_call_target="tpu_custom_call" | custom-call | tf_op jit(solution)/shard_map/pallas_call | solution.py:61
  44.1 0.0 collective-permute-done.22.refs_2_
  44.1 0.0 collective-permute-done.21.refs_1_
  44.1 0.1 shard_map.95
  44.2 0.1 collective-permute-start.24
  44.3 1.1 %shard_map.96 = (bf16[256,1024]{1,0:T(8,128)(2,1)}, bf16[256,1024]{1,0:T(8,128)(2,1)}, f32[8,128]{1,0:T(8,128)S(1)}) custom-call(bf16[2,256,1024]{2,1,0:T(8,128)(2,1)S(1)} %constant_dynamic-update-slice_fusion.refs_0_.refs_1_, bf16[4,128,128]{2,1,0:T(8,128)(2,1)S(1)} %get-tuple-element.65.refs_1_, f32[256,1024]{1,0:T(8,128)S(1)} %get-tuple-element.59.refs_4_.refs_2_, ...), custom_call_target="tpu_custom_call" | custom-call | tf_op jit(solution)/shard_map/pallas_call | solution.py:61
  45.3 0.1 collective-permute-done.26.refs_2_
  45.4 0.2 collective-permute-done.27.refs_3_
  45.6 0.6 %collective-permute-done.25.refs_1_ = bf16[32,1024]{1,0:T(8,128)(2,1)S(1)} collective-permute-done((bf16[32,1024]{1,0:T(8,128)(2,1)S(1)}, bf16[32,1024]{1,0:T(8,128)(2,1)S(1)}, u32[]{:S(2)}, u32[]{:S(2)}) %collective-permute-start.25) | collective-permute-done | bytes 65568 | tf_op jit(solution)/shard_map/ppermute | solution.py:290
  46.3 1.1 %shard_map.98 = (bf16[256,1024]{1,0:T(8,128)(2,1)}, bf16[256,1024]{1,0:T(8,128)(2,1)}, f32[32,1024]{1,0:T(8,128)}) custom-call(bf16[2,256,1024]{2,1,0:T(8,128)(2,1)S(1)} %constant_dynamic-update-slice_fusion.refs_0_.refs_1_, bf16[4,128,128]{2,1,0:T(8,128)(2,1)S(1)} %collective-permute-done.24.refs_1_, ...), custom_call_target="tpu_custom_call", output_to_operand_aliasing={{0}: (5, {}), {1}: (6, {})} | custom-call | tf_op jit(solution)/shard_map/pallas_call | solution.py:61
  (19 shorter events, 0.2 us)
Async XLA Ops:
  0.6 6.2 %collective-permute-start = (bf16[256,1024]{1,0:T(8,128)(2,1)}, bf16[256,1024]{1,0:T(8,128)(2,1)S(1)}, u32[]{:S(2)}, u32[]{:S(2)}) collective-permute-start(bf16[256,1024]{1,0:T(8,128)(2,1)} %bitcast.7), channel_id=1, source_target_pairs={{0,4},{4,0},{8,12},{12,8},{16,20},{20,16},{24,28},{28,24},{1,5},{5... | collective-permute-start | bytes 1572872 | tf_op jit(solution)/shard_map/ppermute | solution.py:278
  1.1 7.4 %collective-permute-start.1 = (bf16[256,1024]{1,0:T(8,128)(2,1)}, bf16[256,1024]{1,0:T(8,128)(2,1)S(1)}, u32[]{:S(2)}, u32[]{:S(2)}) collective-permute-start(bf16[256,1024]{1,0:T(8,128)(2,1)} %bitcast.14), channel_id=1, source_target_pairs={{0,4},{4,0},{8,12},{12,8},{16,20},{20,16},{24,28},{28,24},{1,5},{5... | collective-permute-start | bytes 1572872 | tf_op jit(solution)/shard_map/ppermute | solution.py:278
  1.2 7.4 %collective-permute-start.6 = (bf16[256,1024]{1,0:T(8,128)(2,1)}, bf16[256,1024]{1,0:T(8,128)(2,1)S(1)}, u32[]{:S(2)}, u32[]{:S(2)}) collective-permute-start(bf16[256,1024]{1,0:T(8,128)(2,1)} %bitcast.20), channel_id=1, source_target_pairs={{0,4},{4,0},{8,12},{12,8},{16,20},{20,16},{24,28},{28,24},{1,5},{5... | collective-permute-start | bytes 1572872 | tf_op jit(solution)/shard_map/ppermute | solution.py:278
  1.7 5.2 %copy-start.2 = (bf16[32,1024]{1,0:T(8,128)(2,1)S(1)}, bf16[32,1024]{1,0:T(8,128)(2,1)}, u32[]{:S(2)}) copy-start(bf16[32,1024]{1,0:T(8,128)(2,1)} %refs_0_.1) | copy-start | bytes 196612
  1.7 7.0 %copy-start.3 = (bf16[1,256,1024]{2,1,0:T(8,128)(2,1)S(1)}, bf16[1,256,1024]{2,1,0:T(8,128)(2,1)}, u32[]{:S(2)}) copy-start(bf16[1,256,1024]{2,1,0:T(8,128)(2,1)} %param.7) | copy-start | bytes 1572868
  1.7 7.0 %collective-permute-start.5 = (bf16[256,1024]{1,0:T(8,128)(2,1)}, bf16[256,1024]{1,0:T(8,128)(2,1)S(1)}, u32[]{:S(2)}, u32[]{:S(2)}) collective-permute-start(bf16[256,1024]{1,0:T(8,128)(2,1)} %bitcast.21), channel_id=1, source_target_pairs={{0,4},{4,0},{8,12},{12,8},{16,20},{20,16},{24,28},{28,24},{1,5},{5... | collective-permute-start | bytes 1572872 | tf_op jit(solution)/shard_map/ppermute | solution.py:278
  1.7 10.6 %collective-permute-start.3 = (bf16[32,1024]{1,0:T(8,128)(2,1)}, bf16[32,1024]{1,0:T(8,128)(2,1)S(1)}, u32[]{:S(2)}, u32[]{:S(2)}) collective-permute-start(bf16[32,1024]{1,0:T(8,128)(2,1)} %refs_0_.1), channel_id=1, source_target_pairs={{0,2},{1,3},{2,0},{3,1},{4,6},{5,7},{6,4},{7,5},{8,10},{9,11},{10,... | collective-permute-start | bytes 196616 | tf_op jit(solution)/shard_map/ppermute | solution.py:290
  6.9 5.9 %collective-permute-start.2 = (bf16[32,1024]{1,0:T(8,128)(2,1)S(1)}, bf16[32,1024]{1,0:T(8,128)(2,1)S(1)}, u32[]{:S(2)}, u32[]{:S(2)}) collective-permute-start(bf16[32,1024]{1,0:T(8,128)(2,1)S(1)} %copy-done.2), channel_id=1, source_target_pairs={{0,1},{1,0},{2,3},{3,2},{4,5},{5,4},{6,7},{7,6},{8,9},{9,8},{10,11... | collective-permute-start | bytes 196616 | tf_op jit(solution)/shard_map/ppermute | solution.py:290
  8.5 6.1 %collective-permute-start.4 = (bf16[32,1024]{1,0:T(8,128)(2,1)S(1)}, bf16[32,1024]{1,0:T(8,128)(2,1)S(1)}, u32[]{:S(2)}, u32[]{:S(2)}) collective-permute-start(bf16[32,1024]{1,0:T(8,128)(2,1)S(1)} %copy-done.2), channel_id=1, source_target_pairs={{0,3},{1,2},{2,1},{3,0},{4,7},{5,6},{6,5},{7,4},{8,11},{9,10},{10,... | collective-permute-start | bytes 196616 | tf_op jit(solution)/shard_map/ppermute | solution.py:290
  9.2 8.5 %copy-start = (bf16[1,256,1024]{2,1,0:T(8,128)(2,1)S(1)}, bf16[1,256,1024]{2,1,0:T(8,128)(2,1)}, u32[]{:S(2)}) copy-start(bf16[1,256,1024]{2,1,0:T(8,128)(2,1)} %param.5) | copy-start | bytes 1572868
  9.2 9.4 %collective-permute-start.13 = (bf16[4,128,128]{2,1,0:T(8,128)(2,1)S(1)}, bf16[4,128,128]{2,1,0:T(8,128)(2,1)S(1)}, u32[]{:S(2)}, u32[]{:S(2)}) collective-permute-start(bf16[4,128,128]{2,1,0:T(8,128)(2,1)S(1)} %get-tuple-element.38.refs_4_), channel_id=1, source_target_pairs={{0,24},{4,28},{8,16},{12,20},{16,8},{20,12},{24,0},{28,4},{1,25},{... | collective-permute-start | bytes 393224 | tf_op jit(solution)/shard_map/ppermute | solution.py:287
  11.8 6.8 %collective-permute-start.12 = (bf16[4,128,128]{2,1,0:T(8,128)(2,1)S(1)}, bf16[4,128,128]{2,1,0:T(8,128)(2,1)S(1)}, u32[]{:S(2)}, u32[]{:S(2)}) collective-permute-start(bf16[4,128,128]{2,1,0:T(8,128)(2,1)S(1)} %get-tuple-element.38.refs_4_), channel_id=1, source_target_pairs={{0,16},{4,20},{8,24},{12,28},{16,0},{20,4},{24,8},{28,12},{1,17},{... | collective-permute-start | bytes 393224 | tf_op jit(solution)/shard_map/ppermute | solution.py:284
  12.3 7.2 %collective-permute-start.11 = (bf16[4,128,128]{2,1,0:T(8,128)(2,1)S(1)}, bf16[4,128,128]{2,1,0:T(8,128)(2,1)S(1)}, u32[]{:S(2)}, u32[]{:S(2)}) collective-permute-start(bf16[4,128,128]{2,1,0:T(8,128)(2,1)S(1)} %get-tuple-element.38.refs_4_), channel_id=1, source_target_pairs={{0,8},{4,12},{8,0},{12,4},{16,24},{20,28},{24,16},{28,20},{1,9},{5... | collective-permute-start | bytes 393224 | tf_op jit(solution)/shard_map/ppermute | solution.py:281
  14.6 4.9 %copy-start.1 = (bf16[1,256,1024]{2,1,0:T(8,128)(2,1)S(1)}, bf16[1,256,1024]{2,1,0:T(8,128)(2,1)}, u32[]{:S(2)}) copy-start(bf16[1,256,1024]{2,1,0:T(8,128)(2,1)} %param.8) | copy-start | bytes 1572868
  14.6 9.4 %collective-permute-start.9 = (bf16[128,1024]{1,0:T(8,128)(2,1)S(1)}, bf16[128,1024]{1,0:T(8,128)(2,1)S(1)}, u32[]{:S(2)}, u32[]{:S(2)}) collective-permute-start(bf16[128,1024]{1,0:T(8,128)(2,1)S(1)} %shard_map.85.refs_5_.refs_4_), channel_id=1, source_target_pairs={{0,16},{4,20},{8,24},{12,28},{16,0},{20,4},{24,8},{28,12},{1,17},{... | collective-permute-start | bytes 786440 | tf_op jit(solution)/shard_map/ppermute | solution.py:284
  16.2 9.3 %collective-permute-start.7 = (bf16[128,1024]{1,0:T(8,128)(2,1)S(1)}, bf16[128,1024]{1,0:T(8,128)(2,1)S(1)}, u32[]{:S(2)}, u32[]{:S(2)}) collective-permute-start(bf16[128,1024]{1,0:T(8,128)(2,1)S(1)} %shard_map.85.refs_5_.refs_4_), channel_id=1, source_target_pairs={{0,8},{4,12},{8,0},{12,4},{16,24},{20,28},{24,16},{28,20},{1,9},{5... | collective-permute-start | bytes 786440 | tf_op jit(solution)/shard_map/ppermute | solution.py:281
  20.9 10.1 %collective-permute-start.16 = (bf16[2,128,512]{2,1,0:T(8,128)(2,1)S(1)}, bf16[2,128,512]{2,1,0:T(8,128)(2,1)S(1)}, u32[]{:S(2)}, u32[]{:S(2)}) collective-permute-start(bf16[2,128,512]{2,1,0:T(8,128)(2,1)S(1)} %get-tuple-element.45), channel_id=1, source_target_pairs={{0,8},{4,12},{8,0},{12,4},{16,24},{20,28},{24,16},{28,20},{1,9},{5... | collective-permute-start | bytes 786440 | tf_op jit(solution)/shard_map/ppermute | solution.py:281
  22.4 8.5 %collective-permute-start.15 = (bf16[2,128,512]{2,1,0:T(8,128)(2,1)S(1)}, bf16[2,128,512]{2,1,0:T(8,128)(2,1)S(1)}, u32[]{:S(2)}, u32[]{:S(2)}) collective-permute-start(bf16[2,128,512]{2,1,0:T(8,128)(2,1)S(1)} %get-tuple-element.44), channel_id=1, source_target_pairs={{0,16},{4,20},{8,24},{12,28},{16,0},{20,4},{24,8},{28,12},{1,17},{... | collective-permute-start | bytes 786440 | tf_op jit(solution)/shard_map/ppermute | solution.py:284
  22.9 4.0 %collective-permute-start.14 = (bf16[4,128,128]{2,1,0:T(8,128)(2,1)S(1)}, bf16[4,128,128]{2,1,0:T(8,128)(2,1)S(1)}, u32[]{:S(2)}, u32[]{:S(2)}) collective-permute-start(bf16[4,128,128]{2,1,0:T(8,128)(2,1)S(1)} %get-tuple-element.40), channel_id=1, source_target_pairs={{0,4},{4,0},{8,12},{12,8},{16,20},{20,16},{24,28},{28,24},{1,5},{5... | collective-permute-start | bytes 393224 | tf_op jit(solution)/shard_map/ppermute | solution.py:278
  24.0 9.1 %collective-permute-start.10 = (bf16[64,1024]{1,0:T(8,128)(2,1)S(1)}, bf16[64,1024]{1,0:T(8,128)(2,1)S(1)}, u32[]{:S(2)}, u32[]{:S(2)}) collective-permute-start(bf16[64,1024]{1,0:T(8,128)(2,1)S(1)} %slice.9), channel_id=1, source_target_pairs={{0,8},{4,12},{8,0},{12,4},{16,24},{20,28},{24,16},{28,20},{1,9},{5... | collective-permute-start | bytes 393224 | tf_op jit(solution)/shard_map/ppermute | solution.py:281
  25.6 7.5 %collective-permute-start.8 = (bf16[64,1024]{1,0:T(8,128)(2,1)S(1)}, bf16[64,1024]{1,0:T(8,128)(2,1)S(1)}, u32[]{:S(2)}, u32[]{:S(2)}) collective-permute-start(bf16[64,1024]{1,0:T(8,128)(2,1)S(1)} %slice.8), channel_id=1, source_target_pairs={{0,16},{4,20},{8,24},{12,28},{16,0},{20,4},{24,8},{28,12},{1,17},{... | collective-permute-start | bytes 393224 | tf_op jit(solution)/shard_map/ppermute | solution.py:284
  28.5 7.1 %collective-permute-start.17 = (bf16[256,384]{1,0:T(8,128)(2,1)S(1)}, bf16[256,384]{1,0:T(8,128)(2,1)S(1)}, u32[]{:S(2)}, u32[]{:S(2)}) collective-permute-start(bf16[256,384]{1,0:T(8,128)(2,1)S(1)} %get-tuple-element.50), channel_id=1, source_target_pairs={{0,4},{4,0},{8,12},{12,8},{16,20},{20,16},{24,28},{28,24},{1,5},{5... | collective-permute-start | bytes 589832 | tf_op jit(solution)/shard_map/ppermute | solution.py:278
  31.0 6.7 %collective-permute-start.20 = (bf16[128,512]{1,0:T(8,128)(2,1)S(1)}, bf16[128,512]{1,0:T(8,128)(2,1)S(1)}, u32[]{:S(2)}, u32[]{:S(2)}) collective-permute-start(bf16[128,512]{1,0:T(8,128)(2,1)S(1)} %shard_map.91.refs_8_), channel_id=1, source_target_pairs={{0,8},{4,12},{8,0},{12,4},{16,24},{20,28},{24,16},{28,20},{1,9},{5... | collective-permute-start | bytes 393224 | tf_op jit(solution)/shard_map/ppermute | solution.py:281
  32.6 5.1 %collective-permute-start.19 = (bf16[128,512]{1,0:T(8,128)(2,1)S(1)}, bf16[128,512]{1,0:T(8,128)(2,1)S(1)}, u32[]{:S(2)}, u32[]{:S(2)}) collective-permute-start(bf16[128,512]{1,0:T(8,128)(2,1)S(1)} %shard_map.90.refs_2_), channel_id=1, source_target_pairs={{0,16},{4,20},{8,24},{12,28},{16,0},{20,4},{24,8},{28,12},{1,17},{... | collective-permute-start | bytes 393224 | tf_op jit(solution)/shard_map/ppermute | solution.py:284
  34.0 2.8 %collective-permute-start.18 = (bf16[256,128]{1,0:T(8,128)(2,1)S(1)}, bf16[256,128]{1,0:T(8,128)(2,1)S(1)}, u32[]{:S(2)}, u32[]{:S(2)}) collective-permute-start(bf16[256,128]{1,0:T(8,128)(2,1)S(1)} %get-tuple-element.51), channel_id=1, source_target_pairs={{0,4},{4,0},{8,12},{12,8},{16,20},{20,16},{24,28},{28,24},{1,5},{5... | collective-permute-start | bytes 196616 | tf_op jit(solution)/shard_map/ppermute | solution.py:278
  34.1 7.3 %collective-permute-start.23 = (bf16[4,128,128]{2,1,0:T(8,128)(2,1)S(1)}, bf16[4,128,128]{2,1,0:T(8,128)(2,1)S(1)}, u32[]{:S(2)}, u32[]{:S(2)}) collective-permute-start(bf16[4,128,128]{2,1,0:T(8,128)(2,1)S(1)} %get-tuple-element.58), channel_id=1, source_target_pairs={{0,24},{4,28},{8,16},{12,20},{16,8},{20,12},{24,0},{28,4},{1,25},{... | collective-permute-start | bytes 393224 | tf_op jit(solution)/shard_map/ppermute | solution.py:287
  35.7 8.4 %collective-permute-start.22 = (bf16[4,128,128]{2,1,0:T(8,128)(2,1)S(1)}, bf16[4,128,128]{2,1,0:T(8,128)(2,1)S(1)}, u32[]{:S(2)}, u32[]{:S(2)}) collective-permute-start(bf16[4,128,128]{2,1,0:T(8,128)(2,1)S(1)} %get-tuple-element.58), channel_id=1, source_target_pairs={{0,16},{4,20},{8,24},{12,28},{16,0},{20,4},{24,8},{28,12},{1,17},{... | collective-permute-start | bytes 393224 | tf_op jit(solution)/shard_map/ppermute | solution.py:284
  36.9 7.2 %collective-permute-start.21 = (bf16[4,128,128]{2,1,0:T(8,128)(2,1)S(1)}, bf16[4,128,128]{2,1,0:T(8,128)(2,1)S(1)}, u32[]{:S(2)}, u32[]{:S(2)}) collective-permute-start(bf16[4,128,128]{2,1,0:T(8,128)(2,1)S(1)} %get-tuple-element.58), channel_id=1, source_target_pairs={{0,8},{4,12},{8,0},{12,4},{16,24},{20,28},{24,16},{28,20},{1,9},{5... | collective-permute-start | bytes 393224 | tf_op jit(solution)/shard_map/ppermute | solution.py:281
  37.8 7.6 %collective-permute-start.26 = (bf16[32,1024]{1,0:T(8,128)(2,1)S(1)}, bf16[32,1024]{1,0:T(8,128)(2,1)S(1)}, u32[]{:S(2)}, u32[]{:S(2)}) collective-permute-start(bf16[32,1024]{1,0:T(8,128)(2,1)S(1)} %get-tuple-element.63), channel_id=1, source_target_pairs={{0,2},{1,3},{2,0},{3,1},{4,6},{5,7},{6,4},{7,5},{8,10},{9,11},{10,... | collective-permute-start | bytes 196616 | tf_op jit(solution)/shard_map/ppermute | solution.py:290
  39.1 6.5 %collective-permute-start.27 = (bf16[32,1024]{1,0:T(8,128)(2,1)S(1)}, bf16[32,1024]{1,0:T(8,128)(2,1)S(1)}, u32[]{:S(2)}, u32[]{:S(2)}) collective-permute-start(bf16[32,1024]{1,0:T(8,128)(2,1)S(1)} %get-tuple-element.64), channel_id=1, source_target_pairs={{0,3},{1,2},{2,1},{3,0},{4,7},{5,6},{6,5},{7,4},{8,11},{9,10},{10,... | collective-permute-start | bytes 196616 | tf_op jit(solution)/shard_map/ppermute | solution.py:290
  41.4 4.8 %collective-permute-start.25 = (bf16[32,1024]{1,0:T(8,128)(2,1)S(1)}, bf16[32,1024]{1,0:T(8,128)(2,1)S(1)}, u32[]{:S(2)}, u32[]{:S(2)}) collective-permute-start(bf16[32,1024]{1,0:T(8,128)(2,1)S(1)} %get-tuple-element.55.refs_10_), channel_id=1, source_target_pairs={{0,1},{1,0},{2,3},{3,2},{4,5},{5,4},{6,7},{7,6},{8,9},{9,8},{10,11... | collective-permute-start | bytes 196616 | tf_op jit(solution)/shard_map/ppermute | solution.py:290
  44.2 2.1 %collective-permute-start.24 = (bf16[4,128,128]{2,1,0:T(8,128)(2,1)S(1)}, bf16[4,128,128]{2,1,0:T(8,128)(2,1)S(1)}, u32[]{:S(2)}, u32[]{:S(2)}) collective-permute-start(bf16[4,128,128]{2,1,0:T(8,128)(2,1)S(1)} %get-tuple-element.60), channel_id=1, source_target_pairs={{0,4},{4,0},{8,12},{12,8},{16,20},{20,16},{24,28},{28,24},{1,5},{5... | collective-permute-start | bytes 393224 | tf_op jit(solution)/shard_map/ppermute | solution.py:278
